TPU v7x, 32 devices: a whole 2x2x4 slice. The times are simulated.
32 devices in a mesh: groups: 2 (over x), attn: 4 (over y, core), ffn: 4 (over z).
Axes of the slice: x: 2, y: 2, z: 4, core: 2. Of those that a mesh axis runs over, the one named last changes fastest.
Arguments:
- queries: bfloat16 [256, 16384], P(('groups', 'attn'), 'ffn'), parts along dimension 0, may hold values from -37 to 37
- new_kv: bfloat16 [256, 512], P(('groups', 'attn')), parts along dimension 0, may hold values from -6 to 6
- cache_pool: bfloat16 [112, 256, 512], P(('groups', 'attn')), parts along dimension 0, may hold values from -6 to 6
- request_owner: int32 [256], P('groups'), parts along dimension 0, may hold values from 0 to 3, as said below
- block_req: int32 [8, 14], P('groups'), parts along dimension 0, may hold values from 0 to 128, as said below
- migrate: int32 [8, 4, 1], P('groups'), parts along dimension 0, may hold values from 0 to 14, as said below
- residual_rows: bfloat16 [256, 7168], P('groups', 'attn'), parts along dimension 0, may hold values from -6 to 6
- w_out: bfloat16 [16384, 7168], P('ffn', 'attn'), may hold values from -0.046875 to 0.046875
- w_gate: bfloat16 [7168, 18432], P('attn', 'ffn'), may hold values from -0.0625 to 0.0625
- w_up: bfloat16 [7168, 18432], P('attn', 'ffn'), may hold values from -0.0625 to 0.0625
- w_down: bfloat16 [18432, 7168], P('ffn', 'attn'), may hold values from -0.046875 to 0.046875
Outputs:
- attention: bfloat16 [256, 16384], P(('groups', 'attn'), 'ffn'), parts along dimension 0
- arrived: bfloat16 [24, 256, 512], P(('groups', 'attn')), parts along dimension 0
- ffn_out: bfloat16 [256, 7168], P(('groups', 'ffn'), 'attn'), parts along dimension 0
There are 2 independent parts, one for each index of `groups`. A program takes and returns all parts, laid end to end along the dimension named above; an argument that names none is the same for every part. Nothing has to cross between parts.
Inputs may be any that keep to these rules, and one draw needn't show every extreme that they name: `request_owner`: each source device (requests i*32 to (i+1)*32 - 1) sends exactly 8 requests to each of four attention devices. `block_req`: A device's live pages come first and belong to requests that request_owner maps to that device; a device holds up to 14 live pages. `migrate`: A device moves only its own last live pages, each once; at most 3 pages arrive at one device.
All inputs are finite; a program needn't handle non-finite values.
Results may differ from a plain program's by a relative error of at most 0.0057.
Values may be sent and summed in bfloat16 or wider, within the bound.
No kernel may reach another device: no remote copies, remote signals or barrier semaphores. Data moves between devices by JAX's collectives and lax.ppermute only.
A program may use at most 192 MiB of HBM per device.

v0:
```python
import jax
import jax.numpy as jnp
from jax import lax
from jax.sharding import PartitionSpec as P


def block_terms(blocks, query_rows, head_count):
    head_size = blocks.shape[2] // 2
    queries3 = query_rows.reshape(query_rows.shape[0], head_count, head_size)
    key_part = blocks[:, :, :head_size]
    value_part = blocks[:, :, head_size:]
    scores = jnp.einsum(
        "ehd,etd->eht", queries3, key_part, preferred_element_type=jnp.float32
    ) * head_size ** (-0.5)
    block_top = jnp.max(scores, axis=2)
    weight = jnp.exp(scores - block_top[:, :, None]).astype(jnp.bfloat16)
    block_total = jnp.sum(weight.astype(jnp.float32), axis=2)
    summed = jnp.einsum("eht,etd->ehd", weight, value_part, preferred_element_type=jnp.float32)
    return (block_top, block_total, summed)


def absorb(carried, slot_of, usable, block_top, block_total, summed):
    running_max, denominator, numerator = carried
    slot_total = running_max.shape[0]
    matches = jnp.logical_and(
        slot_of[None, :] == jnp.arange(slot_total, dtype=jnp.int32)[:, None], usable[None, :]
    )
    candidate = jnp.max(jnp.where(matches[:, :, None], block_top[None], -jnp.inf), axis=1)
    merged_max = jnp.maximum(running_max, candidate)
    factor = jnp.where(matches[:, :, None], jnp.exp(block_top[None] - merged_max[:, None]), 0.0)
    rescale = jnp.exp(running_max - merged_max)
    denominator = denominator * rescale + jnp.sum(factor * block_total[None], axis=1)
    numerator = numerator * rescale[:, :, None] + jnp.einsum(
        "seh,ehd->shd", factor, summed, precision=lax.Precision.HIGHEST
    )
    return (merged_max, denominator, numerator)


def body(
    queries,
    new_kv,
    cache_pool,
    request_owner,
    block_req,
    migrate,
    residual_rows,
    w_out,
    w_gate,
    w_up,
    w_down,
):
    attn_count = lax.axis_size("attn")
    ffn_count = lax.axis_size("ffn")
    position = lax.axis_index("attn")
    req_dev = queries.shape[0]
    total_req = request_owner.shape[0]
    capacity = req_dev // 4
    slot_count = attn_count * capacity
    pool_count = cache_pool.shape[0]
    head_size = cache_pool.shape[2] // 2
    head_count = queries.shape[1] // head_size
    pair_room = migrate.shape[2]
    heavy_count = max(2, attn_count // 4)
    room_in = heavy_count + 1
    owner_grid = request_owner.reshape(attn_count, req_dev)
    order = jnp.arange(req_dev, dtype=jnp.int32)
    earlier = order[None, :] < order[:, None]
    same = owner_grid[:, :, None] == owner_grid[:, None, :]
    order_rank = jnp.sum(jnp.logical_and(same, earlier[None]), axis=2)
    within = (jnp.arange(attn_count, dtype=jnp.int32)[:, None] * capacity + order_rank).reshape(-1)
    mine_owner = lax.dynamic_slice_in_dim(owner_grid, position, 1, 0)[0]
    mine_rank = lax.dynamic_slice_in_dim(order_rank, position, 1, 0)[0]
    target_slot = mine_owner * capacity + mine_rank
    picker = (jnp.arange(slot_count, dtype=jnp.int32)[:, None] == target_slot[None, :]).astype(
        jnp.bfloat16
    )
    send_queries = jnp.dot(picker, queries, preferred_element_type=jnp.float32).astype(jnp.bfloat16)
    send_kv = jnp.dot(picker, new_kv, preferred_element_type=jnp.float32).astype(jnp.bfloat16)
    received = (
        lax.all_to_all(
            send_queries.reshape(attn_count, capacity, -1),
            "attn",
            split_axis=0,
            concat_axis=0,
            tiled=True,
        ),
        lax.all_to_all(
            send_kv.reshape(attn_count, capacity, -1),
            "attn",
            split_axis=0,
            concat_axis=0,
            tiled=True,
        ),
    )
    slot_queries = received[0].reshape(slot_count, head_count * head_size)
    slot_kv = received[1].reshape(slot_count, 2 * head_size)
    own_score = jnp.einsum(
        "shd,sd->sh",
        slot_queries.reshape(slot_count, head_count, head_size),
        slot_kv[:, :head_size],
        preferred_element_type=jnp.float32,
    ) * head_size ** (-0.5)
    own_value = jnp.broadcast_to(
        slot_kv[:, None, head_size:].astype(jnp.float32), (slot_count, head_count, head_size)
    )
    carried = (own_score, jnp.ones_like(own_score), own_value)
    my_req = lax.dynamic_slice_in_dim(block_req, position, 1, 0)[0]
    live_count = jnp.sum((my_req < total_req).astype(jnp.int32))
    block_slot = within[jnp.minimum(my_req, total_req - 1)]
    my_moves = lax.dynamic_slice_in_dim(migrate, position, 1, 0)[0]
    sent_usable = (my_moves < pool_count).reshape(-1)
    sent_index = jnp.minimum(my_moves, pool_count - 1).reshape(-1)
    sent_blocks = jnp.take(cache_pool, sent_index, axis=0)
    sent_blocks = jnp.where(sent_usable[:, None, None], sent_blocks, jnp.zeros_like(sent_blocks))
    sent_blocks = sent_blocks.reshape(attn_count, pair_room, cache_pool.shape[1], 2 * head_size)
    landed = lax.all_to_all(sent_blocks, "attn", split_axis=0, concat_axis=0, tiled=True)

    def advance(block_index, partials):
        top_all, total_all, summed_all = partials
        block_data = lax.dynamic_slice_in_dim(cache_pool, block_index, 1, 0)
        query_row = lax.dynamic_slice_in_dim(slot_queries, block_slot[block_index], 1, 0)
        block_top, block_total, summed = block_terms(block_data, query_row, head_count)
        return (
            lax.dynamic_update_slice_in_dim(top_all, block_top, block_index, 0),
            lax.dynamic_update_slice_in_dim(total_all, block_total, block_index, 0),
            lax.dynamic_update_slice_in_dim(summed_all, summed, block_index, 0),
        )

    initial = (
        jnp.zeros((pool_count, head_count), jnp.float32),
        jnp.zeros((pool_count, head_count), jnp.float32),
        jnp.zeros((pool_count, head_count, head_size), jnp.float32),
    )
    partials = lax.fori_loop(0, live_count, advance, initial)
    usable = jnp.arange(pool_count, dtype=jnp.int32) < live_count
    partials, usable = (partials, usable)
    carried = absorb(carried, block_slot, usable, partials[0], partials[1], partials[2])
    running_max, denominator, numerator = carried
    attention = (
        (numerator / denominator[:, :, None])
        .astype(jnp.bfloat16)
        .reshape(slot_count, head_count * head_size)
    )
    incoming = lax.dynamic_slice_in_dim(migrate, position, 1, 1)[:, 0, :].reshape(-1)
    came_usable = incoming < pool_count
    position_in = jnp.cumsum(came_usable.astype(jnp.int32)) - 1
    lanes = jnp.arange(room_in, dtype=jnp.int32)
    matches = jnp.logical_and(came_usable[None, :], position_in[None, :] == lanes[:, None])
    present = jnp.any(matches, axis=1)
    chosen = jnp.argmax(matches, axis=1)
    landed_flat = landed.reshape(attn_count * pair_room, landed.shape[2], landed.shape[3])
    arrived = jnp.take(landed_flat, chosen, axis=0)
    arrived = jnp.where(present[:, None, None], arrived, jnp.zeros_like(arrived))
    slot_global = request_owner * slot_count + within
    projected_slots = jnp.dot(
        lax.all_gather(attention, "attn", axis=0, tiled=True),
        w_out,
        preferred_element_type=jnp.float32,
    )
    projected = jnp.take(projected_slots, slot_global, axis=0)
    output_sum = lax.psum(projected, "ffn")
    mixed = (residual_rows.astype(jnp.float32) + output_sum).astype(jnp.bfloat16)
    gate_part = jnp.dot(mixed, w_gate, preferred_element_type=jnp.float32)
    up_part = jnp.dot(mixed, w_up, preferred_element_type=jnp.float32)
    gate_sum, up_sum = lax.psum((gate_part, up_part), "attn")
    hidden = (jax.nn.silu(gate_sum) * up_sum).astype(jnp.bfloat16)
    row_share = total_req // ffn_count
    down_share = lax.psum_scatter(
        jnp.dot(hidden, w_down, preferred_element_type=jnp.float32),
        "ffn",
        scatter_dimension=0,
        tiled=True,
    )
    kept_rows = lax.dynamic_slice_in_dim(mixed, lax.axis_index("ffn") * row_share, row_share, 0)
    ffn_out = (kept_rows.astype(jnp.float32) + down_share).astype(jnp.bfloat16)
    return (attention, arrived, ffn_out)


def solution(mesh):
    placed = (
        P(("groups", "attn"), "ffn"),
        P(("groups", "attn"), None),
        P(("groups", "attn"), None, None),
        P("groups"),
        P("groups", None),
        P("groups", None, None),
        P("groups", "attn"),
        P("ffn", "attn"),
        P("attn", "ffn"),
        P("attn", "ffn"),
        P("ffn", "attn"),
    )
    return jax.shard_map(
        body,
        mesh=mesh,
        in_specs=placed,
        out_specs=(
            P(("groups", "attn"), "ffn"),
            P(("groups", "attn"), None, None),
            P(("groups", "ffn"), "attn"),
        ),
        check_vma=False,
    )
```

profile of v0, /device:TPU:0, one launch (start us, length us, event | category | flops | bytes accessed | tf_op | source)
XLA Modules:
  0.0 348.8 jit_solution(17341339108561581605)
XLA Ops:
  8.2 1.5 fusion.9
  9.7 4.2 %all-to-all-start = ((bf16[4,8,512]{2,1,0:T(8,128)(2,1)}), bf16[4,8,512]{2,1,0:T(8,128)(2,1)S(1)}, u32[]{:S(2)}, u32[]{:S(2)}) async-start(bf16[4,8,512]{2,1,0:T(8,128)(2,1)} %fusion.9), calls=%async_computation | async-start | bytes 65536 | tf_op jit(solution)/shard_map/all_to_all | solution.py:87
  14.6 1.4 fusion.26
  18.6 3.4 all-to-all-start.1
  22.1 5.9 %all-to-all-done.1 = bf16[4,8,4096]{2,1,0:T(8,128)(2,1)S(1)} async-done(((bf16[4,8,4096]{2,1,0:T(8,128)(2,1)}), bf16[4,8,4096]{2,1,0:T(8,128)(2,1)S(1)}, u32[]{:S(2)}, u32[]{:S(2)}) %all-to-all-start.1) | async-done | bytes 262176 | tf_op jit(solution)/shard_map/all_to_all | solution.py:80
  28.1 84.9 %while.14 = (s32[]{:T(128)}, f32[14,16]{1,0:T(8,128)S(1)}, f32[14,16]{1,0:T(8,128)S(1)}, f32[14,16,256]{2,0,1:T(8,128)S(1)}, s32[]{:T(128)}, /*index=5*/s32[14]{...) while((s32[]{:T(128)}, f32[14,16]{1,0:T(8,128)S(1)}, ...), condition=%wide.region_5.6_spmd, body=%wide.region_2.5_spmd.sunk | while | flops 4227049 | bytes 434933 | solution.py:134
  31.4 1.2 fusion.52
  37.4 1.2 fusion.52
  43.4 1.2 fusion.52
  49.4 1.2 fusion.52
  55.4 1.2 fusion.52
  61.4 1.2 fusion.52
  67.4 1.2 fusion.52
  73.5 1.2 fusion.52
  79.5 1.2 fusion.52
  85.5 1.2 fusion.52
  91.5 1.2 fusion.52
  97.5 1.2 fusion.52
  103.5 1.2 fusion.52
  115.5 17.6 %all-gather.2.cloned.1.call-done = bf16[128,4096]{1,0:T(8,128)(2,1)} async-done(((bf16[32,4096]{1,0:T(8,128)(2,1)}), bf16[128,4096]{1,0:T(8,128)(2,1)}) %all-gather.2.cloned.1.call-update) | async-done | bytes 1048592 | tf_op jit(solution)/shard_map/all_gather | solution.py:156
  133.1 7.6 %fusion.34 = f32[128,1792]{1,0:T(8,128)S(1)} fusion(bf16[128,4096]{1,0:T(8,128)(2,1)} %all-gather.2.cloned.1.call-done, bf16[4096,1792]{1,0:T(8,128)(2,1)} %param.20), kind=kOutput, calls=%fused_computation.92 | convolution fusion | flops 1879048192 | bytes 16646144 | tf_op jit(solution)/shard_map/dot_general | solution.py:155
  142.8 47.9 %all-reduce.4.cloned.1.call-done = f32[128,1792]{1,0:T(8,128)} async-done(((f32[128,1792]{1,0:T(8,128)}), f32[128,1792]{1,0:T(8,128)}) %all-reduce.4.cloned.1.call-update) | async-done | bytes 917520 | tf_op jit(solution)/shard_map/psum | solution.py:161
  190.7 1.3 add_convert_fusion
  192.0 9.5 %fusion.35 = f32[128,4608]{1,0:T(8,128)} fusion(bf16[128,1792]{1,0:T(8,128)(2,1)S(1)} %add_convert_fusion, bf16[1792,4608]{1,0:T(8,128)(2,1)} %param.21), kind=kOutput, calls=%fused_computation.93 | convolution fusion | flops 2113929216 | bytes 19333120 | tf_op jit(solution)/shard_map/dot_general | solution.py:163
  201.4 9.5 %fusion.36 = f32[128,4608]{1,0:T(8,128)} fusion(bf16[128,1792]{1,0:T(8,128)(2,1)S(1)} %add_convert_fusion, bf16[1792,4608]{1,0:T(8,128)(2,1)} %param.22), kind=kOutput, calls=%fused_computation.94 | convolution fusion | flops 2113929216 | bytes 19333120 | tf_op jit(solution)/shard_map/dot_general | solution.py:164
  211.6 2.7 gather_fusion.1
  214.3 90.3 %all-reduce.6.cloned.1.call-done = (f32[128,4608]{1,0:T(8,128)}, f32[128,4608]{1,0:T(8,128)}) async-done(((f32[128,4608]{1,0:T(8,128)}, f32[128,4608]{1,0:T(8,128)}), (f32[128,4608]{1,0:T(8,128)}, f32[128,4608]{1,0:T(8,128)})) %all-reduce.6.cloned.1.call-update) | async-done | bytes 4718608 | tf_op jit(solution)/shard_map/psum | solution.py:165
  304.5 10.7 %fusion.6 = f32[128,1792]{1,0:T(8,128)} fusion(bf16[4608,1792]{1,0:T(8,128)(2,1)} %param.23, f32[128,4608]{1,0:T(8,128)} %get-tuple-element.69, f32[128,4608]{1,0:T(8,128)} %get-tuple-element.70), kind=kOutput, calls=%fused_computation.20 | convolution fusion | flops 2117468160 | bytes 22151168 | tf_op jit(solution)/shard_map/dot_general | solution.py:169
  316.5 3.5 %all-to-all-start.2 = ((bf16[4,1,256,512]{3,2,1,0:T(8,128)(2,1)}), bf16[4,1,256,512]{3,2,1,0:T(8,128)(2,1)S(1)}, u32[]{:S(2)}, u32[]{:S(2)}) async-start(bf16[4,1,256,512]{3,2,1,0:T(8,128)(2,1)} %fusion.10), calls=%async_computation.2 | async-start | bytes 2097152 | tf_op jit(solution)/shard_map/all_to_all | solution.py:116
  321.4 13.0 %all-to-all-done.2 = bf16[4,1,256,512]{3,2,1,0:T(8,128)(2,1)S(1)} async-done(((bf16[4,1,256,512]{3,2,1,0:T(8,128)(2,1)}), bf16[4,1,256,512]{3,2,1,0:T(8,128)(2,1)S(1)}, u32[]{:S(2)}, u32[]{:S(2)}) %all-to-all-start.2) | async-done | bytes 1048608 | tf_op jit(solution)/shard_map/all_to_all | solution.py:116
  336.1 4.6 %reduce-scatter.2.cloned.1.call-done = f32[32,1792]{1,0:T(8,128)} async-done(((f32[128,1792]{1,0:T(8,128)}), f32[32,1792]{1,0:T(8,128)}) %reduce-scatter.2.cloned.1.call-update) | async-done | bytes 229392 | tf_op jit(solution)/shard_map/reduce_scatter | solution.py:168
  340.7 1.6 add_convert_fusion.1
  (194 shorter events, 45.0 us)
Async XLA Ops:
  7.2 10.5 %copy-start = (bf16[32,4096]{1,0:T(8,128)(2,1)S(1)}, bf16[32,4096]{1,0:T(8,128)(2,1)}, u32[]{:S(2)}) copy-start(bf16[32,4096]{1,0:T(8,128)(2,1)} %param.13) | copy-start | bytes 786436
  9.7 8.9 %all-to-all-start = ((bf16[4,8,512]{2,1,0:T(8,128)(2,1)}), bf16[4,8,512]{2,1,0:T(8,128)(2,1)S(1)}, u32[]{:S(2)}, u32[]{:S(2)}) async-start(bf16[4,8,512]{2,1,0:T(8,128)(2,1)} %fusion.9), calls=%async_computation | async-start | bytes 65536 | tf_op jit(solution)/shard_map/all_to_all | solution.py:87
  18.6 9.4 %all-to-all-start.1 = ((bf16[4,8,4096]{2,1,0:T(8,128)(2,1)}), bf16[4,8,4096]{2,1,0:T(8,128)(2,1)S(1)}, u32[]{:S(2)}, u32[]{:S(2)}) async-start(bf16[4,8,4096]{2,1,0:T(8,128)(2,1)} %fusion.2), calls=%async_computation.1 | async-start | bytes 524288 | tf_op jit(solution)/shard_map/all_to_all | solution.py:80
  22.0 93.5 %copy-start.4 = (s32[128]{0:T(128)S(1)}, s32[128]{0:T(128)}, u32[]{:S(2)}) copy-start(s32[128]{0:T(128)} %param.16) | copy-start | bytes 1540
  22.0 111.1 %all-gather.2.cloned.1.call-start = ((), (), s32[]{:S(2)}) async-start(), calls=%async_computation.4 | async-start | bytes 1310720 | tf_op jit(solution)/shard_map/all_gather | solution.py:156
  115.4 75.3 %all-reduce.4.cloned.1.call-start = ((), (), s32[]{:S(2)}) async-start(), calls=%async_computation.5 | async-start | bytes 1835008 | tf_op jit(solution)/shard_map/psum | solution.py:161
  140.7 50.0 %copy-start.2 = (bf16[128,1792]{1,0:T(8,128)(2,1)S(1)}, bf16[128,1792]{1,0:T(8,128)(2,1)}, u32[]{:S(2)}) copy-start(bf16[128,1792]{1,0:T(8,128)(2,1)} %param.19) | copy-start | bytes 1376260
  142.8 161.7 %all-reduce.6.cloned.1.call-start = ((), (), s32[]{:S(2)}) async-start(), calls=%async_computation.7 | async-start | bytes 9437184 | tf_op jit(solution)/shard_map/psum | solution.py:165
  210.9 0.7 copy-start.3
  210.9 129.8 %reduce-scatter.2.cloned.1.call-start = ((), (), s32[]{:S(2)}) async-start(), calls=%async_computation.6 | async-start | bytes 1146880 | tf_op jit(solution)/shard_map/reduce_scatter | solution.py:168
  315.3 27.0 %copy-start.1 = (bf16[32,4096]{1,0:T(8,128)(2,1)S(1)}, bf16[32,4096]{1,0:T(8,128)(2,1)}, u32[]{:S(2)}) copy-start(bf16[32,4096]{1,0:T(8,128)(2,1)} %param.13) | copy-start | bytes 786436
  316.5 18.0 %all-to-all-start.2 = ((bf16[4,1,256,512]{3,2,1,0:T(8,128)(2,1)}), bf16[4,1,256,512]{3,2,1,0:T(8,128)(2,1)S(1)}, u32[]{:S(2)}, u32[]{:S(2)}) async-start(bf16[4,1,256,512]{3,2,1,0:T(8,128)(2,1)} %fusion.10), calls=%async_computation.2 | async-start | bytes 2097152 | tf_op jit(solution)/shard_map/all_to_all | solution.py:116
Sparse Core Ops, SparseCore 0:
  115.5 17.5 all-gather.1
  142.9 47.7 all-reduce.3
  211.0 93.4 all-reduce.5
  315.4 25.2 reduce-scatter.1
where the time goes:
time: 350 us; the launch traced here: 349 us
  waiting for transfers between devices  179 us (51%)
  matrix products  72.8 us (21%)
  loops' own time  38.2 us (11%)
  local copies, waits for them, and re-layouts  19.2 us (5%)
  between operations  14 us (4%)
  other arithmetic  13.8 us (4%)
  starting transfers between devices  11.5 us (3%)
    psum x1, waiting for transfers between devices, body(): gate_sum, up_sum = lax.psum((gate_part, up_part), 'attn')  90.3 us
    psum x1, waiting for transfers between devices, body(): output_sum = lax.psum(projected, 'ffn')  47.9 us
    another operation x1, loops' own time, body(): partials = lax.fori_loop(0, live_count, advance, initial)  38.2 us
    all_gather x1, waiting for transfers between devices, body(): lax.all_gather(attention, 'attn', axis=0, tiled=True)  17.6 us
    dot_general x14, matrix products, block_terms(): jnp.einsum('ehd,etd->eht', queries3, key_part, preferred_element_type=jnp...  16.7 us
    dot_general x14, matrix products, block_terms(): jnp.einsum('eht,etd->ehd', weight, value_part, preferred_element_type=jnp...  15.3 us
    all_to_all x1, waiting for transfers between devices, body(): lax.all_to_all(sent_blocks, 'attn', split_axis=0, concat_axis=0, tiled=True)  13 us
    dot_general x1, matrix products, body(): jnp.dot(hidden, w_down, preferred_element_type=jnp.float32)  10.7 us
  transfers between devices with their start and end apart: 7, of which 6 were waited for; matrix products, arithmetic and copies ran while one was open for 3% of the time, Pallas kernels for 0%

commit v1 on v0

v1 whole, which is shorter than its diff:
```python
import functools

import jax
import jax.numpy as jnp
from jax import lax
from jax.experimental import pallas as pl
from jax.experimental.pallas import tpu as pltpu
from jax.sharding import PartitionSpec as P

CHUNKS = 2


def attention_kernel(
    slot_ref, live_ref, q_ref, kv_ref, pool_ref, out_ref, pages, sems, q3, top_ref, den_ref, num_ref
):
    page_count = pages.shape[0]
    heads, size = q3.shape[1], q3.shape[2]
    lanes = top_ref.shape[2]
    scale = size ** (-0.5)
    copies = [
        pltpu.make_async_copy(pool_ref.at[b], pages.at[b], sems.at[b]) for b in range(page_count)
    ]
    for copy in copies:
        copy.start()
    for h in range(heads):
        q3[:, h, :] = q_ref[:, h * size : (h + 1) * size].astype(jnp.float32)
    key = kv_ref[:, :size].astype(jnp.float32)
    own = jnp.sum(q3[...] * key[:, None, :], axis=2, keepdims=True) * scale
    top_ref[...] = jnp.broadcast_to(own, top_ref.shape)
    den_ref[...] = jnp.ones_like(den_ref)
    num_ref[...] = jnp.broadcast_to(kv_ref[:, size:].astype(jnp.float32)[:, None, :], num_ref.shape)
    terms = []
    for b in range(page_count):
        copies[b].wait()
        q = q3[slot_ref[b]].astype(jnp.bfloat16)
        scores = (
            lax.dot_general(
                q, pages[b, :, :size], (((1,), (1,)), ((), ())), preferred_element_type=jnp.float32
            )
            * scale
        )
        top = jnp.max(scores, axis=1, keepdims=True)
        weight = jnp.exp(scores - top).astype(jnp.bfloat16)
        total = jnp.sum(weight.astype(jnp.float32), axis=1, keepdims=True)
        summed = jnp.dot(weight, pages[b, :, size:], preferred_element_type=jnp.float32)
        top = jnp.where(b < live_ref[0], top, -jnp.inf)
        terms.append((top, total, summed))
    for b in range(page_count):
        top, total, summed = terms[b]
        slot = slot_ref[b]
        old = top_ref[slot]
        top = jnp.broadcast_to(top, old.shape)
        new = jnp.maximum(old, top)
        keep = jnp.exp(old - new)
        take = jnp.exp(top - new)
        top_ref[slot] = new
        den_ref[slot] = den_ref[slot] * keep + take * total
        num_ref[slot] = num_ref[slot] * keep[:, :1] + take[:, :1] * summed
    for h in range(heads):
        out_ref[:, h * size : (h + 1) * size] = (num_ref[:, h, :] / den_ref[:, h, :1]).astype(
            out_ref.dtype
        )


def attend(block_slot, live, slot_queries, slot_kv, cache_pool, heads, size):
    slots = slot_queries.shape[0]
    page_count = cache_pool.shape[0]
    smem = pl.BlockSpec(memory_space=pltpu.SMEM)
    vmem = pl.BlockSpec(memory_space=pltpu.VMEM)
    return pl.pallas_call(
        attention_kernel,
        out_shape=jax.ShapeDtypeStruct(slot_queries.shape, jnp.bfloat16),
        in_specs=[smem, smem, vmem, vmem, pl.BlockSpec(memory_space=pl.ANY)],
        out_specs=vmem,
        scratch_shapes=[
            pltpu.VMEM(cache_pool.shape, jnp.bfloat16),
            pltpu.SemaphoreType.DMA((page_count,)),
            pltpu.VMEM((slots, heads, size), jnp.float32),
            pltpu.VMEM((slots, heads, 128), jnp.float32),
            pltpu.VMEM((slots, heads, 128), jnp.float32),
            pltpu.VMEM((slots, heads, size), jnp.float32),
        ],
        compiler_params=pltpu.CompilerParams(vmem_limit_bytes=40 * 2**20),
        name="attention",
    )(block_slot, live, slot_queries, slot_kv, cache_pool)


def swap_perm(count, bit):
    return [(i, i ^ bit) for i in range(count)]


def block_swap(x, bit, on):
    order = jnp.stack([x[j ^ bit] for j in range(4)])
    return jnp.where(on, order, x)


def body(
    queries,
    new_kv,
    cache_pool,
    request_owner,
    block_req,
    migrate,
    residual_rows,
    w_out,
    w_gate,
    w_up,
    w_down,
):
    attn_count = lax.axis_size("attn")
    ffn_count = lax.axis_size("ffn")
    position = lax.axis_index("attn")
    ffn_position = lax.axis_index("ffn")
    req_dev = queries.shape[0]
    total_req = request_owner.shape[0]
    capacity = req_dev // 4
    slot_count = attn_count * capacity
    pool_count = cache_pool.shape[0]
    head_size = cache_pool.shape[2] // 2
    head_count = queries.shape[1] // head_size
    width = queries.shape[1]
    pair_room = migrate.shape[2]
    room_in = max(2, attn_count // 4) + 1
    paired = attn_count == 4

    owner_grid = request_owner.reshape(attn_count, req_dev)
    order = jnp.arange(req_dev, dtype=jnp.int32)
    earlier = order[None, :] < order[:, None]
    same = owner_grid[:, :, None] == owner_grid[:, None, :]
    order_rank = jnp.sum(jnp.logical_and(same, earlier[None]), axis=2)
    within = (jnp.arange(attn_count, dtype=jnp.int32)[:, None] * capacity + order_rank).reshape(-1)
    mine_owner = lax.dynamic_slice_in_dim(owner_grid, position, 1, 0)[0]
    mine_rank = lax.dynamic_slice_in_dim(order_rank, position, 1, 0)[0]
    target_slot = mine_owner * capacity + mine_rank
    picker = (jnp.arange(slot_count, dtype=jnp.int32)[:, None] == target_slot[None, :]).astype(
        jnp.bfloat16
    )
    send = jnp.dot(
        picker, jnp.concatenate([queries, new_kv], axis=1), preferred_element_type=jnp.float32
    ).astype(jnp.bfloat16)
    received = lax.all_to_all(
        send.reshape(attn_count, capacity, -1), "attn", split_axis=0, concat_axis=0, tiled=True
    ).reshape(slot_count, -1)
    my_req = lax.dynamic_slice_in_dim(block_req, position, 1, 0)[0]
    live_count = jnp.sum((my_req < total_req).astype(jnp.int32))
    block_slot = within[jnp.minimum(my_req, total_req - 1)]
    attention = attend(
        block_slot,
        live_count.reshape(1),
        received[:, :width],
        received[:, width:],
        cache_pool,
        head_count,
        head_size,
    )

    if paired:
        across = lax.ppermute(attention, "attn", swap_perm(4, 2))
        pair = jnp.concatenate([attention, across], axis=0)
        other = lax.ppermute(pair, "attn", swap_perm(4, 1))
        everyone = jnp.concatenate([pair, other], axis=0)
        distance = jnp.bitwise_xor(request_owner, position)
        place = distance // 2 + (distance % 2) * 2
    else:
        everyone = lax.all_gather(attention, "attn", axis=0, tiled=True)
        place = request_owner
    row_of = place * slot_count + within
    row_picker = (
        row_of[:, None] == jnp.arange(attn_count * slot_count, dtype=jnp.int32)[None, :]
    ).astype(jnp.bfloat16)
    ordered = jnp.dot(row_picker, everyone, preferred_element_type=jnp.float32).astype(jnp.bfloat16)

    row_share = total_req // ffn_count
    columns = w_out.shape[1]
    projected = jnp.dot(ordered, w_out, preferred_element_type=jnp.float32).astype(jnp.bfloat16)
    parts = lax.all_to_all(
        projected.reshape(ffn_count, row_share, columns), "ffn", split_axis=0, concat_axis=0, tiled=True
    )
    kept_residual = lax.dynamic_slice_in_dim(residual_rows, ffn_position * row_share, row_share, 0)
    kept = (
        kept_residual.astype(jnp.float32) + jnp.sum(parts.astype(jnp.float32), axis=0)
    ).astype(jnp.bfloat16)
    mixed = lax.all_to_all(
        jnp.broadcast_to(kept[None], (ffn_count, row_share, columns)),
        "ffn",
        split_axis=0,
        concat_axis=0,
        tiled=True,
    )

    my_moves = lax.dynamic_slice_in_dim(migrate, position, 1, 0)[0]
    sent_usable = (my_moves < pool_count).reshape(-1)
    sent_index = jnp.minimum(my_moves, pool_count - 1).reshape(-1)
    sent_blocks = jnp.take(cache_pool, sent_index, axis=0)
    sent_blocks = jnp.where(sent_usable[:, None, None], sent_blocks, jnp.zeros_like(sent_blocks))
    sent_blocks = sent_blocks.reshape(attn_count, pair_room, cache_pool.shape[1], 2 * head_size)
    sent_blocks, _ = lax.optimization_barrier((sent_blocks, attention))
    landed = lax.all_to_all(sent_blocks, "attn", split_axis=0, concat_axis=0, tiled=True)
    incoming = lax.dynamic_slice_in_dim(migrate, position, 1, 1)[:, 0, :].reshape(-1)
    came_usable = incoming < pool_count
    position_in = jnp.cumsum(came_usable.astype(jnp.int32)) - 1
    lanes = jnp.arange(room_in, dtype=jnp.int32)
    matches = jnp.logical_and(came_usable[None, :], position_in[None, :] == lanes[:, None])
    present = jnp.any(matches, axis=1)
    chosen = jnp.argmax(matches, axis=1)
    landed_flat = landed.reshape(attn_count * pair_room, landed.shape[2], landed.shape[3])
    arrived = jnp.take(landed_flat, chosen, axis=0)
    arrived = jnp.where(present[:, None, None], arrived, jnp.zeros_like(arrived))

    hidden_width = w_gate.shape[1]
    step = hidden_width // CHUNKS
    if paired:
        low, high = position % 2 == 1, position >= 2
        mixed4 = mixed.reshape(4, total_req // 4, columns)
        mixed4 = block_swap(block_swap(mixed4, 1, low), 2, high)
        rows = mixed4.reshape(total_req, columns)
        down = None
        for c in range(CHUNKS):
            cut = slice(c * step, (c + 1) * step)
            gate = jnp.dot(rows, w_gate[:, cut], preferred_element_type=jnp.float32)
            up = jnp.dot(rows, w_up[:, cut], preferred_element_type=jnp.float32)
            both = jnp.stack([gate, up]).reshape(2, 4, total_req // 4, step)
            sent = jnp.stack([both[:, 1], both[:, 3]]).astype(jnp.bfloat16)
            sib = lax.ppermute(sent, "attn", swap_perm(4, 1)).astype(jnp.float32)
            near = both[:, 0] + sib[0]
            far = (both[:, 2] + sib[1]).astype(jnp.bfloat16)
            sums = near + lax.ppermute(far, "attn", swap_perm(4, 2)).astype(jnp.float32)
            quarter = (jax.nn.silu(sums[0]) * sums[1]).astype(jnp.bfloat16)
            half = jnp.stack([quarter, lax.ppermute(quarter, "attn", swap_perm(4, 2))])
            other = lax.ppermute(half, "attn", swap_perm(4, 1))
            hidden = jnp.stack([half[0], other[0], half[1], other[1]]).reshape(total_req, step)
            term = jnp.dot(hidden, w_down[cut], preferred_element_type=jnp.float32)
            down = term if down is None else down + term
        down4 = down.astype(jnp.bfloat16).reshape(4, total_req // 4, columns)
        down4 = block_swap(block_swap(down4, 1, low), 2, high)
        down = down4.reshape(total_req, columns)
    else:
        rows = mixed.reshape(total_req, columns)
        gate = jnp.dot(rows, w_gate, preferred_element_type=jnp.float32)
        up = jnp.dot(rows, w_up, preferred_element_type=jnp.float32)
        gate, up = lax.psum_scatter((gate, up), "attn", scatter_dimension=0, tiled=True)
        quarter = (jax.nn.silu(gate) * up).astype(jnp.bfloat16)
        hidden = lax.all_gather(quarter, "attn", axis=0, tiled=True)
        down = jnp.dot(hidden, w_down, preferred_element_type=jnp.float32).astype(jnp.bfloat16)
    shares = lax.all_to_all(
        down.reshape(ffn_count, row_share, columns), "ffn", split_axis=0, concat_axis=0, tiled=True
    )
    ffn_out = (kept.astype(jnp.float32) + jnp.sum(shares.astype(jnp.float32), axis=0)).astype(
        jnp.bfloat16
    )
    return (attention, arrived, ffn_out)


def solution(mesh):
    placed = (
        P(("groups", "attn"), "ffn"),
        P(("groups", "attn"), None),
        P(("groups", "attn"), None, None),
        P("groups"),
        P("groups", None),
        P("groups", None, None),
        P("groups", "attn"),
        P("ffn", "attn"),
        P("attn", "ffn"),
        P("attn", "ffn"),
        P("ffn", "attn"),
    )
    return jax.shard_map(
        body,
        mesh=mesh,
        in_specs=placed,
        out_specs=(
            P(("groups", "attn"), "ffn"),
            P(("groups", "attn"), None, None),
            P(("groups", "ffn"), "attn"),
        ),
        check_vma=False,
    )
```

time: 350 us -> 147 us (0.42)
  waiting for transfers between devices: 179 us -> 63 us
  matrix products: 72.8 us -> 25.7 us
  loops' own time: 38.2 us -> 0 us
  starting transfers between devices: 11.5 us -> 28 us
  between operations: 14 us -> 1.19 us
  local copies, waits for them, and re-layouts: 19.2 us -> 8.12 us
  Pallas kernels: 0 us -> 9.04 us
    psum x2 -> x0, waiting for transfers between devices: 138 us -> none  [the longest x1 90.3 us: body(): gate_sum, up_sum = lax.psum((gate_part, up_part), 'attn')]
    dot_general x36 -> x8, matrix products: 72.8 us -> 25.7 us  [the longest x2 10.2 us: body(): gate = jnp.dot(rows, w_gate[:, cut], preferred_element_type=jnp.float32)]
    another operation x1 -> x0, loops' own time: 38.2 us -> none  [body(): partials = lax.fori_loop(0, live_count, advance, initial)]
    all_to_all x2 -> x4, waiting for transfers between devices: 5.93 us -> 36.2 us  [the longest x1 11.8 us: body(): lax.all_to_all(down.reshape(ffn_count, row_share, columns), 'ffn', split_...]
    ppermute x0 -> x10, waiting for transfers between devices: none -> 26.8 us  [the longest x2 11.4 us: body(): sums = near + lax.ppermute(far, 'attn', swap_perm(4, 2)).astype(jnp.float32)]
    all_gather x1 -> x0, waiting for transfers between devices: 17.6 us -> none  [body(): lax.all_gather(attention, 'attn', axis=0, tiled=True)]
    all_to_all x1, waiting for transfers between devices: 13 us -> 0.01 us  [body(): lax.all_to_all(sent_blocks, 'attn', split_axis=0, concat_axis=0, tiled=True)]
    all_to_all x2 -> x4, starting transfers between devices: 7.64 us -> 16.8 us  [the longest x1 5.66 us: body(): lax.all_to_all(projected.reshape(ffn_count, row_share, columns), 'ffn', s...]
  transfers between devices with their start and end apart: 7 -> 15, of which waited for: 6 -> 12; matrix products, arithmetic and copies ran while one was open for 3% -> 19% of each run, Pallas kernels for 0% -> 0%
where the time goes in v1:
time: 147 us; the launch traced here: 146 us
  waiting for transfers between devices  63 us (43%)
  starting transfers between devices  28 us (19%)
  matrix products  25.7 us (17%)
  other arithmetic  11.3 us (8%)
  Pallas kernels  9.04 us (6%)
  local copies, waits for them, and re-layouts  8.12 us (6%)
    all_to_all x1, waiting for transfers between devices, body(): lax.all_to_all(down.reshape(ffn_count, row_share, columns), 'ffn', split_...  11.8 us
    ppermute x2, waiting for transfers between devices, body(): sums = near + lax.ppermute(far, 'attn', swap_perm(4, 2)).astype(jnp.float32)  11.4 us
    all_to_all x1, waiting for transfers between devices, body(): lax.all_to_all(jnp.broadcast_to(kept[None], (ffn_count, row_share, column...  10.8 us
    dot_general x2, matrix products, body(): gate = jnp.dot(rows, w_gate[:, cut], preferred_element_type=jnp.float32)  10.2 us
    all_to_all x1, waiting for transfers between devices, body(): lax.all_to_all(projected.reshape(ffn_count, row_share, columns), 'ffn', s...  9.99 us
    pallas_call x1, Pallas kernels, attend(): pl.pallas_call(attention_kernel, out_shape=jax.ShapeDtypeStruct(slot_quer...  9.04 us
    dot_general x1, matrix products, body(): jnp.dot(ordered, w_out, preferred_element_type=jnp.float32)  8.55 us
    ppermute x1, waiting for transfers between devices, body(): across = lax.ppermute(attention, 'attn', swap_perm(4, 2))  7.54 us
  transfers between devices with their start and end apart: 15, of which 12 were waited for; matrix products, arithmetic and copies ran while one was open for 19% of the time, Pallas kernels for 0%

profile of v1, /device:TPU:0, one launch (start us, length us, event | category | flops | bytes accessed | tf_op | source)
XLA Modules:
  0.0 146.3 jit_solution(63317232550032334)
XLA Ops:
  1.6 1.9 %fusion.16 = bf16[4,8,4608]{2,1,0:T(8,128)(2,1)} fusion(bf16[32,512]{1,0:T(8,128)(2,1)} %param.12, bf16[32,4096]{1,0:T(8,128)(2,1)} %param.11, s32[32]{0:T(128)S(1)} %fusion.85), kind=kOutput, calls=%fused_computation.20 | convolution fusion | flops 10175488 | bytes 589952 | tf_op jit(solution)/shard_map/dot_general | solution.py:138
  3.5 4.2 %all-to-all-start = ((bf16[4,8,4608]{2,1,0:T(8,128)(2,1)}), bf16[4,8,4608]{2,1,0:T(8,128)(2,1)S(1)}, u32[]{:S(2)}, u32[]{:S(2)}) async-start(bf16[4,8,4608]{2,1,0:T(8,128)(2,1)} %fusion.16), calls=%async_computation | async-start | bytes 589824 | tf_op jit(solution)/shard_map/all_to_all | solution.py:141
  9.3 1.3 fusion.80
  10.6 3.5 %all-to-all-done = bf16[4,8,4608]{2,1,0:T(8,128)(2,1)S(1)} async-done(((bf16[4,8,4608]{2,1,0:T(8,128)(2,1)}), bf16[4,8,4608]{2,1,0:T(8,128)(2,1)S(1)}, u32[]{:S(2)}, u32[]{:S(2)}) %all-to-all-start) | async-done | bytes 294944 | tf_op jit(solution)/shard_map/all_to_all | solution.py:141
  14.2 2.0 %copy-done = bf16[14,256,512]{2,1,0:T(8,128)(2,1)S(1)} copy-done((bf16[14,256,512]{2,1,0:T(8,128)(2,1)S(1)}, bf16[14,256,512]{2,1,0:T(8,128)(2,1)}, u32[]{:S(2)}) %copy-start) | copy-done | bytes 3670040
  16.2 9.0 %attention.1 = bf16[32,4096]{1,0:T(8,128)(2,1)} custom-call(s32[14]{0:T(128)S(1)} %gather_fusion, s32[1]{0:T(128)} %bitcast.2.live_ref, bf16[32,4096]{1,0:T(8,128)(2,1)S(1)} %slice.194.q_ref, bf16[32,512]{1,0:T(8,128)(2,1)S(1)} %slice.195.kv_ref, bf16[14,256,512]{2,1,0:T(8,128)(2,1)S(1)} %copy-done), custom_call_target="tpu_custom_call" | custom-call | tf_op jit(solution)/shard_map/attention/pallas_call | solution.py:70
  25.7 7.5 %collective-permute-done = bf16[32,4096]{1,0:T(8,128)(2,1)S(1)} collective-permute-done((bf16[32,4096]{1,0:T(8,128)(2,1)}, bf16[32,4096]{1,0:T(8,128)(2,1)S(1)}, u32[]{:S(2)}, u32[]{:S(2)}) %collective-permute-start) | collective-permute-done | bytes 262176 | tf_op jit(solution)/shard_map/ppermute | solution.py:158
  34.4 1.9 %collective-permute-done.1 = bf16[64,4096]{1,0:T(8,128)(2,1)S(1)} collective-permute-done((bf16[64,4096]{1,0:T(8,128)(2,1)S(1)}, bf16[64,4096]{1,0:T(8,128)(2,1)S(1)}, u32[]{:S(2)}, u32[]{:S(2)}) %collective-permute-start.1) | collective-permute-done | bytes 524320 | tf_op jit(solution)/shard_map/ppermute | solution.py:160
  36.2 8.5 %convolution_convert_fusion.2 = bf16[128,1792]{1,0:T(8,128)(2,1)} fusion(bf16[4096,1792]{1,0:T(8,128)(2,1)} %param.18, bf16[64,4096]{1,0:T(8,128)(2,1)S(1)} %collective-permute-done.1, bf16[32,4096]{1,0:T(8,128)(2,1)S(1)} %collective-permute-done, bf16[32,4096]{1,0:T(8,128)(2,1)} %attention.1, s32[128]{0:T(128)S(1)} %multiply_add_fusion), kind=kOutput, calls=%fused_computation.36 | convolution fusion | flops 2017181696 | bytes 16187904 | tf_op jit(solution)/shard_map/dot_general | solution.py:175
  44.8 5.7 %all-to-all-start.2 = ((bf16[4,32,1792]{2,1,0:T(8,128)(2,1)}), bf16[4,32,1792]{2,1,0:T(8,128)(2,1)S(1)}, u32[]{:S(2)}, u32[]{:S(2)}) async-start(bf16[4,32,1792]{2,1,0:T(8,128)(2,1)} %bitcast.13), calls=%async_computation.2 | async-start | bytes 917504 | tf_op jit(solution)/shard_map/all_to_all | solution.py:176
  50.5 2.7 %gather_fusion.1 = bf16[4,256,512]{2,1,0:T(8,128)(2,1)S(1)} fusion(bf16[14,256,512]{2,1,0:T(8,128)(2,1)} %pool_ref.1, s32[1024]{0:T(1024)S(1)} %pad_clamp_fusion.1), kind=kCustom, calls=%fused_computation.1 | custom fusion | bytes 2097168 | tf_op jit(solution)/shard_map/jit(_take)/gather | solution.py:194
  53.8 10.0 %all-to-all-done.2 = bf16[4,32,1792]{2,1,0:T(8,128)(2,1)S(1)} async-done(((bf16[4,32,1792]{2,1,0:T(8,128)(2,1)}), bf16[4,32,1792]{2,1,0:T(8,128)(2,1)S(1)}, u32[]{:S(2)}, u32[]{:S(2)}) %all-to-all-start.2) | async-done | bytes 458784 | tf_op jit(solution)/shard_map/all_to_all | solution.py:176
  65.6 3.5 %all-to-all-start.3 = ((bf16[4,32,1792]{2,1,0:T(8,128)(2,1)}), bf16[4,32,1792]{2,1,0:T(8,128)(2,1)S(1)}, u32[]{:S(2)}, u32[]{:S(2)}) async-start(bf16[4,32,1792]{2,1,0:T(8,128)(2,1)} %broadcast_in_dim.72), calls=%async_computation.3 | async-start | bytes 917504 | tf_op jit(solution)/shard_map/all_to_all | solution.py:183
  69.7 1.2 fusion.46
  70.9 10.8 %all-to-all-done.3 = bf16[4,32,1792]{2,1,0:T(8,128)(2,1)S(1)} async-done(((bf16[4,32,1792]{2,1,0:T(8,128)(2,1)}), bf16[4,32,1792]{2,1,0:T(8,128)(2,1)S(1)}, u32[]{:S(2)}, u32[]{:S(2)}) %all-to-all-start.3) | async-done | bytes 458784 | tf_op jit(solution)/shard_map/all_to_all | solution.py:183
  81.7 3.7 %all-to-all-start.1 = ((bf16[4,1,256,512]{3,2,1,0:T(8,128)(2,1)}), bf16[4,1,256,512]{3,2,1,0:T(8,128)(2,1)S(1)}, u32[]{:S(2)}, u32[]{:S(2)}) async-start(bf16[4,1,256,512]{3,2,1,0:T(8,128)(2,1)} %fusion.46), calls=%async_computation.1 | async-start | bytes 2097152 | tf_op jit(solution)/shard_map/all_to_all | solution.py:198
  85.7 4.8 %fusion.17 = f32[1,4,32,2304]{3,2,1,0:T(8,128)S(1)} fusion(bf16[4,32,1792]{2,1,0:T(8,128)(2,1)S(1)} %maximum_select_fusion.1, bf16[1792,4608]{1,0:T(8,128)(2,1)} %param.19), kind=kOutput, calls=%fused_computation.22 | convolution fusion | flops 1056964608 | bytes 9895936 | tf_op jit(solution)/shard_map/dot_general | solution.py:220
  90.5 5.4 %fusion.23 = f32[1,4,32,2304]{3,2,0,1:T(8,128)S(1)} fusion(bf16[4,32,1792]{2,1,0:T(8,128)(2,1)S(1)} %maximum_select_fusion.1, bf16[1792,4608]{1,0:T(8,128)(2,1)} %param.19), kind=kOutput, calls=%fused_computation.24 | convolution fusion | flops 1056964608 | bytes 9895936 | tf_op jit(solution)/shard_map/dot_general | solution.py:220
  96.2 1.3 fusion.20
  97.5 1.3 fusion.26
  99.8 1.2 collective-permute-done.2
  101.1 1.9 %collective-permute-start.3 = (bf16[2,32,2304]{2,1,0:T(8,128)(2,1)S(1)}, bf16[2,32,2304]{2,1,0:T(8,128)(2,1)S(1)}, u32[]{:S(2)}, u32[]{:S(2)}) collective-permute-start(bf16[2,32,2304]{2,1,0:T(8,128)(2,1)S(1)} %fusion.50), channel_id=1, source_target_pairs={{0,8},{4,12},{8,0},{12,4},{1,9},{5,13},{9,1},{13,5},{2,10},{6,14},... | collective-permute-start | bytes 884744 | tf_op jit(solution)/shard_map/ppermute | solution.py:227
  103.9 7.2 %collective-permute-done.3 = bf16[2,32,2304]{2,1,0:T(8,128)(2,1)S(1)} collective-permute-done((bf16[2,32,2304]{2,1,0:T(8,128)(2,1)S(1)}, bf16[2,32,2304]{2,1,0:T(8,128)(2,1)S(1)}, u32[]{:S(2)}, u32[]{:S(2)}) %collective-permute-start.3) | collective-permute-done | bytes 294944 | tf_op jit(solution)/shard_map/ppermute | solution.py:227
  111.3 1.9 %collective-permute-start.4 = (bf16[32,2304]{1,0:T(8,128)(2,1)S(1)}, bf16[32,2304]{1,0:T(8,128)(2,1)S(1)}, u32[]{:S(2)}, u32[]{:S(2)}) collective-permute-start(bf16[32,2304]{1,0:T(8,128)(2,1)S(1)} %fusion.68), channel_id=1, source_target_pairs={{0,8},{4,12},{8,0},{12,4},{1,9},{5,13},{9,1},{13,5},{2,10},{6,14},... | collective-permute-start | bytes 442376 | tf_op jit(solution)/shard_map/ppermute | solution.py:229
  113.2 4.2 %collective-permute-done.7 = bf16[2,32,2304]{2,1,0:T(8,128)(2,1)S(1)} collective-permute-done((bf16[2,32,2304]{2,1,0:T(8,128)(2,1)S(1)}, bf16[2,32,2304]{2,1,0:T(8,128)(2,1)S(1)}, u32[]{:S(2)}, u32[]{:S(2)}) %collective-permute-start.7) | collective-permute-done | bytes 294944 | tf_op jit(solution)/shard_map/ppermute | solution.py:227
  117.6 1.9 %collective-permute-start.8 = (bf16[32,2304]{1,0:T(8,128)(2,1)S(1)}, bf16[32,2304]{1,0:T(8,128)(2,1)S(1)}, u32[]{:S(2)}, u32[]{:S(2)}) collective-permute-start(bf16[32,2304]{1,0:T(8,128)(2,1)S(1)} %fusion.64), channel_id=1, source_target_pairs={{0,8},{4,12},{8,0},{12,4},{1,9},{5,13},{9,1},{13,5},{2,10},{6,14},... | collective-permute-start | bytes 442376 | tf_op jit(solution)/shard_map/ppermute | solution.py:229
  120.6 2.4 %collective-permute-done.8 = bf16[32,2304]{1,0:T(8,128)(2,1)S(1)} collective-permute-done((bf16[32,2304]{1,0:T(8,128)(2,1)S(1)}, bf16[32,2304]{1,0:T(8,128)(2,1)S(1)}, u32[]{:S(2)}, u32[]{:S(2)}) %collective-permute-start.8) | collective-permute-done | bytes 147488 | tf_op jit(solution)/shard_map/ppermute | solution.py:229
  123.3 1.4 collective-permute-done.9
  124.9 1.3 fusion.8
  126.2 1.3 fusion.32
  128.5 3.5 %all-to-all-start.4 = ((bf16[4,32,1792]{2,1,0:T(8,128)(2,1)}), bf16[4,32,1792]{2,1,0:T(8,128)(2,1)S(1)}, u32[]{:S(2)}, u32[]{:S(2)}) async-start(bf16[4,32,1792]{2,1,0:T(8,128)(2,1)} %maximum_select_fusion.3), calls=%async_computation.4 | async-start | bytes 917504 | tf_op jit(solution)/shard_map/all_to_all | solution.py:245
  133.7 11.8 %all-to-all-done.4 = bf16[4,32,1792]{2,1,0:T(8,128)(2,1)S(1)} async-done(((bf16[4,32,1792]{2,1,0:T(8,128)(2,1)}), bf16[4,32,1792]{2,1,0:T(8,128)(2,1)S(1)}, u32[]{:S(2)}, u32[]{:S(2)}) %all-to-all-start.4) | async-done | bytes 458784 | tf_op jit(solution)/shard_map/all_to_all | solution.py:245
  (97 shorter events, 15.1 us)
Async XLA Ops:
  3.5 10.6 %all-to-all-start = ((bf16[4,8,4608]{2,1,0:T(8,128)(2,1)}), bf16[4,8,4608]{2,1,0:T(8,128)(2,1)S(1)}, u32[]{:S(2)}, u32[]{:S(2)}) async-start(bf16[4,8,4608]{2,1,0:T(8,128)(2,1)} %fusion.16), calls=%async_computation | async-start | bytes 589824 | tf_op jit(solution)/shard_map/all_to_all | solution.py:141
  14.2 2.0 %copy-start = (bf16[14,256,512]{2,1,0:T(8,128)(2,1)S(1)}, bf16[14,256,512]{2,1,0:T(8,128)(2,1)}, u32[]{:S(2)}) copy-start(bf16[14,256,512]{2,1,0:T(8,128)(2,1)} %pool_ref.1) | copy-start | bytes 11010052
  16.2 18.1 %copy-start.2 = (s32[128]{0:T(128)S(1)}, s32[128]{0:T(128)}, u32[]{:S(2)}) copy-start(s32[128]{0:T(128)} %param.14) | copy-start | bytes 1540
  25.3 7.9 %collective-permute-start = (bf16[32,4096]{1,0:T(8,128)(2,1)}, bf16[32,4096]{1,0:T(8,128)(2,1)S(1)}, u32[]{:S(2)}, u32[]{:S(2)}) collective-permute-start(bf16[32,4096]{1,0:T(8,128)(2,1)} %attention.1), channel_id=1, source_target_pairs={{0,8},{4,12},{8,0},{12,4},{1,9},{5,13},{9,1},{13,5},{2,10},{6,14},... | collective-permute-start | bytes 786440 | tf_op jit(solution)/shard_map/ppermute | solution.py:158
  34.2 2.0 %collective-permute-start.1 = (bf16[64,4096]{1,0:T(8,128)(2,1)S(1)}, bf16[64,4096]{1,0:T(8,128)(2,1)S(1)}, u32[]{:S(2)}, u32[]{:S(2)}) collective-permute-start(bf16[64,4096]{1,0:T(8,128)(2,1)S(1)} %pad_maximum_fusion.6), channel_id=1, source_target_pairs={{0,4},{4,0},{8,12},{12,8},{1,5},{5,1},{9,13},{13,9},{2,6},{6,2},{1... | collective-permute-start | bytes 1572872 | tf_op jit(solution)/shard_map/ppermute | solution.py:160
  34.4 16.1 %copy-start.1 = (s32[4,4,1]{1,2,0:T(1,128)S(1)}, s32[4,4,1]{1,2,0:T(1,128)}, u32[]{:S(2)}) copy-start(s32[4,4,1]{1,2,0:T(1,128)} %param.16) | copy-start | bytes 196
  44.8 19.0 %all-to-all-start.2 = ((bf16[4,32,1792]{2,1,0:T(8,128)(2,1)}), bf16[4,32,1792]{2,1,0:T(8,128)(2,1)S(1)}, u32[]{:S(2)}, u32[]{:S(2)}) async-start(bf16[4,32,1792]{2,1,0:T(8,128)(2,1)} %bitcast.13), calls=%async_computation.2 | async-start | bytes 917504 | tf_op jit(solution)/shard_map/all_to_all | solution.py:176
  65.6 16.1 %all-to-all-start.3 = ((bf16[4,32,1792]{2,1,0:T(8,128)(2,1)}), bf16[4,32,1792]{2,1,0:T(8,128)(2,1)S(1)}, u32[]{:S(2)}, u32[]{:S(2)}) async-start(bf16[4,32,1792]{2,1,0:T(8,128)(2,1)} %broadcast_in_dim.72), calls=%async_computation.3 | async-start | bytes 917504 | tf_op jit(solution)/shard_map/all_to_all | solution.py:183
  81.7 46.8 %all-to-all-start.1 = ((bf16[4,1,256,512]{3,2,1,0:T(8,128)(2,1)}), bf16[4,1,256,512]{3,2,1,0:T(8,128)(2,1)S(1)}, u32[]{:S(2)}, u32[]{:S(2)}) async-start(bf16[4,1,256,512]{3,2,1,0:T(8,128)(2,1)} %fusion.46), calls=%async_computation.1 | async-start | bytes 2097152 | tf_op jit(solution)/shard_map/all_to_all | solution.py:198
  85.5 10.4 %slice-start = ((s8[16515072]{0:T(1024)(128)(4,1)}), s8[4194304]{0:T(1024)(128)(4,1)S(1)}, s32[]{:S(2)}) async-start(s8[16515072]{0:T(1024)(128)(4,1)} %bitcast.169), calls=%async_computation.5 | async-start | bytes 8388608
  85.7 10.3 %slice-start.1 = ((s8[16515072]{0:T(1024)(128)(4,1)}), s8[4194304]{0:T(1024)(128)(4,1)S(1)}, s32[]{:S(2)}) async-start(s8[16515072]{0:T(1024)(128)(4,1)} %bitcast.169), calls=%async_computation.6 | async-start | bytes 8388608
  85.7 10.3 %slice-start.2 = ((s8[16515072]{0:T(1024)(128)(4,1)}), s8[4194304]{0:T(1024)(128)(4,1)S(1)}, s32[]{:S(2)}) async-start(s8[16515072]{0:T(1024)(128)(4,1)} %bitcast.169), calls=%async_computation.7 | async-start | bytes 8388608
  90.5 5.7 %slice-start.3 = ((s8[16515072]{0:T(1024)(128)(4,1)}), s8[3932160]{0:T(1024)(128)(4,1)S(1)}, s32[]{:S(2)}) async-start(s8[16515072]{0:T(1024)(128)(4,1)} %bitcast.169), calls=%async_computation.8 | async-start | bytes 7864320
  98.9 2.1 %collective-permute-start.2 = (bf16[2,2,32,2304]{3,2,1,0:T(8,128)(2,1)S(1)}, bf16[2,2,32,2304]{3,2,1,0:T(8,128)(2,1)S(1)}, u32[]{:S(2)}, u32[]{:S(2)}) collective-permute-start(bf16[2,2,32,2304]{3,2,1,0:T(8,128)(2,1)S(1)} %pad_maximum_fusion.2), channel_id=1, source_target_pairs={{0,4},{4,0},{8,12},{12,8},{1,5},{5,1},{9,13},{13,9},{2,6},{6,2},{1... | collective-permute-start | bytes 1769480 | tf_op jit(solution)/shard_map/ppermute | solution.py:224
  99.2 25.6 %slice-start.4 = ((s8[16515072]{0:T(1024)(128)(4,1)}), s8[3932160]{0:T(1024)(128)(4,1)S(1)}, s32[]{:S(2)}) async-start(s8[16515072]{0:T(1024)(128)(4,1)} %bitcast.171), calls=%async_computation.9 | async-start | bytes 7864320
  99.5 3.5 %collective-permute-start.6 = (bf16[2,2,32,2304]{3,2,1,0:T(8,128)(2,1)S(1)}, bf16[2,2,32,2304]{3,2,1,0:T(8,128)(2,1)S(1)}, u32[]{:S(2)}, u32[]{:S(2)}) collective-permute-start(bf16[2,2,32,2304]{3,2,1,0:T(8,128)(2,1)S(1)} %pad_maximum_fusion.4), channel_id=1, source_target_pairs={{0,4},{4,0},{8,12},{12,8},{1,5},{5,1},{9,13},{13,9},{2,6},{6,2},{1... | collective-permute-start | bytes 1769480 | tf_op jit(solution)/shard_map/ppermute | solution.py:224
  101.1 23.8 %slice-start.5 = ((s8[16515072]{0:T(1024)(128)(4,1)}), s8[4194304]{0:T(1024)(128)(4,1)S(1)}, s32[]{:S(2)}) async-start(s8[16515072]{0:T(1024)(128)(4,1)} %bitcast.171), calls=%async_computation.10 | async-start | bytes 8388608
  101.1 9.9 %collective-permute-start.3 = (bf16[2,32,2304]{2,1,0:T(8,128)(2,1)S(1)}, bf16[2,32,2304]{2,1,0:T(8,128)(2,1)S(1)}, u32[]{:S(2)}, u32[]{:S(2)}) collective-permute-start(bf16[2,32,2304]{2,1,0:T(8,128)(2,1)S(1)} %fusion.50), channel_id=1, source_target_pairs={{0,8},{4,12},{8,0},{12,4},{1,9},{5,13},{9,1},{13,5},{2,10},{6,14},... | collective-permute-start | bytes 884744 | tf_op jit(solution)/shard_map/ppermute | solution.py:227
  103.1 21.7 %slice-start.6 = ((s8[16515072]{0:T(1024)(128)(4,1)}), s8[4194304]{0:T(1024)(128)(4,1)S(1)}, s32[]{:S(2)}) async-start(s8[16515072]{0:T(1024)(128)(4,1)} %bitcast.171), calls=%async_computation.11 | async-start | bytes 8388608
  103.2 14.2 %collective-permute-start.7 = (bf16[2,32,2304]{2,1,0:T(8,128)(2,1)S(1)}, bf16[2,32,2304]{2,1,0:T(8,128)(2,1)S(1)}, u32[]{:S(2)}, u32[]{:S(2)}) collective-permute-start(bf16[2,32,2304]{2,1,0:T(8,128)(2,1)S(1)} %fusion.58), channel_id=1, source_target_pairs={{0,8},{4,12},{8,0},{12,4},{1,9},{5,13},{9,1},{13,5},{2,10},{6,14},... | collective-permute-start | bytes 884744 | tf_op jit(solution)/shard_map/ppermute | solution.py:227
  111.3 13.5 %slice-start.7 = ((s8[16515072]{0:T(1024)(128)(4,1)}), s8[4194304]{0:T(1024)(128)(4,1)S(1)}, s32[]{:S(2)}) async-start(s8[16515072]{0:T(1024)(128)(4,1)} %bitcast.171), calls=%async_computation.12 | async-start | bytes 8388608
  111.3 9.2 %collective-permute-start.4 = (bf16[32,2304]{1,0:T(8,128)(2,1)S(1)}, bf16[32,2304]{1,0:T(8,128)(2,1)S(1)}, u32[]{:S(2)}, u32[]{:S(2)}) collective-permute-start(bf16[32,2304]{1,0:T(8,128)(2,1)S(1)} %fusion.68), channel_id=1, source_target_pairs={{0,8},{4,12},{8,0},{12,4},{1,9},{5,13},{9,1},{13,5},{2,10},{6,14},... | collective-permute-start | bytes 442376 | tf_op jit(solution)/shard_map/ppermute | solution.py:229
  117.6 5.4 %collective-permute-start.8 = (bf16[32,2304]{1,0:T(8,128)(2,1)S(1)}, bf16[32,2304]{1,0:T(8,128)(2,1)S(1)}, u32[]{:S(2)}, u32[]{:S(2)}) collective-permute-start(bf16[32,2304]{1,0:T(8,128)(2,1)S(1)} %fusion.64), channel_id=1, source_target_pairs={{0,8},{4,12},{8,0},{12,4},{1,9},{5,13},{9,1},{13,5},{2,10},{6,14},... | collective-permute-start | bytes 442376 | tf_op jit(solution)/shard_map/ppermute | solution.py:229
  120.6 2.6 %collective-permute-start.5 = (bf16[2,32,2304]{2,1,0:T(8,128)(2,1)S(1)}, bf16[2,32,2304]{2,1,0:T(8,128)(2,1)S(1)}, u32[]{:S(2)}, u32[]{:S(2)}) collective-permute-start(bf16[2,32,2304]{2,1,0:T(8,128)(2,1)S(1)} %pad_maximum_fusion.7), channel_id=1, source_target_pairs={{0,4},{4,0},{8,12},{12,8},{1,5},{5,1},{9,13},{13,9},{2,6},{6,2},{1... | collective-permute-start | bytes 884744 | tf_op jit(solution)/shard_map/ppermute | solution.py:230
  123.1 1.6 %collective-permute-start.9 = (bf16[2,32,2304]{2,1,0:T(8,128)(2,1)S(1)}, bf16[2,32,2304]{2,1,0:T(8,128)(2,1)S(1)}, u32[]{:S(2)}, u32[]{:S(2)}) collective-permute-start(bf16[2,32,2304]{2,1,0:T(8,128)(2,1)S(1)} %pad_maximum_fusion.8), channel_id=1, source_target_pairs={{0,4},{4,0},{8,12},{12,8},{1,5},{5,1},{9,13},{13,9},{2,6},{6,2},{1... | collective-permute-start | bytes 884744 | tf_op jit(solution)/shard_map/ppermute | solution.py:230
  128.5 17.1 %all-to-all-start.4 = ((bf16[4,32,1792]{2,1,0:T(8,128)(2,1)}), bf16[4,32,1792]{2,1,0:T(8,128)(2,1)S(1)}, u32[]{:S(2)}, u32[]{:S(2)}) async-start(bf16[4,32,1792]{2,1,0:T(8,128)(2,1)} %maximum_select_fusion.3), calls=%async_computation.4 | async-start | bytes 917504 | tf_op jit(solution)/shard_map/all_to_all | solution.py:245

commit v2 on v1

v2 whole, which is shorter than its diff:
```python
import functools

import jax
import jax.numpy as jnp
from jax import lax
from jax.experimental import pallas as pl
from jax.experimental.pallas import tpu as pltpu
from jax.sharding import PartitionSpec as P

CHUNKS = 2


def attention_kernel(number_ref, *refs, distances):
    block_refs, refs = refs[: len(distances)], refs[len(distances) :]
    pool_ref, out_ref, twin_ref, *moved_refs, pages, move_sems, sems, q3, top_ref, den_ref, num_ref = refs
    page_count = pages.shape[0]
    place = number_ref[0]
    lanes = move_sems.shape[1]
    first = 1 + page_count + move_sems.shape[0] * lanes
    requests = number_ref.shape[0] - first
    heads, size = q3.shape[1], q3.shape[2]
    width = heads * size
    scale = size ** (-0.5)
    copies = [
        pltpu.make_async_copy(pool_ref.at[b], pages.at[b], sems.at[b]) for b in range(page_count)
    ]
    for copy in copies:
        copy.start()
    moves = []
    for d, moved_ref in enumerate(moved_refs):
        for m in range(moved_ref.shape[0]):
            page = number_ref[1 + page_count + jnp.bitwise_xor(place, d) * lanes + m]
            page = jnp.minimum(page, page_count - 1)
            moves.append(
                pltpu.make_async_copy(pool_ref.at[page], moved_ref.at[m], move_sems.at[d, m])
            )
    for move in moves:
        move.start()
    for i, block_ref in enumerate(block_refs):
        rows = block_ref.shape[0]
        at = pl.ds(jnp.bitwise_xor(place, distances[i]) * rows if len(distances) > 1 else 0, rows)
        for h in range(heads):
            q3[at, h, :] = block_ref[:, h * size : (h + 1) * size].astype(jnp.float32)
        key = block_ref[:, width : width + size].astype(jnp.float32)
        value = block_ref[:, width + size :].astype(jnp.float32)
        own = jnp.sum(q3[at] * key[:, None, :], axis=2, keepdims=True) * scale
        top_ref[at] = jnp.broadcast_to(own, (rows, heads, top_ref.shape[2]))
        num_ref[at] = jnp.broadcast_to(value[:, None, :], (rows, heads, size))
    den_ref[...] = jnp.ones_like(den_ref)
    terms = []
    slots = []
    for b in range(page_count):
        request = number_ref[1 + b]
        slots.append(number_ref[first + jnp.minimum(request, requests - 1)])
        copies[b].wait()
        q = q3[slots[b]].astype(jnp.bfloat16)
        scores = (
            lax.dot_general(
                q, pages[b, :, :size], (((1,), (1,)), ((), ())), preferred_element_type=jnp.float32
            )
            * scale
        )
        top = jnp.max(scores, axis=1, keepdims=True)
        weight = jnp.exp(scores - top).astype(jnp.bfloat16)
        total = jnp.sum(weight.astype(jnp.float32), axis=1, keepdims=True)
        summed = jnp.dot(weight, pages[b, :, size:], preferred_element_type=jnp.float32)
        top = jnp.where(request < requests, top, -jnp.inf)
        terms.append((top, total, summed))
    for b in range(page_count):
        top, total, summed = terms[b]
        slot = slots[b]
        old = top_ref[slot]
        top = jnp.broadcast_to(top, old.shape)
        new = jnp.maximum(old, top)
        keep = jnp.exp(old - new)
        take = jnp.exp(top - new)
        top_ref[slot] = new
        den_ref[slot] = den_ref[slot] * keep + take * total
        num_ref[slot] = num_ref[slot] * keep[:, :1] + take[:, :1] * summed
    for h in range(heads):
        cut = slice(h * size, (h + 1) * size)
        result = (num_ref[:, h, :] / den_ref[:, h, :1]).astype(out_ref.dtype)
        out_ref[:, cut] = result
        twin_ref[:, cut] = result
    for move in moves:
        move.wait()


def in_hbm(x):
    return pltpu.with_memory_space_constraint(x, pltpu.HBM)


def attend(numbers, room, received, distances, cache_pool, slots, heads, size):
    page_count = cache_pool.shape[0]
    moved = jax.ShapeDtypeStruct((room[1],) + cache_pool.shape[1:], cache_pool.dtype)
    moved = [moved] * (len(distances) if len(distances) > 1 else 0)
    smem = pl.BlockSpec(memory_space=pltpu.SMEM)
    vmem = pl.BlockSpec(memory_space=pltpu.VMEM)
    return pl.pallas_call(
        functools.partial(attention_kernel, distances=distances),
        out_shape=[jax.ShapeDtypeStruct((slots, heads * size), jnp.bfloat16)] * 2 + moved,
        in_specs=[smem] + [vmem] * len(received) + [pl.BlockSpec(memory_space=pl.ANY)],
        out_specs=[vmem, vmem] + [pl.BlockSpec(memory_space=pl.ANY)] * len(moved),
        scratch_shapes=[
            pltpu.VMEM(cache_pool.shape, jnp.bfloat16),
            pltpu.SemaphoreType.DMA(room),
            pltpu.SemaphoreType.DMA((page_count,)),
            pltpu.VMEM((slots, heads, size), jnp.float32),
            pltpu.VMEM((slots, heads, 128), jnp.float32),
            pltpu.VMEM((slots, heads, 128), jnp.float32),
            pltpu.VMEM((slots, heads, size), jnp.float32),
        ],
        compiler_params=pltpu.CompilerParams(vmem_limit_bytes=24 * 2**20),
        name="attention",
    )(numbers, *received, in_hbm(cache_pool))


def swap_perm(count, bit):
    return [(i, i ^ bit) for i in range(count)]


def tie(x, *others):
    return lax.optimization_barrier((x, others))[0]


def fold_first(sent, far, axis):
    came = lax.ppermute(sent, axis, swap_perm(4, 1))
    return came[0], (far + came[1].astype(jnp.float32)).astype(jnp.bfloat16)


def fold_last(leaving, own, axis):
    far = lax.ppermute(leaving, axis, swap_perm(4, 2))
    total = own[0].astype(jnp.float32)
    for part in own[1:]:
        total = total + part.astype(jnp.float32)
    return lax.optimization_barrier(total) + far.astype(jnp.float32)


def spread(x, axis):
    half = jnp.stack([x, lax.ppermute(x, axis, swap_perm(4, 2))])
    other = lax.ppermute(half, axis, swap_perm(4, 1))
    return jnp.stack([half[0], other[0], half[1], other[1]])


def split_store(block, columns, near_ref, far_ref, sent_ref):
    share = near_ref.shape[0]
    near_ref[:, columns] = block[:share].astype(near_ref.dtype)
    sent_ref[0, :, columns] = block[share : 2 * share].astype(sent_ref.dtype)
    far_ref[:, columns] = block[2 * share : 3 * share].astype(far_ref.dtype)
    sent_ref[1, :, columns] = block[3 * share :].astype(sent_ref.dtype)


def project_kernel(picker_ref, *refs):
    *piece_refs, w_ref, near_ref, far_ref, sent_ref, tiles, acc_ref, sems = refs
    count, depth = tiles.shape[0], tiles.shape[1]
    copies = [
        pltpu.make_async_copy(w_ref.at[pl.ds(i * depth, depth)], tiles.at[i], sems.at[i])
        for i in range(count)
    ]
    for copy in copies:
        copy.start()
    picker = picker_ref[...]
    for i in range(count):
        cut = slice(i * depth, (i + 1) * depth)
        rows = jnp.concatenate([piece_ref[:, cut] for piece_ref in piece_refs], axis=0)
        x = jnp.dot(picker, rows, preferred_element_type=jnp.float32).astype(jnp.bfloat16)
        copies[i].wait()
        for n in range(0, acc_ref.shape[1], 256):
            to = slice(n, n + 256)
            block = jnp.dot(x, tiles[i, :, to], preferred_element_type=jnp.float32)
            if i > 0:
                block += acc_ref[:, to]
            if i < count - 1:
                acc_ref[:, to] = block
            else:
                split_store(block, to, near_ref, far_ref, sent_ref)


def split_shapes(share, columns):
    return [
        jax.ShapeDtypeStruct((share, columns), jnp.float32),
        jax.ShapeDtypeStruct((share, columns), jnp.float32),
        jax.ShapeDtypeStruct((2, share, columns), jnp.bfloat16),
    ]


def project(picker, pieces, w):
    vmem = pl.BlockSpec(memory_space=pltpu.VMEM)
    depth, columns = w.shape
    tile = 512
    return pl.pallas_call(
        project_kernel,
        out_shape=split_shapes(picker.shape[0] // 4, columns),
        in_specs=[vmem] * (1 + len(pieces)) + [pl.BlockSpec(memory_space=pl.ANY)],
        out_specs=[vmem] * 3,
        scratch_shapes=[
            pltpu.VMEM((depth // tile, tile, columns), w.dtype),
            pltpu.VMEM((picker.shape[0], columns), jnp.float32),
            pltpu.SemaphoreType.DMA((depth // tile,)),
        ],
        compiler_params=pltpu.CompilerParams(vmem_limit_bytes=32 * 2**20),
        name="project",
    )(picker, *pieces, in_hbm(w))


def gate_kernel(x_ref, gate_ref, up_ref, near_ref, far_ref, sent_ref, tiles, sems, *, start):
    count, width = tiles.shape[0] // 2, tiles.shape[2]
    copies = []
    for i in range(2 * count):
        w_ref = gate_ref if i < count else up_ref
        at = pl.ds(start + (i % count) * width, width)
        copies.append(pltpu.make_async_copy(w_ref.at[:, at], tiles.at[i], sems.at[i]))
    for copy in copies:
        copy.start()
    x = x_ref[...]
    for i in range(2 * count):
        copies[i].wait()
        for n in range(0, width, 256):
            block = jnp.dot(x, tiles[i, :, n : n + 256], preferred_element_type=jnp.float32)
            at = i * width + n
            split_store(block, slice(at, at + 256), near_ref, far_ref, sent_ref)


def gate_and_up(x, w_gate, w_up, start, width):
    vmem = pl.BlockSpec(memory_space=pltpu.VMEM)
    hbm = pl.BlockSpec(memory_space=pl.ANY)
    tile = 768
    count = 2 * (width // tile)
    return pl.pallas_call(
        functools.partial(gate_kernel, start=start),
        out_shape=split_shapes(x.shape[0] // 4, 2 * width),
        in_specs=[vmem, hbm, hbm],
        out_specs=[vmem] * 3,
        scratch_shapes=[
            pltpu.VMEM((count, x.shape[1], tile), w_gate.dtype),
            pltpu.SemaphoreType.DMA((count,)),
        ],
        compiler_params=pltpu.CompilerParams(vmem_limit_bytes=32 * 2**20),
        name="gate_and_up",
    )(x, in_hbm(w_gate), in_hbm(w_up))


def in_vmem(w):
    return pltpu.with_memory_space_constraint(w, pltpu.VMEM)


def down_kernel(at_ref, *refs):
    *x_refs, w_ref, near_ref, far_ref, sent_ref, turned_ref = refs
    share = near_ref.shape[0]
    width = x_refs[0].shape[1]
    xs = [x_ref[...] for x_ref in x_refs]
    for n in range(0, w_ref.shape[1], 256):
        cut = slice(n, n + 256)
        block = sum(
            jnp.dot(x, w_ref[i * width : (i + 1) * width, cut], preferred_element_type=jnp.float32)
            for i, x in enumerate(xs)
        )
        for j in range(4):
            turned_ref[jnp.bitwise_xor(at_ref[0], j)] = block[j * share : (j + 1) * share]
        near_ref[:, cut] = turned_ref[0]
        sent_ref[0, :, cut] = turned_ref[1].astype(sent_ref.dtype)
        far_ref[:, cut] = turned_ref[2]
        sent_ref[1, :, cut] = turned_ref[3].astype(sent_ref.dtype)


def down_project(at, xs, w):
    share = xs[0].shape[0] // 4
    vmem = pl.BlockSpec(memory_space=pltpu.VMEM)
    return pl.pallas_call(
        down_kernel,
        out_shape=split_shapes(share, w.shape[1]),
        in_specs=[pl.BlockSpec(memory_space=pltpu.SMEM)] + [vmem] * (len(xs) + 1),
        out_specs=[vmem] * 3,
        scratch_shapes=[pltpu.VMEM((4, share, 256), jnp.float32)],
        compiler_params=pltpu.CompilerParams(vmem_limit_bytes=6 * 2**20),
        name="down_project",
    )(at.reshape(1), *xs, in_vmem(w))


def paired_rows(
    pieces, row_picker, residual, turn, position, pages, w_out, w_gate, w_up, w_down
):
    count = row_picker.shape[0]
    share = count // 4
    columns = w_out.shape[1]
    step = w_gate.shape[1] // CHUNKS
    mine = lax.dynamic_slice_in_dim(residual, turn * share, share, 0)
    pieces, mine, pages = lax.optimization_barrier((pieces, mine, pages))
    landed = list(pages)
    landed[2] = lax.ppermute(pages[2], "attn", swap_perm(4, 2))
    near, far, sent = project(row_picker, pieces, w_out)
    sent, landed[2], pages[1] = lax.optimization_barrier((sent, landed[2], pages[1]))
    landed[1] = lax.ppermute(pages[1], "attn", swap_perm(4, 1))
    came, leaving = fold_first(sent, far, "ffn")
    leaving, landed[1] = lax.optimization_barrier((leaving, landed[1]))
    kept = fold_last(leaving, (mine, near, came), "ffn").astype(jnp.bfloat16)
    mixed = spread(kept, "ffn")
    mixed, pages[3] = lax.optimization_barrier((mixed, pages[3]))
    landed[3] = lax.ppermute(pages[3], "attn", swap_perm(4, 3))
    rows = mixed.reshape(count, columns)

    stages = []
    for c in range(CHUNKS):
        near, far, sent = gate_and_up(rows, w_gate, w_up, c * step, step)
        if c == 0:
            sent, landed[3] = lax.optimization_barrier((sent, landed[3]))
        came, leaving = fold_first(sent, far, "attn")
        rows = tie(rows, leaving)
        stages.append((near, came, leaving))
    hiddens = []
    for c in range(CHUNKS):
        near, came, leaving = stages[c]
        sums = fold_last(leaving, (near, came), "attn")
        quarter = (jax.nn.silu(sums[:, :step]) * sums[:, step:]).astype(jnp.bfloat16)
        across = lax.ppermute(quarter, "attn", swap_perm(4, 2))
        if c + 1 < CHUNKS:
            across = tie(across, stages[c + 1][2])
        half = jnp.stack([quarter, across])
        other = lax.ppermute(half, "attn", swap_perm(4, 1))
        hidden = jnp.stack([half[0], other[0], half[1], other[1]]).reshape(count, step)
        hiddens.append(hidden)
    near, far, sent = down_project(position, hiddens, w_down)
    came, leaving = fold_first(sent, far, "ffn")
    kept = lax.dynamic_index_in_dim(mixed, position, 0, keepdims=False)
    total = fold_last(leaving, (kept, near, came), "ffn")
    return total.astype(jnp.bfloat16), landed


def settle(landed, incoming, pool_count, room_in, turn):
    came_usable = incoming < pool_count
    position_in = jnp.cumsum(came_usable.astype(jnp.int32)) - 1
    lanes = jnp.arange(room_in, dtype=jnp.int32)
    matches = jnp.logical_and(came_usable[None, :], position_in[None, :] == lanes[:, None])
    present = jnp.any(matches, axis=1)
    chosen = jnp.argmax(matches, axis=1)
    if turn is not None:
        pair_room = landed.shape[0] // 4
        chosen = jnp.bitwise_xor(chosen // pair_room, turn) * pair_room + chosen % pair_room
    arrived = jnp.take(landed, chosen, axis=0)
    return jnp.where(present[:, None, None], arrived, jnp.zeros_like(arrived))


def body(
    queries,
    new_kv,
    cache_pool,
    request_owner,
    block_req,
    migrate,
    residual_rows,
    w_out,
    w_gate,
    w_up,
    w_down,
):
    attn_count = lax.axis_size("attn")
    ffn_count = lax.axis_size("ffn")
    position = lax.axis_index("attn")
    ffn_position = lax.axis_index("ffn")
    req_dev = queries.shape[0]
    total_req = request_owner.shape[0]
    capacity = req_dev // 4
    slot_count = attn_count * capacity
    pool_count = cache_pool.shape[0]
    head_size = cache_pool.shape[2] // 2
    head_count = queries.shape[1] // head_size
    pair_room = migrate.shape[2]
    room_in = max(2, attn_count // 4) + 1
    paired = attn_count == 4 and ffn_count == 4

    owner_grid = request_owner.reshape(attn_count, req_dev)
    order = jnp.arange(req_dev, dtype=jnp.int32)
    earlier = order[None, :] < order[:, None]
    same = owner_grid[:, :, None] == owner_grid[:, None, :]
    order_rank = jnp.sum(jnp.logical_and(same, earlier[None]), axis=2)
    within = (jnp.arange(attn_count, dtype=jnp.int32)[:, None] * capacity + order_rank).reshape(-1)
    mine_owner = lax.dynamic_slice_in_dim(owner_grid, position, 1, 0)[0]
    mine_rank = lax.dynamic_slice_in_dim(order_rank, position, 1, 0)[0]
    target = jnp.bitwise_xor(mine_owner, position) if paired else mine_owner
    picker = (
        jnp.arange(slot_count, dtype=jnp.int32)[:, None] == (target * capacity + mine_rank)[None, :]
    ).astype(jnp.bfloat16)
    send = (
        jnp.dot(
            picker, jnp.concatenate([queries, new_kv], axis=1), preferred_element_type=jnp.float32
        )
        .astype(jnp.bfloat16)
        .reshape(attn_count, capacity, -1)
    )
    if paired:
        received = [send[0]] + [
            lax.ppermute(send[d], "attn", swap_perm(4, d)) for d in (2, 3, 1)
        ]
        distances = (0, 2, 3, 1)
    else:
        received = lax.all_to_all(send, "attn", split_axis=0, concat_axis=0, tiled=True)
        received = [received.reshape(slot_count, -1)]
        distances = (0,)
    my_moves = lax.dynamic_index_in_dim(migrate, position, 0, keepdims=False)
    numbers = jnp.concatenate(
        [
            position.astype(jnp.int32).reshape(1),
            lax.dynamic_index_in_dim(block_req, position, 0, keepdims=False),
            my_moves.reshape(-1),
            within,
        ]
    )
    attention, twin, *pages = attend(
        numbers,
        (attn_count, pair_room),
        received,
        distances,
        cache_pool,
        slot_count,
        head_count,
        head_size,
    )

    if paired:
        across = lax.ppermute(twin, "attn", swap_perm(4, 2))
        beside = lax.ppermute(twin, "attn", swap_perm(4, 1))
        corner = lax.ppermute(across, "attn", swap_perm(4, 1))
        everyone = [twin, across, beside, corner]
        distance = jnp.bitwise_xor(request_owner, position)
        place = distance // 2 + (distance % 2) * 2
    else:
        everyone = lax.all_gather(attention, "attn", axis=0, tiled=True)
        place = request_owner
    row_share = total_req // ffn_count
    row_of = (place * slot_count + within).reshape(ffn_count, row_share)
    if paired:
        turn = jnp.bitwise_xor(ffn_position, position)
        row_of = jnp.take(row_of, jnp.bitwise_xor(jnp.arange(4, dtype=jnp.int32), turn), axis=0)
    row_of = row_of.reshape(-1)
    row_picker = (
        row_of[:, None] == jnp.arange(attn_count * slot_count, dtype=jnp.int32)[None, :]
    ).astype(jnp.bfloat16)

    incoming = lax.dynamic_slice_in_dim(migrate, position, 1, 1)[:, 0, :].reshape(-1)
    if paired:
        ffn_out, landed = paired_rows(
            everyone, row_picker, residual_rows, turn, position, pages, w_out, w_gate, w_up, w_down
        )
        arrived = settle(jnp.concatenate(landed), incoming, pool_count, room_in, position)
        return (attention, arrived, ffn_out)

    sent_index = jnp.minimum(my_moves, pool_count - 1).reshape(-1)
    sent_blocks = jnp.take(cache_pool, sent_index, axis=0)
    sent_blocks = sent_blocks.reshape(attn_count, pair_room, cache_pool.shape[1], 2 * head_size)
    landed = lax.all_to_all(sent_blocks, "attn", split_axis=0, concat_axis=0, tiled=True)
    landed = landed.reshape(attn_count * pair_room, landed.shape[2], landed.shape[3])
    arrived = settle(landed, incoming, pool_count, room_in, None)

    ordered = jnp.dot(row_picker, everyone, preferred_element_type=jnp.float32).astype(jnp.bfloat16)
    columns = w_out.shape[1]
    projected = jnp.dot(ordered, w_out, preferred_element_type=jnp.float32).astype(jnp.bfloat16)
    parts = projected.reshape(ffn_count, row_share, columns)
    parts = lax.all_to_all(parts, "ffn", split_axis=0, concat_axis=0, tiled=True)
    mine = lax.dynamic_slice_in_dim(residual_rows, ffn_position * row_share, row_share, 0)
    kept = (mine.astype(jnp.float32) + jnp.sum(parts.astype(jnp.float32), axis=0)).astype(
        jnp.bfloat16
    )
    rows = lax.all_gather(kept, "ffn", axis=0, tiled=True)
    gate = jnp.dot(rows, w_gate, preferred_element_type=jnp.float32)
    up = jnp.dot(rows, w_up, preferred_element_type=jnp.float32)
    gate, up = lax.psum_scatter((gate, up), "attn", scatter_dimension=0, tiled=True)
    quarter = (jax.nn.silu(gate) * up).astype(jnp.bfloat16)
    hidden = lax.all_gather(quarter, "attn", axis=0, tiled=True)
    down = jnp.dot(hidden, w_down, preferred_element_type=jnp.float32).astype(jnp.bfloat16)
    shares = lax.all_to_all(
        down.reshape(ffn_count, row_share, columns), "ffn", split_axis=0, concat_axis=0, tiled=True
    )
    total = jnp.sum(shares.astype(jnp.float32), axis=0)
    ffn_out = (kept.astype(jnp.float32) + total).astype(jnp.bfloat16)
    return (attention, arrived, ffn_out)


def solution(mesh):
    placed = (
        P(("groups", "attn"), "ffn"),
        P(("groups", "attn"), None),
        P(("groups", "attn"), None, None),
        P("groups"),
        P("groups", None),
        P("groups", None, None),
        P("groups", "attn"),
        P("ffn", "attn"),
        P("attn", "ffn"),
        P("attn", "ffn"),
        P("ffn", "attn"),
    )
    return jax.shard_map(
        body,
        mesh=mesh,
        in_specs=placed,
        out_specs=(
            P(("groups", "attn"), "ffn"),
            P(("groups", "attn"), None, None),
            P(("groups", "ffn"), "attn"),
        ),
        check_vma=False,
    )
```

time: 147 us -> 125 us (0.85)
  matrix products: 25.7 us -> 1.19 us
  Pallas kernels: 9.04 us -> 30.2 us
  waiting for transfers between devices: 63 us -> 50.8 us
  local copies, waits for them, and re-layouts: 8.12 us -> 4.6 us
  other arithmetic: 11.3 us -> 8.97 us
    all_to_all x5 -> x0, waiting for transfers between devices: 36.2 us -> none  [the longest x1 11.8 us: body(): lax.all_to_all(down.reshape(ffn_count, row_share, columns), 'ffn', split_...]
    ppermute x10 -> x23, waiting for transfers between devices: 26.8 us -> 50.8 us  [the longest x4 12.7 us: fold_last(): far = lax.ppermute(leaving, axis, swap_perm(4, 2))]
    dot_general x7 -> x0, matrix products: 23.8 us -> none  [the longest x2 10.2 us: body(): gate = jnp.dot(rows, w_gate[:, cut], preferred_element_type=jnp.float32)]
    pallas_call x1 -> x5, Pallas kernels: 9.04 us -> 30.2 us  [the longest x2 13.3 us: gate_and_up(): pl.pallas_call(functools.partial(gate_kernel, start=start), out_shape=spl...]
    all_to_all x5 -> x0, starting transfers between devices: 20.5 us -> none  [the longest x1 5.66 us: body(): lax.all_to_all(projected.reshape(ffn_count, row_share, columns), 'ffn', s...]
    ppermute x10 -> x23, starting transfers between devices: 7.52 us -> 27.9 us  [the longest x4 7.06 us: fold_last(): far = lax.ppermute(leaving, axis, swap_perm(4, 2))]
    unnamed x22, local copies, waits for them, and re-layouts: 2.36 us -> 0.07 us
    gather x3 -> x2, local copies, waits for them, and re-layouts: 3.91 us -> 2.06 us  [the longest x1 1.5 us: settle(): arrived = jnp.take(landed, chosen, axis=0)]
  transfers between devices with their start and end apart: 15 -> 23, of which waited for: 12 -> 18; matrix products, arithmetic and copies ran while one was open for 19% -> 8% of each run, Pallas kernels for 0% -> 15%
where the time goes in v2:
time: 125 us
  waiting for transfers between devices  50.8 us (41%)
  Pallas kernels  30.2 us (24%)
  starting transfers between devices  27.9 us (22%)
  other arithmetic  8.97 us (7%)
  local copies, waits for them, and re-layouts  4.6 us (4%)
    pallas_call x2, Pallas kernels, gate_and_up(): pl.pallas_call(functools.partial(gate_kernel, start=start), out_shape=spl...  13.3 us
    ppermute x4, waiting for transfers between devices, fold_last(): far = lax.ppermute(leaving, axis, swap_perm(4, 2))  12.7 us
    ppermute x4, waiting for transfers between devices, fold_first(): came = lax.ppermute(sent, axis, swap_perm(4, 1))  9.88 us
    pallas_call x1, Pallas kernels, attend(): pl.pallas_call(functools.partial(attention_kernel, distances=distances),...  8.82 us
    ppermute x2, waiting for transfers between devices, paired_rows(): across = lax.ppermute(quarter, 'attn', swap_perm(4, 2))  8.46 us
    ppermute x4, starting transfers between devices, fold_last(): far = lax.ppermute(leaving, axis, swap_perm(4, 2))  7.06 us
    pallas_call x1, Pallas kernels, project(): pl.pallas_call(project_kernel, out_shape=split_shapes(picker.shape[0] //...  5.76 us
    ppermute x1, waiting for transfers between devices, body(): across = lax.ppermute(twin, 'attn', swap_perm(4, 2))  5.29 us
  transfers between devices with their start and end apart: 23, of which 18 were waited for; matrix products, arithmetic and copies ran while one was open for 8% of the time, Pallas kernels for 15%

profile of v2, /device:TPU:0, one launch (start us, length us, event | category | flops | bytes accessed | tf_op | source)
XLA Modules:
  0.0 124.7 jit_solution(10556934479564873884)
XLA Ops:
  3.4 2.6 %collective-permute-start.1 = (bf16[8,4608]{1,0:T(8,128)(2,1)S(1)}, bf16[8,4608]{1,0:T(8,128)(2,1)S(1)}, u32[]{:S(2)}, u32[]{:S(2)}) collective-permute-start(bf16[8,4608]{1,0:T(8,128)(2,1)S(1)} %get-tuple-element.92), channel_id=1, source_target_pairs={{0,12},{4,8},{8,4},{12,0},{1,13},{5,9},{9,5},{13,1},{2,14},{6,10},... | collective-permute-start | bytes 221192 | tf_op jit(solution)/shard_map/ppermute | solution.py:392
  8.7 1.8 %collective-permute-done.refs_1_ = bf16[8,4608]{1,0:T(8,128)(2,1)S(1)} collective-permute-done((bf16[8,4608]{1,0:T(8,128)(2,1)S(1)}, bf16[8,4608]{1,0:T(8,128)(2,1)S(1)}, u32[]{:S(2)}, u32[]{:S(2)}) %collective-permute-start) | collective-permute-done | bytes 73760 | tf_op jit(solution)/shard_map/ppermute | solution.py:392
  10.5 8.8 %attention.1 = (bf16[32,4096]{1,0:T(8,128)(2,1)}, bf16[32,4096]{1,0:T(8,128)(2,1)S(1)}, bf16[1,256,512]{2,1,0:T(8,128)(2,1)S(1)}, bf16[1,256,512]{2,1,0:T(8,128)...) custom-call(s32[147]{0:T(256)S(1)} %pad_add_fusion.number_ref, ...), custom_call_target="tpu_custom_call" | custom-call | tf_op jit(solution)/shard_map/attention/pallas_call | solution.py:99
  19.3 1.8 %collective-permute-start.3 = (bf16[32,4096]{1,0:T(8,128)(2,1)S(1)}, bf16[32,4096]{1,0:T(8,128)(2,1)S(1)}, u32[]{:S(2)}, u32[]{:S(2)}) collective-permute-start(bf16[32,4096]{1,0:T(8,128)(2,1)S(1)} %get-tuple-element.50.refs_0_), channel_id=1, source_target_pairs={{0,8},{4,12},{8,0},{12,4},{1,9},{5,13},{9,1},{13,5},{2,10},{6,14},... | collective-permute-start | bytes 786440 | tf_op jit(solution)/shard_map/ppermute | solution.py:420
  21.8 5.3 %collective-permute-done.3.refs_1_ = bf16[32,4096]{1,0:T(8,128)(2,1)S(1)} collective-permute-done((bf16[32,4096]{1,0:T(8,128)(2,1)S(1)}, bf16[32,4096]{1,0:T(8,128)(2,1)S(1)}, u32[]{:S(2)}, u32[]{:S(2)}) %collective-permute-start.3) | collective-permute-done | bytes 262176 | tf_op jit(solution)/shard_map/ppermute | solution.py:420
  28.7 1.7 %collective-permute-start.6 = (bf16[1,256,512]{2,1,0:T(8,128)(2,1)S(1)}, bf16[1,256,512]{2,1,0:T(8,128)(2,1)S(1)}, u32[]{:S(2)}, u32[]{:S(2)}) collective-permute-start(bf16[1,256,512]{2,1,0:T(8,128)(2,1)S(1)} %get-tuple-element.56), channel_id=1, source_target_pairs={{0,8},{4,12},{8,0},{12,4},{1,9},{5,13},{9,1},{13,5},{2,10},{6,14},... | collective-permute-start | bytes 786440 | tf_op jit(solution)/shard_map/ppermute | solution.py:290
  30.6 5.8 %project.1 = (f32[32,1792]{1,0:T(8,128)S(1)}, f32[32,1792]{1,0:T(8,128)S(1)}, bf16[2,32,1792]{2,1,0:T(8,128)(2,1)S(1)}) custom-call(bf16[128,128]{1,0:T(8,128)(2,1)S(1)} %fusion.9.picker_ref, bf16[32,4096]{1,0:T(8,128)(2,1)S(1)} %get-tuple-element.50.refs_0_, bf16[32,4096]{1,0:T(8,128)(2,1)S(1)} %collective-permute-done.3.refs_1_, ...), custom_call_target="tpu_custom_call" | custom-call | tf_op jit(solution)/shard_map/project/pallas_call | solution.py:191
  37.0 1.8 %collective-permute-start.7 = (bf16[2,32,1792]{2,1,0:T(8,128)(2,1)S(1)}, bf16[2,32,1792]{2,1,0:T(8,128)(2,1)S(1)}, u32[]{:S(2)}, u32[]{:S(2)}) collective-permute-start(bf16[2,32,1792]{2,1,0:T(8,128)(2,1)S(1)} %get-tuple-element.58), channel_id=1, source_target_pairs={{0,1},{1,0},{2,3},{3,2},{4,5},{5,4},{6,7},{7,6},{8,9},{9,8},{10,11... | collective-permute-start | bytes 688136 | tf_op jit(solution)/shard_map/ppermute | solution.py:127
  38.8 5.1 %collective-permute-done.7 = bf16[2,32,1792]{2,1,0:T(8,128)(2,1)S(1)} collective-permute-done((bf16[2,32,1792]{2,1,0:T(8,128)(2,1)S(1)}, bf16[2,32,1792]{2,1,0:T(8,128)(2,1)S(1)}, u32[]{:S(2)}, u32[]{:S(2)}) %collective-permute-start.7) | collective-permute-done | bytes 229408 | tf_op jit(solution)/shard_map/ppermute | solution.py:127
  44.0 2.8 %collective-permute-start.9 = (bf16[32,1792]{1,0:T(8,128)(2,1)S(1)}, bf16[32,1792]{1,0:T(8,128)(2,1)S(1)}, u32[]{:S(2)}, u32[]{:S(2)}) collective-permute-start(bf16[32,1792]{1,0:T(8,128)(2,1)S(1)} %get-tuple-element.64), channel_id=1, source_target_pairs={{0,2},{1,3},{2,0},{3,1},{4,6},{5,7},{6,4},{7,5},{8,10},{9,11},{10,... | collective-permute-start | bytes 344072 | tf_op jit(solution)/shard_map/ppermute | solution.py:132
  46.8 2.9 %collective-permute-done.9 = bf16[32,1792]{1,0:T(8,128)(2,1)S(1)} collective-permute-done((bf16[32,1792]{1,0:T(8,128)(2,1)S(1)}, bf16[32,1792]{1,0:T(8,128)(2,1)S(1)}, u32[]{:S(2)}, u32[]{:S(2)}) %collective-permute-start.9) | collective-permute-done | bytes 114720 | tf_op jit(solution)/shard_map/ppermute | solution.py:132
  49.8 2.9 %collective-permute-start.10 = (bf16[32,1792]{1,0:T(8,128)(2,1)S(1)}, bf16[32,1792]{1,0:T(8,128)(2,1)S(1)}, u32[]{:S(2)}, u32[]{:S(2)}) collective-permute-start(bf16[32,1792]{1,0:T(8,128)(2,1)S(1)} %add_convert_fusion.1), channel_id=1, source_target_pairs={{0,2},{1,3},{2,0},{3,1},{4,6},{5,7},{6,4},{7,5},{8,10},{9,11},{10,... | collective-permute-start | bytes 344072 | tf_op jit(solution)/shard_map/ppermute | solution.py:140
  52.7 2.9 %collective-permute-done.10 = bf16[32,1792]{1,0:T(8,128)(2,1)S(1)} collective-permute-done((bf16[32,1792]{1,0:T(8,128)(2,1)S(1)}, bf16[32,1792]{1,0:T(8,128)(2,1)S(1)}, u32[]{:S(2)}, u32[]{:S(2)}) %collective-permute-start.10) | collective-permute-done | bytes 114720 | tf_op jit(solution)/shard_map/ppermute | solution.py:140
  55.6 4.9 %collective-permute-start.11 = (bf16[2,32,1792]{2,1,0:T(8,128)(2,1)S(1)}, bf16[2,32,1792]{2,1,0:T(8,128)(2,1)S(1)}, u32[]{:S(2)}, u32[]{:S(2)}) collective-permute-start(bf16[2,32,1792]{2,1,0:T(8,128)(2,1)S(1)} %pad_maximum_fusion.6), channel_id=1, source_target_pairs={{0,1},{1,0},{2,3},{3,2},{4,5},{5,4},{6,7},{7,6},{8,9},{9,8},{10,11... | collective-permute-start | bytes 688136 | tf_op jit(solution)/shard_map/ppermute | solution.py:141
  60.5 4.0 %collective-permute-done.11 = bf16[2,32,1792]{2,1,0:T(8,128)(2,1)S(1)} collective-permute-done((bf16[2,32,1792]{2,1,0:T(8,128)(2,1)S(1)}, bf16[2,32,1792]{2,1,0:T(8,128)(2,1)S(1)}, u32[]{:S(2)}, u32[]{:S(2)}) %collective-permute-start.11) | collective-permute-done | bytes 229408 | tf_op jit(solution)/shard_map/ppermute | solution.py:141
  64.7 6.6 %gate_and_up.2 = (f32[32,4608]{1,0:T(8,128)S(1)}, f32[32,4608]{1,0:T(8,128)S(1)}, bf16[2,32,4608]{2,1,0:T(8,128)(2,1)S(1)}) custom-call(bf16[128,1792]{1,0:T(8,128)(2,1)S(1)} %bitcast.68, bf16[1792,4608]{1,0:T(8,128)(2,1)} %gate_ref.3, bf16[1792,4608]{1,0:T(8,128)(2,1)} %up_ref.3), custom_call_target="tpu_custom_call" | custom-call | tf_op jit(solution)/shard_map/gate_and_up/pallas_call | solution.py:229
  71.3 1.9 %collective-permute-done.12 = bf16[1,256,512]{2,1,0:T(8,128)(2,1)S(1)} collective-permute-done((bf16[1,256,512]{2,1,0:T(8,128)(2,1)S(1)}, bf16[1,256,512]{2,1,0:T(8,128)(2,1)S(1)}, u32[]{:S(2)}, u32[]{:S(2)}) %collective-permute-start.12) | collective-permute-done | bytes 262176 | tf_op jit(solution)/shard_map/ppermute | solution.py:299
  77.4 6.7 %gate_and_up.3 = (f32[32,4608]{1,0:T(8,128)S(1)}, f32[32,4608]{1,0:T(8,128)S(1)}, bf16[2,32,4608]{2,1,0:T(8,128)(2,1)S(1)}) custom-call(bf16[128,1792]{1,0:T(8,128)(2,1)S(1)} %bitcast.69, bf16[1792,4608]{1,0:T(8,128)(2,1)} %gate_ref.3, bf16[1792,4608]{1,0:T(8,128)(2,1)} %up_ref.3), custom_call_target="tpu_custom_call" | custom-call | tf_op jit(solution)/shard_map/gate_and_up/pallas_call | solution.py:229
  84.2 1.4 %collective-permute-done.14 = bf16[32,4608]{1,0:T(8,128)(2,1)S(1)} collective-permute-done((bf16[32,4608]{1,0:T(8,128)(2,1)S(1)}, bf16[32,4608]{1,0:T(8,128)(2,1)S(1)}, u32[]{:S(2)}, u32[]{:S(2)}) %collective-permute-start.14) | collective-permute-done | bytes 294944 | tf_op jit(solution)/shard_map/ppermute | solution.py:132
  86.7 1.4 %collective-permute-start.18 = (bf16[32,4608]{1,0:T(8,128)(2,1)S(1)}, bf16[32,4608]{1,0:T(8,128)(2,1)S(1)}, u32[]{:S(2)}, u32[]{:S(2)}) collective-permute-start(bf16[32,4608]{1,0:T(8,128)(2,1)S(1)} %get-tuple-element.84), channel_id=1, source_target_pairs={{0,8},{4,12},{8,0},{12,4},{1,9},{5,13},{9,1},{13,5},{2,10},{6,14},... | collective-permute-start | bytes 884744 | tf_op jit(solution)/shard_map/ppermute | solution.py:132
  88.1 4.5 %collective-permute-done.15 = bf16[32,2304]{1,0:T(8,128)(2,1)S(1)} collective-permute-done((bf16[32,2304]{1,0:T(8,128)(2,1)S(1)}, bf16[32,2304]{1,0:T(8,128)(2,1)S(1)}, u32[]{:S(2)}, u32[]{:S(2)}) %collective-permute-start.15) | collective-permute-done | bytes 147488 | tf_op jit(solution)/shard_map/ppermute | solution.py:315
  92.7 4.5 %collective-permute-done.18 = bf16[32,4608]{1,0:T(8,128)(2,1)S(1)} collective-permute-done((bf16[32,4608]{1,0:T(8,128)(2,1)S(1)}, bf16[32,4608]{1,0:T(8,128)(2,1)S(1)}, u32[]{:S(2)}, u32[]{:S(2)}) %collective-permute-start.18) | collective-permute-done | bytes 294944 | tf_op jit(solution)/shard_map/ppermute | solution.py:132
  97.5 1.2 collective-permute-start.19
  98.7 4.0 %collective-permute-done.19 = bf16[32,2304]{1,0:T(8,128)(2,1)S(1)} collective-permute-done((bf16[32,2304]{1,0:T(8,128)(2,1)S(1)}, bf16[32,2304]{1,0:T(8,128)(2,1)S(1)}, u32[]{:S(2)}, u32[]{:S(2)}) %collective-permute-start.19) | collective-permute-done | bytes 147488 | tf_op jit(solution)/shard_map/ppermute | solution.py:315
  102.9 1.5 %collective-permute-done.20 = bf16[2,32,2304]{2,1,0:T(8,128)(2,1)S(1)} collective-permute-done((bf16[2,32,2304]{2,1,0:T(8,128)(2,1)S(1)}, bf16[2,32,2304]{2,1,0:T(8,128)(2,1)S(1)}, u32[]{:S(2)}, u32[]{:S(2)}) %collective-permute-start.20) | collective-permute-done | bytes 294944 | tf_op jit(solution)/shard_map/ppermute | solution.py:319
  104.5 2.3 %down_project.1 = (f32[32,1792]{1,0:T(8,128)S(1)}, f32[32,1792]{1,0:T(8,128)S(1)}, bf16[2,32,1792]{2,1,0:T(8,128)(2,1)S(1)}) custom-call(s32[1]{0:T(128)} %bitcast.at_ref, bf16[128,2304]{1,0:T(8,128)(2,1)S(1)} %bitcast.70, bf16[128,2304]{1,0:T(8,128)(2,1)S(1)} %bitcast.71, bf16[4608,1792]{1,0:T(8,128)(2,1)S(1)} %bitcast.67), custom_call_target="tpu_custom_call" | custom-call | tf_op jit(solution)/shard_map/down_project/pallas_call | solution.py:269
  106.9 2.1 %collective-permute-start.21 = (bf16[2,32,1792]{2,1,0:T(8,128)(2,1)S(1)}, bf16[2,32,1792]{2,1,0:T(8,128)(2,1)}, u32[]{:S(2)}, u32[]{:S(2)}) collective-permute-start(bf16[2,32,1792]{2,1,0:T(8,128)(2,1)S(1)} %get-tuple-element.79), channel_id=1, source_target_pairs={{0,1},{1,0},{2,3},{3,2},{4,5},{5,4},{6,7},{7,6},{8,9},{9,8},{10,11... | collective-permute-start | bytes 688136 | tf_op jit(solution)/shard_map/ppermute | solution.py:127
  109.1 1.5 %gather_fusion.1 = bf16[3,256,512]{2,1,0:T(8,128)(2,1)} fusion(bf16[4,256,512]{2,1,0:T(8,128)(2,1)S(1)} %pad_maximum_fusion, s32[1024]{0:T(1024)S(1)} %pad_clamp_fusion), kind=kCustom, calls=%fused_computation.1 | custom fusion | bytes 1572876 | tf_op jit(solution)/shard_map/jit(_take)/gather | solution.py:339
  110.6 4.3 %collective-permute-done.21 = bf16[2,32,1792]{2,1,0:T(8,128)(2,1)} collective-permute-done((bf16[2,32,1792]{2,1,0:T(8,128)(2,1)S(1)}, bf16[2,32,1792]{2,1,0:T(8,128)(2,1)}, u32[]{:S(2)}, u32[]{:S(2)}) %collective-permute-start.21) | collective-permute-done | bytes 229408 | tf_op jit(solution)/shard_map/ppermute | solution.py:127
  116.0 2.1 %collective-permute-start.22 = (bf16[32,1792]{1,0:T(8,128)(2,1)S(1)}, bf16[32,1792]{1,0:T(8,128)(2,1)S(1)}, u32[]{:S(2)}, u32[]{:S(2)}) collective-permute-start(bf16[32,1792]{1,0:T(8,128)(2,1)S(1)} %get-tuple-element.95), channel_id=1, source_target_pairs={{0,2},{1,3},{2,0},{3,1},{4,6},{5,7},{6,4},{7,5},{8,10},{9,11},{10,... | collective-permute-start | bytes 344072 | tf_op jit(solution)/shard_map/ppermute | solution.py:132
  118.0 2.2 %select_select_fusion = bf16[3,256,512]{2,1,0:T(8,128)(2,1)} fusion(bf16[3,256,512]{2,1,0:T(8,128)(2,1)} %gather_fusion.1, pred[3]{0:T(512)(128)(4,1)S(1)} %get-tuple-element.81, pred[3]{0:T(512)(128)(4,1)S(1)} %fusion.13), kind=kLoop, calls=%fused_computation.4 | loop fusion | flops 786432 | bytes 1572870 | tf_op jit(solution)/shard_map/jit(_where)/select_n | solution.py:340
  120.2 3.8 %collective-permute-done.22 = bf16[32,1792]{1,0:T(8,128)(2,1)S(1)} collective-permute-done((bf16[32,1792]{1,0:T(8,128)(2,1)S(1)}, bf16[32,1792]{1,0:T(8,128)(2,1)S(1)}, u32[]{:S(2)}, u32[]{:S(2)}) %collective-permute-start.22) | collective-permute-done | bytes 114720 | tf_op jit(solution)/shard_map/ppermute | solution.py:132
  (96 shorter events, 16.4 us)
Async XLA Ops:
  0.6 27.2 %copy-start = (bf16[128,1792]{1,0:T(8,128)(2,1)S(1)}, bf16[128,1792]{1,0:T(8,128)(2,1)}, u32[]{:S(2)}) copy-start(bf16[128,1792]{1,0:T(8,128)(2,1)} %param.17) | copy-start | bytes 1376260
  2.9 4.8 %collective-permute-start.2 = (bf16[8,4608]{1,0:T(8,128)(2,1)S(1)}, bf16[8,4608]{1,0:T(8,128)(2,1)S(1)}, u32[]{:S(2)}, u32[]{:S(2)}) collective-permute-start(bf16[8,4608]{1,0:T(8,128)(2,1)S(1)} %get-tuple-element.91), channel_id=1, source_target_pairs={{0,4},{4,0},{8,12},{12,8},{1,5},{5,1},{9,13},{13,9},{2,6},{6,2},{1... | collective-permute-start | bytes 221192 | tf_op jit(solution)/shard_map/ppermute | solution.py:392
  3.4 5.2 %collective-permute-start.1 = (bf16[8,4608]{1,0:T(8,128)(2,1)S(1)}, bf16[8,4608]{1,0:T(8,128)(2,1)S(1)}, u32[]{:S(2)}, u32[]{:S(2)}) collective-permute-start(bf16[8,4608]{1,0:T(8,128)(2,1)S(1)} %get-tuple-element.92), channel_id=1, source_target_pairs={{0,12},{4,8},{8,4},{12,0},{1,13},{5,9},{9,5},{13,1},{2,14},{6,10},... | collective-permute-start | bytes 221192 | tf_op jit(solution)/shard_map/ppermute | solution.py:392
  6.1 4.4 %collective-permute-start = (bf16[8,4608]{1,0:T(8,128)(2,1)S(1)}, bf16[8,4608]{1,0:T(8,128)(2,1)S(1)}, u32[]{:S(2)}, u32[]{:S(2)}) collective-permute-start(bf16[8,4608]{1,0:T(8,128)(2,1)S(1)} %get-tuple-element.93), channel_id=1, source_target_pairs={{0,8},{4,12},{8,0},{12,4},{1,9},{5,13},{9,1},{13,5},{2,10},{6,14},... | collective-permute-start | bytes 221192 | tf_op jit(solution)/shard_map/ppermute | solution.py:392
  19.3 7.8 %collective-permute-start.3 = (bf16[32,4096]{1,0:T(8,128)(2,1)S(1)}, bf16[32,4096]{1,0:T(8,128)(2,1)S(1)}, u32[]{:S(2)}, u32[]{:S(2)}) collective-permute-start(bf16[32,4096]{1,0:T(8,128)(2,1)S(1)} %get-tuple-element.50.refs_0_), channel_id=1, source_target_pairs={{0,8},{4,12},{8,0},{12,4},{1,9},{5,13},{9,1},{13,5},{2,10},{6,14},... | collective-permute-start | bytes 786440 | tf_op jit(solution)/shard_map/ppermute | solution.py:420
  21.7 6.1 %collective-permute-start.4 = (bf16[32,4096]{1,0:T(8,128)(2,1)S(1)}, bf16[32,4096]{1,0:T(8,128)(2,1)S(1)}, u32[]{:S(2)}, u32[]{:S(2)}) collective-permute-start(bf16[32,4096]{1,0:T(8,128)(2,1)S(1)} %get-tuple-element.50.refs_0_), channel_id=1, source_target_pairs={{0,4},{4,0},{8,12},{12,8},{1,5},{5,1},{9,13},{13,9},{2,6},{6,2},{1... | collective-permute-start | bytes 786440 | tf_op jit(solution)/shard_map/ppermute | solution.py:421
  27.1 1.5 %collective-permute-start.5 = (bf16[32,4096]{1,0:T(8,128)(2,1)S(1)}, bf16[32,4096]{1,0:T(8,128)(2,1)S(1)}, u32[]{:S(2)}, u32[]{:S(2)}) collective-permute-start(bf16[32,4096]{1,0:T(8,128)(2,1)S(1)} %collective-permute-done.3.refs_1_), channel_id=1, source_target_pairs={{0,4},{4,0},{8,12},{12,8},{1,5},{5,1},{9,13},{13,9},{2,6},{6,2},{1... | collective-permute-start | bytes 786440 | tf_op jit(solution)/shard_map/ppermute | solution.py:422
  28.7 8.3 %collective-permute-start.6 = (bf16[1,256,512]{2,1,0:T(8,128)(2,1)S(1)}, bf16[1,256,512]{2,1,0:T(8,128)(2,1)S(1)}, u32[]{:S(2)}, u32[]{:S(2)}) collective-permute-start(bf16[1,256,512]{2,1,0:T(8,128)(2,1)S(1)} %get-tuple-element.56), channel_id=1, source_target_pairs={{0,8},{4,12},{8,0},{12,4},{1,9},{5,13},{9,1},{13,5},{2,10},{6,14},... | collective-permute-start | bytes 786440 | tf_op jit(solution)/shard_map/ppermute | solution.py:290
  37.0 6.9 %collective-permute-start.7 = (bf16[2,32,1792]{2,1,0:T(8,128)(2,1)S(1)}, bf16[2,32,1792]{2,1,0:T(8,128)(2,1)S(1)}, u32[]{:S(2)}, u32[]{:S(2)}) collective-permute-start(bf16[2,32,1792]{2,1,0:T(8,128)(2,1)S(1)} %get-tuple-element.58), channel_id=1, source_target_pairs={{0,1},{1,0},{2,3},{3,2},{4,5},{5,4},{6,7},{7,6},{8,9},{9,8},{10,11... | collective-permute-start | bytes 688136 | tf_op jit(solution)/shard_map/ppermute | solution.py:127
  38.8 5.1 %collective-permute-start.8 = (bf16[1,256,512]{2,1,0:T(8,128)(2,1)S(1)}, bf16[1,256,512]{2,1,0:T(8,128)(2,1)S(1)}, u32[]{:S(2)}, u32[]{:S(2)}) collective-permute-start(bf16[1,256,512]{2,1,0:T(8,128)(2,1)S(1)} %get-tuple-element.59), channel_id=1, source_target_pairs={{0,4},{4,0},{8,12},{12,8},{1,5},{5,1},{9,13},{13,9},{2,6},{6,2},{1... | collective-permute-start | bytes 786440 | tf_op jit(solution)/shard_map/ppermute | solution.py:293
  44.0 20.7 %copy-start.2 = (bf16[1,256,512]{2,1,0:T(8,128)(2,1)}, bf16[1,256,512]{2,1,0:T(8,128)(2,1)S(1)}, u32[]{:S(2)}) copy-start(bf16[1,256,512]{2,1,0:T(8,128)(2,1)S(1)} %collective-permute-done.8) | copy-start | bytes 786436
  44.0 5.8 %collective-permute-start.9 = (bf16[32,1792]{1,0:T(8,128)(2,1)S(1)}, bf16[32,1792]{1,0:T(8,128)(2,1)S(1)}, u32[]{:S(2)}, u32[]{:S(2)}) collective-permute-start(bf16[32,1792]{1,0:T(8,128)(2,1)S(1)} %get-tuple-element.64), channel_id=1, source_target_pairs={{0,2},{1,3},{2,0},{3,1},{4,6},{5,7},{6,4},{7,5},{8,10},{9,11},{10,... | collective-permute-start | bytes 344072 | tf_op jit(solution)/shard_map/ppermute | solution.py:132
  49.8 5.8 %collective-permute-start.10 = (bf16[32,1792]{1,0:T(8,128)(2,1)S(1)}, bf16[32,1792]{1,0:T(8,128)(2,1)S(1)}, u32[]{:S(2)}, u32[]{:S(2)}) collective-permute-start(bf16[32,1792]{1,0:T(8,128)(2,1)S(1)} %add_convert_fusion.1), channel_id=1, source_target_pairs={{0,2},{1,3},{2,0},{3,1},{4,6},{5,7},{6,4},{7,5},{8,10},{9,11},{10,... | collective-permute-start | bytes 344072 | tf_op jit(solution)/shard_map/ppermute | solution.py:140
  55.6 8.9 %collective-permute-start.11 = (bf16[2,32,1792]{2,1,0:T(8,128)(2,1)S(1)}, bf16[2,32,1792]{2,1,0:T(8,128)(2,1)S(1)}, u32[]{:S(2)}, u32[]{:S(2)}) collective-permute-start(bf16[2,32,1792]{2,1,0:T(8,128)(2,1)S(1)} %pad_maximum_fusion.6), channel_id=1, source_target_pairs={{0,1},{1,0},{2,3},{3,2},{4,5},{5,4},{6,7},{7,6},{8,9},{9,8},{10,11... | collective-permute-start | bytes 688136 | tf_op jit(solution)/shard_map/ppermute | solution.py:141
  64.6 8.6 %collective-permute-start.12 = (bf16[1,256,512]{2,1,0:T(8,128)(2,1)S(1)}, bf16[1,256,512]{2,1,0:T(8,128)(2,1)S(1)}, u32[]{:S(2)}, u32[]{:S(2)}) collective-permute-start(bf16[1,256,512]{2,1,0:T(8,128)(2,1)S(1)} %get-tuple-element.68), channel_id=1, source_target_pairs={{0,12},{4,8},{8,4},{12,0},{1,13},{5,9},{9,5},{13,1},{2,14},{6,10},... | collective-permute-start | bytes 786440 | tf_op jit(solution)/shard_map/ppermute | solution.py:299
  73.2 2.1 %collective-permute-start.13 = (bf16[2,32,4608]{2,1,0:T(8,128)(2,1)S(1)}, bf16[2,32,4608]{2,1,0:T(8,128)(2,1)}, u32[]{:S(2)}, u32[]{:S(2)}) collective-permute-start(bf16[2,32,4608]{2,1,0:T(8,128)(2,1)S(1)} %get-tuple-element.71), channel_id=1, source_target_pairs={{0,4},{4,0},{8,12},{12,8},{1,5},{5,1},{9,13},{13,9},{2,6},{6,2},{1... | collective-permute-start | bytes 1769480 | tf_op jit(solution)/shard_map/ppermute | solution.py:127
  76.5 9.1 %collective-permute-start.14 = (bf16[32,4608]{1,0:T(8,128)(2,1)S(1)}, bf16[32,4608]{1,0:T(8,128)(2,1)S(1)}, u32[]{:S(2)}, u32[]{:S(2)}) collective-permute-start(bf16[32,4608]{1,0:T(8,128)(2,1)S(1)} %get-tuple-element.85), channel_id=1, source_target_pairs={{0,8},{4,12},{8,0},{12,4},{1,9},{5,13},{9,1},{13,5},{2,10},{6,14},... | collective-permute-start | bytes 884744 | tf_op jit(solution)/shard_map/ppermute | solution.py:132
  77.3 27.1 %slice-start = ((s8[16515072]{0:T(1024)(128)(4,1)}), s8[4194304]{0:T(1024)(128)(4,1)S(1)}, s32[]{:S(2)}) async-start(s8[16515072]{0:T(1024)(128)(4,1)} %bitcast.66), calls=%async_computation | async-start | bytes 8388608
  77.3 27.1 %slice-start.1 = ((s8[16515072]{0:T(1024)(128)(4,1)}), s8[4194304]{0:T(1024)(128)(4,1)S(1)}, s32[]{:S(2)}) async-start(s8[16515072]{0:T(1024)(128)(4,1)} %bitcast.66), calls=%async_computation.1 | async-start | bytes 8388608
  77.4 27.1 %slice-start.2 = ((s8[16515072]{0:T(1024)(128)(4,1)}), s8[3932160]{0:T(1024)(128)(4,1)S(1)}, s32[]{:S(2)}) async-start(s8[16515072]{0:T(1024)(128)(4,1)} %bitcast.66), calls=%async_computation.2 | async-start | bytes 7864320
  84.1 24.9 %copy-start.3 = (bf16[1,256,512]{2,1,0:T(8,128)(2,1)S(1)}, bf16[1,256,512]{2,1,0:T(8,128)(2,1)}, u32[]{:S(2)}) copy-start(bf16[1,256,512]{2,1,0:T(8,128)(2,1)} %copy-done.2) | copy-start | bytes 786436
  84.1 24.9 %copy-start.5 = (bf16[1,256,512]{2,1,0:T(8,128)(2,1)S(1)}, bf16[1,256,512]{2,1,0:T(8,128)(2,1)}, u32[]{:S(2)}) copy-start(bf16[1,256,512]{2,1,0:T(8,128)(2,1)} %copy-done.4) | copy-start | bytes 786436
  84.1 2.5 %collective-permute-start.16 = (bf16[2,32,4608]{2,1,0:T(8,128)(2,1)S(1)}, bf16[2,32,4608]{2,1,0:T(8,128)(2,1)S(1)}, u32[]{:S(2)}, u32[]{:S(2)}) collective-permute-start(bf16[2,32,4608]{2,1,0:T(8,128)(2,1)S(1)} %get-tuple-element.75), channel_id=1, source_target_pairs={{0,4},{4,0},{8,12},{12,8},{1,5},{5,1},{9,13},{13,9},{2,6},{6,2},{1... | collective-permute-start | bytes 1769480 | tf_op jit(solution)/shard_map/ppermute | solution.py:127
  85.7 18.8 %slice-start.3 = ((s8[16515072]{0:T(1024)(128)(4,1)}), s8[4194304]{0:T(1024)(128)(4,1)S(1)}, s32[]{:S(2)}) async-start(s8[16515072]{0:T(1024)(128)(4,1)} %bitcast.66), calls=%async_computation.3 | async-start | bytes 8388608
  85.8 6.8 %collective-permute-start.15 = (bf16[32,2304]{1,0:T(8,128)(2,1)S(1)}, bf16[32,2304]{1,0:T(8,128)(2,1)S(1)}, u32[]{:S(2)}, u32[]{:S(2)}) collective-permute-start(bf16[32,2304]{1,0:T(8,128)(2,1)S(1)} %fusion.3), channel_id=1, source_target_pairs={{0,8},{4,12},{8,0},{12,4},{1,9},{5,13},{9,1},{13,5},{2,10},{6,14},... | collective-permute-start | bytes 442376 | tf_op jit(solution)/shard_map/ppermute | solution.py:315
  86.6 38.1 %copy-start.1 = (bf16[128,1792]{1,0:T(8,128)(2,1)S(1)}, bf16[128,1792]{1,0:T(8,128)(2,1)}, u32[]{:S(2)}) copy-start(bf16[128,1792]{1,0:T(8,128)(2,1)} %param.17) | copy-start | bytes 1376260
  86.7 10.5 %collective-permute-start.18 = (bf16[32,4608]{1,0:T(8,128)(2,1)S(1)}, bf16[32,4608]{1,0:T(8,128)(2,1)S(1)}, u32[]{:S(2)}, u32[]{:S(2)}) collective-permute-start(bf16[32,4608]{1,0:T(8,128)(2,1)S(1)} %get-tuple-element.84), channel_id=1, source_target_pairs={{0,8},{4,12},{8,0},{12,4},{1,9},{5,13},{9,1},{13,5},{2,10},{6,14},... | collective-permute-start | bytes 884744 | tf_op jit(solution)/shard_map/ppermute | solution.py:132
  92.7 6.0 %collective-permute-start.17 = (bf16[2,32,2304]{2,1,0:T(8,128)(2,1)S(1)}, bf16[2,32,2304]{2,1,0:T(8,128)(2,1)S(1)}, u32[]{:S(2)}, u32[]{:S(2)}) collective-permute-start(bf16[2,32,2304]{2,1,0:T(8,128)(2,1)S(1)} %pad_maximum_fusion.4), channel_id=1, source_target_pairs={{0,4},{4,0},{8,12},{12,8},{1,5},{5,1},{9,13},{13,9},{2,6},{6,2},{1... | collective-permute-start | bytes 884744 | tf_op jit(solution)/shard_map/ppermute | solution.py:319
  97.5 5.2 %collective-permute-start.19 = (bf16[32,2304]{1,0:T(8,128)(2,1)S(1)}, bf16[32,2304]{1,0:T(8,128)(2,1)S(1)}, u32[]{:S(2)}, u32[]{:S(2)}) collective-permute-start(bf16[32,2304]{1,0:T(8,128)(2,1)S(1)} %fusion.2), channel_id=1, source_target_pairs={{0,8},{4,12},{8,0},{12,4},{1,9},{5,13},{9,1},{13,5},{2,10},{6,14},... | collective-permute-start | bytes 442376 | tf_op jit(solution)/shard_map/ppermute | solution.py:315
  102.7 1.6 %collective-permute-start.20 = (bf16[2,32,2304]{2,1,0:T(8,128)(2,1)S(1)}, bf16[2,32,2304]{2,1,0:T(8,128)(2,1)S(1)}, u32[]{:S(2)}, u32[]{:S(2)}) collective-permute-start(bf16[2,32,2304]{2,1,0:T(8,128)(2,1)S(1)} %pad_maximum_fusion.5), channel_id=1, source_target_pairs={{0,4},{4,0},{8,12},{12,8},{1,5},{5,1},{9,13},{13,9},{2,6},{6,2},{1... | collective-permute-start | bytes 884744 | tf_op jit(solution)/shard_map/ppermute | solution.py:319
  106.9 8.1 %collective-permute-start.21 = (bf16[2,32,1792]{2,1,0:T(8,128)(2,1)S(1)}, bf16[2,32,1792]{2,1,0:T(8,128)(2,1)}, u32[]{:S(2)}, u32[]{:S(2)}) collective-permute-start(bf16[2,32,1792]{2,1,0:T(8,128)(2,1)S(1)} %get-tuple-element.79), channel_id=1, source_target_pairs={{0,1},{1,0},{2,3},{3,2},{4,5},{5,4},{6,7},{7,6},{8,9},{9,8},{10,11... | collective-permute-start | bytes 688136 | tf_op jit(solution)/shard_map/ppermute | solution.py:127
  116.0 8.1 %collective-permute-start.22 = (bf16[32,1792]{1,0:T(8,128)(2,1)S(1)}, bf16[32,1792]{1,0:T(8,128)(2,1)S(1)}, u32[]{:S(2)}, u32[]{:S(2)}) collective-permute-start(bf16[32,1792]{1,0:T(8,128)(2,1)S(1)} %get-tuple-element.95), channel_id=1, source_target_pairs={{0,2},{1,3},{2,0},{3,1},{4,6},{5,7},{6,4},{7,5},{8,10},{9,11},{10,... | collective-permute-start | bytes 344072 | tf_op jit(solution)/shard_map/ppermute | solution.py:132
  (2 other events, 10.8 us)

commit v3 on v2

--- a/solution.py
+++ b/solution.py
@@ -8,6 +8,7 @@
 from jax.sharding import PartitionSpec as P
 
 CHUNKS = 2
+PARTS = 2
 
 
 def attention_kernel(number_ref, *refs, distances):
@@ -49,23 +50,29 @@
     den_ref[...] = jnp.ones_like(den_ref)
     terms = []
     slots = []
-    for b in range(page_count):
-        request = number_ref[1 + b]
-        slots.append(number_ref[first + jnp.minimum(request, requests - 1)])
-        copies[b].wait()
-        q = q3[slots[b]].astype(jnp.bfloat16)
-        scores = (
-            lax.dot_general(
-                q, pages[b, :, :size], (((1,), (1,)), ((), ())), preferred_element_type=jnp.float32
+    for first_page in range(0, page_count, 7):
+        group = range(first_page, min(first_page + 7, page_count))
+        for b in group:
+            copies[b].wait()
+        live = []
+        scores = []
+        for b in group:
+            request = number_ref[1 + b]
+            slots.append(number_ref[first + jnp.minimum(request, requests - 1)])
+            live.append(request < requests)
+            q = q3[slots[b]].astype(jnp.bfloat16)
+            scores.append(
+                lax.dot_general(
+                    q, pages[b, :, :size], (((1,), (1,)), ((), ())), preferred_element_type=jnp.float32
+                )
+                * scale
             )
-            * scale
-        )
-        top = jnp.max(scores, axis=1, keepdims=True)
-        weight = jnp.exp(scores - top).astype(jnp.bfloat16)
-        total = jnp.sum(weight.astype(jnp.float32), axis=1, keepdims=True)
-        summed = jnp.dot(weight, pages[b, :, size:], preferred_element_type=jnp.float32)
-        top = jnp.where(request < requests, top, -jnp.inf)
-        terms.append((top, total, summed))
+        tops = [jnp.max(score, axis=1, keepdims=True) for score in scores]
+        weights = [jnp.exp(score - top).astype(jnp.bfloat16) for score, top in zip(scores, tops)]
+        for b, alive, top, weight in zip(group, live, tops, weights):
+            total = jnp.sum(weight.astype(jnp.float32), axis=1, keepdims=True)
+            summed = jnp.dot(weight, pages[b, :, size:], preferred_element_type=jnp.float32)
+            terms.append((jnp.where(alive, top, -jnp.inf), total, summed))
     for b in range(page_count):
         top, total, summed = terms[b]
         slot = slots[b]
@@ -245,36 +252,66 @@
 
 
 def down_kernel(at_ref, *refs):
-    *x_refs, w_ref, near_ref, far_ref, sent_ref, turned_ref = refs
-    share = near_ref.shape[0]
+    refs, turned_ref = refs[:-1], refs[-1]
+    refs, outs = refs[: -3 * PARTS], refs[-3 * PARTS :]
+    *x_refs, w_ref = refs
+    share, columns = outs[0].shape
     width = x_refs[0].shape[1]
     xs = [x_ref[...] for x_ref in x_refs]
-    for n in range(0, w_ref.shape[1], 256):
-        cut = slice(n, n + 256)
-        block = sum(
-            jnp.dot(x, w_ref[i * width : (i + 1) * width, cut], preferred_element_type=jnp.float32)
-            for i, x in enumerate(xs)
-        )
-        for j in range(4):
-            turned_ref[jnp.bitwise_xor(at_ref[0], j)] = block[j * share : (j + 1) * share]
-        near_ref[:, cut] = turned_ref[0]
-        sent_ref[0, :, cut] = turned_ref[1].astype(sent_ref.dtype)
-        far_ref[:, cut] = turned_ref[2]
-        sent_ref[1, :, cut] = turned_ref[3].astype(sent_ref.dtype)
+    for p in range(PARTS):
+        near_ref, far_ref, sent_ref = outs[3 * p : 3 * p + 3]
+        for n in range(0, columns, 256):
+            cut = slice(n, min(n + 256, columns))
+            size = cut.stop - cut.start
+            at = pl.ds(p * columns + n, size)
+            block = sum(
+                jnp.dot(x, w_ref[i * width : (i + 1) * width, at], preferred_element_type=jnp.float32)
+                for i, x in enumerate(xs)
+            )
+            for j in range(4):
+                turned_ref[jnp.bitwise_xor(at_ref[0], j), :, :size] = block[
+                    j * share : (j + 1) * share
+                ]
+            near_ref[:, cut] = turned_ref[0, :, :size]
+            sent_ref[0, :, cut] = turned_ref[1, :, :size].astype(sent_ref.dtype)
+            far_ref[:, cut] = turned_ref[2, :, :size]
+            sent_ref[1, :, cut] = turned_ref[3, :, :size].astype(sent_ref.dtype)
 
 
 def down_project(at, xs, w):
     share = xs[0].shape[0] // 4
     vmem = pl.BlockSpec(memory_space=pltpu.VMEM)
-    return pl.pallas_call(
+    outs = pl.pallas_call(
         down_kernel,
-        out_shape=split_shapes(share, w.shape[1]),
+        out_shape=split_shapes(share, w.shape[1] // PARTS) * PARTS,
         in_specs=[pl.BlockSpec(memory_space=pltpu.SMEM)] + [vmem] * (len(xs) + 1),
-        out_specs=[vmem] * 3,
+        out_specs=[vmem] * (3 * PARTS),
         scratch_shapes=[pltpu.VMEM((4, share, 256), jnp.float32)],
         compiler_params=pltpu.CompilerParams(vmem_limit_bytes=6 * 2**20),
         name="down_project",
     )(at.reshape(1), *xs, in_vmem(w))
+    return [outs[3 * p : 3 * p + 3] for p in range(PARTS)]
+
+
+def sum_first(sums):
+    near, leaving = [], []
+    for at_hand, far, sent in sums:
+        came = lax.ppermute(sent, "ffn", swap_perm(4, 1))
+        if leaving:
+            came = tie(came, leaving[-1])
+        near.append((at_hand, came[0]))
+        leaving.append((far + came[1].astype(jnp.float32)).astype(jnp.bfloat16))
+    return near, leaving
+
+
+def sum_last(leaving, own, near):
+    outs = []
+    for p, last in enumerate(leaving):
+        far = lax.ppermute(last, "ffn", swap_perm(4, 2))
+        far = tie(far, outs[-1] if outs else leaving[-1])
+        base = own[p].astype(jnp.float32) + near[p][0] + near[p][1].astype(jnp.float32)
+        outs.append((lax.optimization_barrier(base) + far.astype(jnp.float32)).astype(jnp.bfloat16))
+    return outs
 
 
 def paired_rows(
@@ -319,11 +356,13 @@
         other = lax.ppermute(half, "attn", swap_perm(4, 1))
         hidden = jnp.stack([half[0], other[0], half[1], other[1]]).reshape(count, step)
         hiddens.append(hidden)
-    near, far, sent = down_project(position, hiddens, w_down)
-    came, leaving = fold_first(sent, far, "ffn")
+    sums = down_project(position, hiddens, w_down)
+    sums, landed = lax.optimization_barrier((sums, landed))
+    near, leaving = sum_first(sums)
     kept = lax.dynamic_index_in_dim(mixed, position, 0, keepdims=False)
-    total = fold_last(leaving, (kept, near, came), "ffn")
-    return total.astype(jnp.bfloat16), landed
+    part = columns // PARTS
+    outs = sum_last(leaving, [kept[:, p * part : (p + 1) * part] for p in range(PARTS)], near)
+    return jnp.concatenate(outs, axis=1), landed
 
 
 def settle(landed, incoming, pool_count, room_in, turn):

time: 125 us -> 118 us (0.944)
  Pallas kernels: 30.2 us -> 26.9 us
  waiting for transfers between devices: 50.8 us -> 48.2 us
  other arithmetic: 8.97 us -> 6.62 us
  starting transfers between devices: 27.9 us -> 29.9 us
    ppermute x0 -> x4, starting transfers between devices: none -> 6.31 us  [the longest x2 4.15 us: sum_last(): far = lax.ppermute(last, 'ffn', swap_perm(4, 2))]
    ppermute x0 -> x4, waiting for transfers between devices: none -> 5.49 us  [the longest x2 3.42 us: sum_last(): far = lax.ppermute(last, 'ffn', swap_perm(4, 2))]
    ppermute x4 -> x3, waiting for transfers between devices: 9.88 us -> 5.76 us  [fold_first(): came = lax.ppermute(sent, axis, swap_perm(4, 1))]
    ppermute x4 -> x3, waiting for transfers between devices: 12.7 us -> 8.98 us  [fold_last(): far = lax.ppermute(leaving, axis, swap_perm(4, 2))]
    pallas_call x1, Pallas kernels: 8.82 us -> 5.25 us  [attend(): pl.pallas_call(functools.partial(attention_kernel, distances=distances),...]
    ppermute x4 -> x3, starting transfers between devices: 7.06 us -> 4.98 us  [fold_last(): far = lax.ppermute(leaving, axis, swap_perm(4, 2))]
    ppermute x4 -> x3, starting transfers between devices: 4.08 us -> 2.02 us  [fold_first(): came = lax.ppermute(sent, axis, swap_perm(4, 1))]
    convert_element_type x3 -> x2, other arithmetic: 2.2 us -> 0.14 us  [fold_first(): return (came[0], (far + came[1].astype(jnp.float32)).astype(jnp.bfloat16))]
  transfers between devices with their start and end apart: 23 -> 25, of which waited for: 18 -> 19; matrix products, arithmetic and copies ran while one was open for 8% -> 7% of each run, Pallas kernels for 15% -> 16%
where the time goes in v3:
time: 118 us
  waiting for transfers between devices  48.2 us (41%)
  starting transfers between devices  29.9 us (25%)
  Pallas kernels  26.9 us (23%)
  other arithmetic  6.62 us (6%)
  local copies, waits for them, and re-layouts  3.7 us (3%)
  matrix products  1.19 us (1%)
    pallas_call x2, Pallas kernels, gate_and_up(): pl.pallas_call(functools.partial(gate_kernel, start=start), out_shape=spl...  13.3 us
    ppermute x3, waiting for transfers between devices, fold_last(): far = lax.ppermute(leaving, axis, swap_perm(4, 2))  8.98 us
    ppermute x2, waiting for transfers between devices, paired_rows(): across = lax.ppermute(quarter, 'attn', swap_perm(4, 2))  8.56 us
    pallas_call x1, Pallas kernels, project(): pl.pallas_call(project_kernel, out_shape=split_shapes(picker.shape[0] //...  5.76 us
    ppermute x3, waiting for transfers between devices, fold_first(): came = lax.ppermute(sent, axis, swap_perm(4, 1))  5.76 us
    ppermute x1, waiting for transfers between devices, body(): across = lax.ppermute(twin, 'attn', swap_perm(4, 2))  5.26 us
    pallas_call x1, Pallas kernels, attend(): pl.pallas_call(functools.partial(attention_kernel, distances=distances),...  5.25 us
    ppermute x3, starting transfers between devices, fold_last(): far = lax.ppermute(leaving, axis, swap_perm(4, 2))  4.98 us
  transfers between devices with their start and end apart: 25, of which 19 were waited for; matrix products, arithmetic and copies ran while one was open for 7% of the time, Pallas kernels for 16%

profile of v3, /device:TPU:0, one launch (start us, length us, event | category | flops | bytes accessed | tf_op | source)
XLA Modules:
  0.0 117.6 jit_solution(17913907955606523072)
XLA Ops:
  1.7 1.2 %convolution_convert_fusion = bf16[32,4608]{1,0:T(8,128)(2,1)S(1)} fusion(bf16[32,512]{1,0:T(8,128)(2,1)} %param.12, bf16[32,4096]{1,0:T(8,128)(2,1)} %param.11, s32[32]{0:T(128)S(1)} %fusion.23), kind=kOutput, calls=%fused_computation.2 | convolution fusion | flops 10175488 | bytes 589952 | tf_op jit(solution)/shard_map/dot_general | solution.py:423
  3.5 2.6 %collective-permute-start.1 = (bf16[8,4608]{1,0:T(8,128)(2,1)S(1)}, bf16[8,4608]{1,0:T(8,128)(2,1)S(1)}, u32[]{:S(2)}, u32[]{:S(2)}) collective-permute-start(bf16[8,4608]{1,0:T(8,128)(2,1)S(1)} %get-tuple-element.124), channel_id=1, source_target_pairs={{0,12},{4,8},{8,4},{12,0},{1,13},{5,9},{9,5},{13,1},{2,14},{6,10},... | collective-permute-start | bytes 221192 | tf_op jit(solution)/shard_map/ppermute | solution.py:431
  8.7 1.8 %collective-permute-done.refs_1_ = bf16[8,4608]{1,0:T(8,128)(2,1)S(1)} collective-permute-done((bf16[8,4608]{1,0:T(8,128)(2,1)S(1)}, bf16[8,4608]{1,0:T(8,128)(2,1)S(1)}, u32[]{:S(2)}, u32[]{:S(2)}) %collective-permute-start) | collective-permute-done | bytes 73760 | tf_op jit(solution)/shard_map/ppermute | solution.py:431
  10.5 5.2 %attention.1 = (bf16[32,4096]{1,0:T(8,128)(2,1)}, bf16[32,4096]{1,0:T(8,128)(2,1)S(1)}, bf16[1,256,512]{2,1,0:T(8,128)(2,1)S(1)}, bf16[1,256,512]{2,1,0:T(8,128)...) custom-call(s32[147]{0:T(256)S(1)} %pad_add_fusion.number_ref, ...), custom_call_target="tpu_custom_call" | custom-call | tf_op jit(solution)/shard_map/attention/pallas_call | solution.py:106
  15.7 1.8 %collective-permute-start.3 = (bf16[32,4096]{1,0:T(8,128)(2,1)S(1)}, bf16[32,4096]{1,0:T(8,128)(2,1)S(1)}, u32[]{:S(2)}, u32[]{:S(2)}) collective-permute-start(bf16[32,4096]{1,0:T(8,128)(2,1)S(1)} %get-tuple-element.66.refs_0_), channel_id=1, source_target_pairs={{0,8},{4,12},{8,0},{12,4},{1,9},{5,13},{9,1},{13,5},{2,10},{6,14},... | collective-permute-start | bytes 786440 | tf_op jit(solution)/shard_map/ppermute | solution.py:459
  18.3 5.3 %collective-permute-done.3.refs_1_ = bf16[32,4096]{1,0:T(8,128)(2,1)S(1)} collective-permute-done((bf16[32,4096]{1,0:T(8,128)(2,1)S(1)}, bf16[32,4096]{1,0:T(8,128)(2,1)S(1)}, u32[]{:S(2)}, u32[]{:S(2)}) %collective-permute-start.3) | collective-permute-done | bytes 262176 | tf_op jit(solution)/shard_map/ppermute | solution.py:459
  25.1 1.7 %collective-permute-start.6 = (bf16[1,256,512]{2,1,0:T(8,128)(2,1)S(1)}, bf16[1,256,512]{2,1,0:T(8,128)(2,1)S(1)}, u32[]{:S(2)}, u32[]{:S(2)}) collective-permute-start(bf16[1,256,512]{2,1,0:T(8,128)(2,1)S(1)} %get-tuple-element.72), channel_id=1, source_target_pairs={{0,8},{4,12},{8,0},{12,4},{1,9},{5,13},{9,1},{13,5},{2,10},{6,14},... | collective-permute-start | bytes 786440 | tf_op jit(solution)/shard_map/ppermute | solution.py:327
  27.1 5.8 %project.1 = (f32[32,1792]{1,0:T(8,128)S(1)}, f32[32,1792]{1,0:T(8,128)S(1)}, bf16[2,32,1792]{2,1,0:T(8,128)(2,1)S(1)}) custom-call(bf16[128,128]{1,0:T(8,128)(2,1)S(1)} %fusion.10.picker_ref, bf16[32,4096]{1,0:T(8,128)(2,1)S(1)} %get-tuple-element.66.refs_0_, bf16[32,4096]{1,0:T(8,128)(2,1)S(1)} %collective-permute-done.3.refs_1_, ...), custom_call_target="tpu_custom_call" | custom-call | tf_op jit(solution)/shard_map/project/pallas_call | solution.py:198
  33.4 1.8 %collective-permute-start.7 = (bf16[2,32,1792]{2,1,0:T(8,128)(2,1)S(1)}, bf16[2,32,1792]{2,1,0:T(8,128)(2,1)S(1)}, u32[]{:S(2)}, u32[]{:S(2)}) collective-permute-start(bf16[2,32,1792]{2,1,0:T(8,128)(2,1)S(1)} %get-tuple-element.74), channel_id=1, source_target_pairs={{0,1},{1,0},{2,3},{3,2},{4,5},{5,4},{6,7},{7,6},{8,9},{9,8},{10,11... | collective-permute-start | bytes 688136 | tf_op jit(solution)/shard_map/ppermute | solution.py:134
  35.2 5.1 %collective-permute-done.7 = bf16[2,32,1792]{2,1,0:T(8,128)(2,1)S(1)} collective-permute-done((bf16[2,32,1792]{2,1,0:T(8,128)(2,1)S(1)}, bf16[2,32,1792]{2,1,0:T(8,128)(2,1)S(1)}, u32[]{:S(2)}, u32[]{:S(2)}) %collective-permute-start.7) | collective-permute-done | bytes 229408 | tf_op jit(solution)/shard_map/ppermute | solution.py:134
  40.4 2.8 %collective-permute-start.9 = (bf16[32,1792]{1,0:T(8,128)(2,1)S(1)}, bf16[32,1792]{1,0:T(8,128)(2,1)S(1)}, u32[]{:S(2)}, u32[]{:S(2)}) collective-permute-start(bf16[32,1792]{1,0:T(8,128)(2,1)S(1)} %get-tuple-element.77), channel_id=1, source_target_pairs={{0,2},{1,3},{2,0},{3,1},{4,6},{5,7},{6,4},{7,5},{8,10},{9,11},{10,... | collective-permute-start | bytes 344072 | tf_op jit(solution)/shard_map/ppermute | solution.py:139
  43.2 2.9 %collective-permute-done.9 = bf16[32,1792]{1,0:T(8,128)(2,1)S(1)} collective-permute-done((bf16[32,1792]{1,0:T(8,128)(2,1)S(1)}, bf16[32,1792]{1,0:T(8,128)(2,1)S(1)}, u32[]{:S(2)}, u32[]{:S(2)}) %collective-permute-start.9) | collective-permute-done | bytes 114720 | tf_op jit(solution)/shard_map/ppermute | solution.py:139
  46.2 2.9 %collective-permute-start.10 = (bf16[32,1792]{1,0:T(8,128)(2,1)S(1)}, bf16[32,1792]{1,0:T(8,128)(2,1)S(1)}, u32[]{:S(2)}, u32[]{:S(2)}) collective-permute-start(bf16[32,1792]{1,0:T(8,128)(2,1)S(1)} %add_convert_fusion), channel_id=1, source_target_pairs={{0,2},{1,3},{2,0},{3,1},{4,6},{5,7},{6,4},{7,5},{8,10},{9,11},{10,... | collective-permute-start | bytes 344072 | tf_op jit(solution)/shard_map/ppermute | solution.py:147
  49.1 2.9 %collective-permute-done.10 = bf16[32,1792]{1,0:T(8,128)(2,1)S(1)} collective-permute-done((bf16[32,1792]{1,0:T(8,128)(2,1)S(1)}, bf16[32,1792]{1,0:T(8,128)(2,1)S(1)}, u32[]{:S(2)}, u32[]{:S(2)}) %collective-permute-start.10) | collective-permute-done | bytes 114720 | tf_op jit(solution)/shard_map/ppermute | solution.py:147
  52.0 4.9 %collective-permute-start.11 = (bf16[2,32,1792]{2,1,0:T(8,128)(2,1)S(1)}, bf16[2,32,1792]{2,1,0:T(8,128)(2,1)S(1)}, u32[]{:S(2)}, u32[]{:S(2)}) collective-permute-start(bf16[2,32,1792]{2,1,0:T(8,128)(2,1)S(1)} %pad_maximum_fusion.6), channel_id=1, source_target_pairs={{0,1},{1,0},{2,3},{3,2},{4,5},{5,4},{6,7},{7,6},{8,9},{9,8},{10,11... | collective-permute-start | bytes 688136 | tf_op jit(solution)/shard_map/ppermute | solution.py:148
  56.9 4.0 %collective-permute-done.11 = bf16[2,32,1792]{2,1,0:T(8,128)(2,1)S(1)} collective-permute-done((bf16[2,32,1792]{2,1,0:T(8,128)(2,1)S(1)}, bf16[2,32,1792]{2,1,0:T(8,128)(2,1)S(1)}, u32[]{:S(2)}, u32[]{:S(2)}) %collective-permute-start.11) | collective-permute-done | bytes 229408 | tf_op jit(solution)/shard_map/ppermute | solution.py:148
  61.5 6.6 %gate_and_up.2 = (f32[32,4608]{1,0:T(8,128)S(1)}, f32[32,4608]{1,0:T(8,128)S(1)}, bf16[2,32,4608]{2,1,0:T(8,128)(2,1)S(1)}) custom-call(bf16[128,1792]{1,0:T(8,128)(2,1)S(1)} %bitcast.73, bf16[1792,4608]{1,0:T(8,128)(2,1)} %gate_ref.3, bf16[1792,4608]{1,0:T(8,128)(2,1)} %up_ref.3), custom_call_target="tpu_custom_call" | custom-call | tf_op jit(solution)/shard_map/gate_and_up/pallas_call | solution.py:236
  68.1 1.5 %collective-permute-done.12 = bf16[1,256,512]{2,1,0:T(8,128)(2,1)S(1)} collective-permute-done((bf16[1,256,512]{2,1,0:T(8,128)(2,1)S(1)}, bf16[1,256,512]{2,1,0:T(8,128)(2,1)S(1)}, u32[]{:S(2)}, u32[]{:S(2)}) %collective-permute-start.12) | collective-permute-done | bytes 262176 | tf_op jit(solution)/shard_map/ppermute | solution.py:336
  72.5 6.7 %gate_and_up.3 = (f32[32,4608]{1,0:T(8,128)S(1)}, f32[32,4608]{1,0:T(8,128)S(1)}, bf16[2,32,4608]{2,1,0:T(8,128)(2,1)S(1)}) custom-call(bf16[128,1792]{1,0:T(8,128)(2,1)S(1)} %bitcast.74, bf16[1792,4608]{1,0:T(8,128)(2,1)} %gate_ref.3, bf16[1792,4608]{1,0:T(8,128)(2,1)} %up_ref.3), custom_call_target="tpu_custom_call" | custom-call | tf_op jit(solution)/shard_map/gate_and_up/pallas_call | solution.py:236
  79.3 1.5 %collective-permute-done.14 = bf16[32,4608]{1,0:T(8,128)(2,1)S(1)} collective-permute-done((bf16[32,4608]{1,0:T(8,128)(2,1)S(1)}, bf16[32,4608]{1,0:T(8,128)(2,1)S(1)}, u32[]{:S(2)}, u32[]{:S(2)}) %collective-permute-start.14) | collective-permute-done | bytes 294944 | tf_op jit(solution)/shard_map/ppermute | solution.py:139
  81.9 1.4 %collective-permute-start.18 = (bf16[32,4608]{1,0:T(8,128)(2,1)S(1)}, bf16[32,4608]{1,0:T(8,128)(2,1)S(1)}, u32[]{:S(2)}, u32[]{:S(2)}) collective-permute-start(bf16[32,4608]{1,0:T(8,128)(2,1)S(1)} %get-tuple-element.116), channel_id=1, source_target_pairs={{0,8},{4,12},{8,0},{12,4},{1,9},{5,13},{9,1},{13,5},{2,10},{6,14},... | collective-permute-start | bytes 884744 | tf_op jit(solution)/shard_map/ppermute | solution.py:139
  83.4 4.5 %collective-permute-done.15 = bf16[32,2304]{1,0:T(8,128)(2,1)S(1)} collective-permute-done((bf16[32,2304]{1,0:T(8,128)(2,1)S(1)}, bf16[32,2304]{1,0:T(8,128)(2,1)S(1)}, u32[]{:S(2)}, u32[]{:S(2)}) %collective-permute-start.15) | collective-permute-done | bytes 147488 | tf_op jit(solution)/shard_map/ppermute | solution.py:352
  88.0 4.5 %collective-permute-done.18 = bf16[32,4608]{1,0:T(8,128)(2,1)S(1)} collective-permute-done((bf16[32,4608]{1,0:T(8,128)(2,1)S(1)}, bf16[32,4608]{1,0:T(8,128)(2,1)S(1)}, u32[]{:S(2)}, u32[]{:S(2)}) %collective-permute-start.18) | collective-permute-done | bytes 294944 | tf_op jit(solution)/shard_map/ppermute | solution.py:139
  92.7 1.1 collective-permute-start.19
  93.8 4.1 %collective-permute-done.19 = bf16[32,2304]{1,0:T(8,128)(2,1)S(1)} collective-permute-done((bf16[32,2304]{1,0:T(8,128)(2,1)S(1)}, bf16[32,2304]{1,0:T(8,128)(2,1)S(1)}, u32[]{:S(2)}, u32[]{:S(2)}) %collective-permute-start.19) | collective-permute-done | bytes 147488 | tf_op jit(solution)/shard_map/ppermute | solution.py:352
  98.1 1.5 %collective-permute-done.20 = bf16[2,32,2304]{2,1,0:T(8,128)(2,1)S(1)} collective-permute-done((bf16[2,32,2304]{2,1,0:T(8,128)(2,1)S(1)}, bf16[2,32,2304]{2,1,0:T(8,128)(2,1)S(1)}, u32[]{:S(2)}, u32[]{:S(2)}) %collective-permute-start.20) | collective-permute-done | bytes 294944 | tf_op jit(solution)/shard_map/ppermute | solution.py:356
  99.7 2.7 %down_project.1 = (f32[32,896]{1,0:T(8,128)S(1)}, f32[32,896]{1,0:T(8,128)S(1)}, bf16[2,32,896]{2,1,0:T(8,128)(2,1)S(1)}, f32[32,896]{1,0:T(8,128)S(1)}, f32[32,...) custom-call(s32[1]{0:T(128)} %bitcast.at_ref, bf16[128,2304]{1,0:T(8,128)(2,1)S(1)} %bitcast.75, ...), custom_call_target="tpu_custom_call" | custom-call | tf_op jit(solution)/shard_map/down_project/pallas_call | solution.py:284
  102.4 2.1 %collective-permute-start.21 = (bf16[2,32,896]{2,1,0:T(8,128)(2,1)S(1)}, bf16[2,32,896]{2,1,0:T(8,128)(2,1)S(1)}, u32[]{:S(2)}, u32[]{:S(2)}) collective-permute-start(bf16[2,32,896]{2,1,0:T(8,128)(2,1)S(1)} %get-tuple-element.105), channel_id=1, source_target_pairs={{0,1},{1,0},{2,3},{3,2},{4,5},{5,4},{6,7},{7,6},{8,9},{9,8},{10,11... | collective-permute-start | bytes 344072 | tf_op jit(solution)/shard_map/ppermute | solution.py:299
  106.4 2.1 %collective-permute-done.21 = bf16[2,32,896]{2,1,0:T(8,128)(2,1)S(1)} collective-permute-done((bf16[2,32,896]{2,1,0:T(8,128)(2,1)S(1)}, bf16[2,32,896]{2,1,0:T(8,128)(2,1)S(1)}, u32[]{:S(2)}, u32[]{:S(2)}) %collective-permute-start.21) | collective-permute-done | bytes 114720 | tf_op jit(solution)/shard_map/ppermute | solution.py:299
  108.5 2.1 %collective-permute-start.22 = (bf16[32,896]{1,0:T(8,128)(2,1)S(1)}, bf16[32,896]{1,0:T(8,128)(2,1)S(1)}, u32[]{:S(2)}, u32[]{:S(2)}) collective-permute-start(bf16[32,896]{1,0:T(8,128)(2,1)S(1)} %fusion.9), channel_id=1, source_target_pairs={{0,2},{1,3},{2,0},{3,1},{4,6},{5,7},{6,4},{7,5},{8,10},{9,11},{10,... | collective-permute-start | bytes 172040 | tf_op jit(solution)/shard_map/ppermute | solution.py:310
  111.5 2.1 %collective-permute-start.24 = (bf16[32,896]{1,0:T(8,128)(2,1)S(1)}, bf16[32,896]{1,0:T(8,128)(2,1)S(1)}, u32[]{:S(2)}, u32[]{:S(2)}) collective-permute-start(bf16[32,896]{1,0:T(8,128)(2,1)S(1)} %get-tuple-element.133), channel_id=1, source_target_pairs={{0,2},{1,3},{2,0},{3,1},{4,6},{5,7},{6,4},{7,5},{8,10},{9,11},{10,... | collective-permute-start | bytes 172040 | tf_op jit(solution)/shard_map/ppermute | solution.py:310
  113.6 3.3 %collective-permute-done.24 = bf16[32,896]{1,0:T(8,128)(2,1)S(1)} collective-permute-done((bf16[32,896]{1,0:T(8,128)(2,1)S(1)}, bf16[32,896]{1,0:T(8,128)(2,1)S(1)}, u32[]{:S(2)}, u32[]{:S(2)}) %collective-permute-start.24) | collective-permute-done | bytes 57376 | tf_op jit(solution)/shard_map/ppermute | solution.py:310
  (100 shorter events, 16.0 us)
Async XLA Ops:
  0.6 23.6 %copy-start = (bf16[128,1792]{1,0:T(8,128)(2,1)S(1)}, bf16[128,1792]{1,0:T(8,128)(2,1)}, u32[]{:S(2)}) copy-start(bf16[128,1792]{1,0:T(8,128)(2,1)} %param.17) | copy-start | bytes 1376260
  0.6 60.4 %copy-start.4 = (s32[4,4,1]{1,2,0:T(1,128)S(1)}, s32[4,4,1]{1,2,0:T(1,128)}, u32[]{:S(2)}) copy-start(s32[4,4,1]{1,2,0:T(1,128)} %param.16) | copy-start | bytes 196
  2.9 4.8 %collective-permute-start.2 = (bf16[8,4608]{1,0:T(8,128)(2,1)S(1)}, bf16[8,4608]{1,0:T(8,128)(2,1)S(1)}, u32[]{:S(2)}, u32[]{:S(2)}) collective-permute-start(bf16[8,4608]{1,0:T(8,128)(2,1)S(1)} %get-tuple-element.123), channel_id=1, source_target_pairs={{0,4},{4,0},{8,12},{12,8},{1,5},{5,1},{9,13},{13,9},{2,6},{6,2},{1... | collective-permute-start | bytes 221192 | tf_op jit(solution)/shard_map/ppermute | solution.py:431
  3.5 5.2 %collective-permute-start.1 = (bf16[8,4608]{1,0:T(8,128)(2,1)S(1)}, bf16[8,4608]{1,0:T(8,128)(2,1)S(1)}, u32[]{:S(2)}, u32[]{:S(2)}) collective-permute-start(bf16[8,4608]{1,0:T(8,128)(2,1)S(1)} %get-tuple-element.124), channel_id=1, source_target_pairs={{0,12},{4,8},{8,4},{12,0},{1,13},{5,9},{9,5},{13,1},{2,14},{6,10},... | collective-permute-start | bytes 221192 | tf_op jit(solution)/shard_map/ppermute | solution.py:431
  6.1 4.4 %collective-permute-start = (bf16[8,4608]{1,0:T(8,128)(2,1)S(1)}, bf16[8,4608]{1,0:T(8,128)(2,1)S(1)}, u32[]{:S(2)}, u32[]{:S(2)}) collective-permute-start(bf16[8,4608]{1,0:T(8,128)(2,1)S(1)} %get-tuple-element.125), channel_id=1, source_target_pairs={{0,8},{4,12},{8,0},{12,4},{1,9},{5,13},{9,1},{13,5},{2,10},{6,14},... | collective-permute-start | bytes 221192 | tf_op jit(solution)/shard_map/ppermute | solution.py:431
  15.7 7.8 %collective-permute-start.3 = (bf16[32,4096]{1,0:T(8,128)(2,1)S(1)}, bf16[32,4096]{1,0:T(8,128)(2,1)S(1)}, u32[]{:S(2)}, u32[]{:S(2)}) collective-permute-start(bf16[32,4096]{1,0:T(8,128)(2,1)S(1)} %get-tuple-element.66.refs_0_), channel_id=1, source_target_pairs={{0,8},{4,12},{8,0},{12,4},{1,9},{5,13},{9,1},{13,5},{2,10},{6,14},... | collective-permute-start | bytes 786440 | tf_op jit(solution)/shard_map/ppermute | solution.py:459
  18.2 6.0 %collective-permute-start.4 = (bf16[32,4096]{1,0:T(8,128)(2,1)S(1)}, bf16[32,4096]{1,0:T(8,128)(2,1)S(1)}, u32[]{:S(2)}, u32[]{:S(2)}) collective-permute-start(bf16[32,4096]{1,0:T(8,128)(2,1)S(1)} %get-tuple-element.66.refs_0_), channel_id=1, source_target_pairs={{0,4},{4,0},{8,12},{12,8},{1,5},{5,1},{9,13},{13,9},{2,6},{6,2},{1... | collective-permute-start | bytes 786440 | tf_op jit(solution)/shard_map/ppermute | solution.py:460
  23.5 1.5 %collective-permute-start.5 = (bf16[32,4096]{1,0:T(8,128)(2,1)S(1)}, bf16[32,4096]{1,0:T(8,128)(2,1)S(1)}, u32[]{:S(2)}, u32[]{:S(2)}) collective-permute-start(bf16[32,4096]{1,0:T(8,128)(2,1)S(1)} %collective-permute-done.3.refs_1_), channel_id=1, source_target_pairs={{0,4},{4,0},{8,12},{12,8},{1,5},{5,1},{9,13},{13,9},{2,6},{6,2},{1... | collective-permute-start | bytes 786440 | tf_op jit(solution)/shard_map/ppermute | solution.py:461
  25.1 8.3 %collective-permute-start.6 = (bf16[1,256,512]{2,1,0:T(8,128)(2,1)S(1)}, bf16[1,256,512]{2,1,0:T(8,128)(2,1)S(1)}, u32[]{:S(2)}, u32[]{:S(2)}) collective-permute-start(bf16[1,256,512]{2,1,0:T(8,128)(2,1)S(1)} %get-tuple-element.72), channel_id=1, source_target_pairs={{0,8},{4,12},{8,0},{12,4},{1,9},{5,13},{9,1},{13,5},{2,10},{6,14},... | collective-permute-start | bytes 786440 | tf_op jit(solution)/shard_map/ppermute | solution.py:327
  33.4 6.9 %collective-permute-start.7 = (bf16[2,32,1792]{2,1,0:T(8,128)(2,1)S(1)}, bf16[2,32,1792]{2,1,0:T(8,128)(2,1)S(1)}, u32[]{:S(2)}, u32[]{:S(2)}) collective-permute-start(bf16[2,32,1792]{2,1,0:T(8,128)(2,1)S(1)} %get-tuple-element.74), channel_id=1, source_target_pairs={{0,1},{1,0},{2,3},{3,2},{4,5},{5,4},{6,7},{7,6},{8,9},{9,8},{10,11... | collective-permute-start | bytes 688136 | tf_op jit(solution)/shard_map/ppermute | solution.py:134
  35.2 5.1 %collective-permute-start.8 = (bf16[1,256,512]{2,1,0:T(8,128)(2,1)S(1)}, bf16[1,256,512]{2,1,0:T(8,128)(2,1)S(1)}, u32[]{:S(2)}, u32[]{:S(2)}) collective-permute-start(bf16[1,256,512]{2,1,0:T(8,128)(2,1)S(1)} %get-tuple-element.76), channel_id=1, source_target_pairs={{0,4},{4,0},{8,12},{12,8},{1,5},{5,1},{9,13},{13,9},{2,6},{6,2},{1... | collective-permute-start | bytes 786440 | tf_op jit(solution)/shard_map/ppermute | solution.py:330
  40.4 5.8 %collective-permute-start.9 = (bf16[32,1792]{1,0:T(8,128)(2,1)S(1)}, bf16[32,1792]{1,0:T(8,128)(2,1)S(1)}, u32[]{:S(2)}, u32[]{:S(2)}) collective-permute-start(bf16[32,1792]{1,0:T(8,128)(2,1)S(1)} %get-tuple-element.77), channel_id=1, source_target_pairs={{0,2},{1,3},{2,0},{3,1},{4,6},{5,7},{6,4},{7,5},{8,10},{9,11},{10,... | collective-permute-start | bytes 344072 | tf_op jit(solution)/shard_map/ppermute | solution.py:139
  46.2 5.8 %collective-permute-start.10 = (bf16[32,1792]{1,0:T(8,128)(2,1)S(1)}, bf16[32,1792]{1,0:T(8,128)(2,1)S(1)}, u32[]{:S(2)}, u32[]{:S(2)}) collective-permute-start(bf16[32,1792]{1,0:T(8,128)(2,1)S(1)} %add_convert_fusion), channel_id=1, source_target_pairs={{0,2},{1,3},{2,0},{3,1},{4,6},{5,7},{6,4},{7,5},{8,10},{9,11},{10,... | collective-permute-start | bytes 344072 | tf_op jit(solution)/shard_map/ppermute | solution.py:147
  52.0 8.9 %collective-permute-start.11 = (bf16[2,32,1792]{2,1,0:T(8,128)(2,1)S(1)}, bf16[2,32,1792]{2,1,0:T(8,128)(2,1)S(1)}, u32[]{:S(2)}, u32[]{:S(2)}) collective-permute-start(bf16[2,32,1792]{2,1,0:T(8,128)(2,1)S(1)} %pad_maximum_fusion.6), channel_id=1, source_target_pairs={{0,1},{1,0},{2,3},{3,2},{4,5},{5,4},{6,7},{7,6},{8,9},{9,8},{10,11... | collective-permute-start | bytes 688136 | tf_op jit(solution)/shard_map/ppermute | solution.py:148
  61.0 8.6 %collective-permute-start.12 = (bf16[1,256,512]{2,1,0:T(8,128)(2,1)S(1)}, bf16[1,256,512]{2,1,0:T(8,128)(2,1)S(1)}, u32[]{:S(2)}, u32[]{:S(2)}) collective-permute-start(bf16[1,256,512]{2,1,0:T(8,128)(2,1)S(1)} %get-tuple-element.82), channel_id=1, source_target_pairs={{0,12},{4,8},{8,4},{12,0},{1,13},{5,9},{9,5},{13,1},{2,14},{6,10},... | collective-permute-start | bytes 786440 | tf_op jit(solution)/shard_map/ppermute | solution.py:336
  69.6 2.0 %collective-permute-start.13 = (bf16[2,32,4608]{2,1,0:T(8,128)(2,1)S(1)}, bf16[2,32,4608]{2,1,0:T(8,128)(2,1)S(1)}, u32[]{:S(2)}, u32[]{:S(2)}) collective-permute-start(bf16[2,32,4608]{2,1,0:T(8,128)(2,1)S(1)} %get-tuple-element.83), channel_id=1, source_target_pairs={{0,4},{4,0},{8,12},{12,8},{1,5},{5,1},{9,13},{13,9},{2,6},{6,2},{1... | collective-permute-start | bytes 1769480 | tf_op jit(solution)/shard_map/ppermute | solution.py:134
  71.7 9.1 %collective-permute-start.14 = (bf16[32,4608]{1,0:T(8,128)(2,1)S(1)}, bf16[32,4608]{1,0:T(8,128)(2,1)S(1)}, u32[]{:S(2)}, u32[]{:S(2)}) collective-permute-start(bf16[32,4608]{1,0:T(8,128)(2,1)S(1)} %get-tuple-element.117), channel_id=1, source_target_pairs={{0,8},{4,12},{8,0},{12,4},{1,9},{5,13},{9,1},{13,5},{2,10},{6,14},... | collective-permute-start | bytes 884744 | tf_op jit(solution)/shard_map/ppermute | solution.py:139
  72.4 27.3 %slice-start = ((s8[16515072]{0:T(1024)(128)(4,1)}), s8[4194304]{0:T(1024)(128)(4,1)S(1)}, s32[]{:S(2)}) async-start(s8[16515072]{0:T(1024)(128)(4,1)} %bitcast.71), calls=%async_computation | async-start | bytes 8388608
  72.5 27.2 %slice-start.1 = ((s8[16515072]{0:T(1024)(128)(4,1)}), s8[4194304]{0:T(1024)(128)(4,1)S(1)}, s32[]{:S(2)}) async-start(s8[16515072]{0:T(1024)(128)(4,1)} %bitcast.71), calls=%async_computation.1 | async-start | bytes 8388608
  72.5 27.2 %slice-start.2 = ((s8[16515072]{0:T(1024)(128)(4,1)}), s8[3932160]{0:T(1024)(128)(4,1)S(1)}, s32[]{:S(2)}) async-start(s8[16515072]{0:T(1024)(128)(4,1)} %bitcast.71), calls=%async_computation.2 | async-start | bytes 7864320
  79.2 25.4 %copy-start.3 = (bf16[1,256,512]{2,1,0:T(8,128)(2,1)S(1)}, bf16[1,256,512]{2,1,0:T(8,128)(2,1)}, u32[]{:S(2)}) copy-start(bf16[1,256,512]{2,1,0:T(8,128)(2,1)} %copy-done.2) | copy-start | bytes 786436
  79.2 2.6 %collective-permute-start.16 = (bf16[2,32,4608]{2,1,0:T(8,128)(2,1)S(1)}, bf16[2,32,4608]{2,1,0:T(8,128)(2,1)S(1)}, u32[]{:S(2)}, u32[]{:S(2)}) collective-permute-start(bf16[2,32,4608]{2,1,0:T(8,128)(2,1)S(1)} %get-tuple-element.87), channel_id=1, source_target_pairs={{0,4},{4,0},{8,12},{12,8},{1,5},{5,1},{9,13},{13,9},{2,6},{6,2},{1... | collective-permute-start | bytes 1769480 | tf_op jit(solution)/shard_map/ppermute | solution.py:134
  81.0 6.8 %collective-permute-start.15 = (bf16[32,2304]{1,0:T(8,128)(2,1)S(1)}, bf16[32,2304]{1,0:T(8,128)(2,1)S(1)}, u32[]{:S(2)}, u32[]{:S(2)}) collective-permute-start(bf16[32,2304]{1,0:T(8,128)(2,1)S(1)} %fusion.3), channel_id=1, source_target_pairs={{0,8},{4,12},{8,0},{12,4},{1,9},{5,13},{9,1},{13,5},{2,10},{6,14},... | collective-permute-start | bytes 442376 | tf_op jit(solution)/shard_map/ppermute | solution.py:352
  81.8 35.8 %copy-start.1 = (bf16[128,1792]{1,0:T(8,128)(2,1)S(1)}, bf16[128,1792]{1,0:T(8,128)(2,1)}, u32[]{:S(2)}) copy-start(bf16[128,1792]{1,0:T(8,128)(2,1)} %param.17) | copy-start | bytes 1376260
  81.9 10.5 %collective-permute-start.18 = (bf16[32,4608]{1,0:T(8,128)(2,1)S(1)}, bf16[32,4608]{1,0:T(8,128)(2,1)S(1)}, u32[]{:S(2)}, u32[]{:S(2)}) collective-permute-start(bf16[32,4608]{1,0:T(8,128)(2,1)S(1)} %get-tuple-element.116), channel_id=1, source_target_pairs={{0,8},{4,12},{8,0},{12,4},{1,9},{5,13},{9,1},{13,5},{2,10},{6,14},... | collective-permute-start | bytes 884744 | tf_op jit(solution)/shard_map/ppermute | solution.py:139
  87.9 5.9 %collective-permute-start.17 = (bf16[2,32,2304]{2,1,0:T(8,128)(2,1)S(1)}, bf16[2,32,2304]{2,1,0:T(8,128)(2,1)S(1)}, u32[]{:S(2)}, u32[]{:S(2)}) collective-permute-start(bf16[2,32,2304]{2,1,0:T(8,128)(2,1)S(1)} %pad_maximum_fusion.4), channel_id=1, source_target_pairs={{0,4},{4,0},{8,12},{12,8},{1,5},{5,1},{9,13},{13,9},{2,6},{6,2},{1... | collective-permute-start | bytes 884744 | tf_op jit(solution)/shard_map/ppermute | solution.py:356
  92.7 5.2 %collective-permute-start.19 = (bf16[32,2304]{1,0:T(8,128)(2,1)S(1)}, bf16[32,2304]{1,0:T(8,128)(2,1)S(1)}, u32[]{:S(2)}, u32[]{:S(2)}) collective-permute-start(bf16[32,2304]{1,0:T(8,128)(2,1)S(1)} %fusion.2), channel_id=1, source_target_pairs={{0,8},{4,12},{8,0},{12,4},{1,9},{5,13},{9,1},{13,5},{2,10},{6,14},... | collective-permute-start | bytes 442376 | tf_op jit(solution)/shard_map/ppermute | solution.py:352
  97.9 1.6 %collective-permute-start.20 = (bf16[2,32,2304]{2,1,0:T(8,128)(2,1)S(1)}, bf16[2,32,2304]{2,1,0:T(8,128)(2,1)S(1)}, u32[]{:S(2)}, u32[]{:S(2)}) collective-permute-start(bf16[2,32,2304]{2,1,0:T(8,128)(2,1)S(1)} %pad_maximum_fusion.5), channel_id=1, source_target_pairs={{0,4},{4,0},{8,12},{12,8},{1,5},{5,1},{9,13},{13,9},{2,6},{6,2},{1... | collective-permute-start | bytes 884744 | tf_op jit(solution)/shard_map/ppermute | solution.py:356
  102.4 6.0 %collective-permute-start.21 = (bf16[2,32,896]{2,1,0:T(8,128)(2,1)S(1)}, bf16[2,32,896]{2,1,0:T(8,128)(2,1)S(1)}, u32[]{:S(2)}, u32[]{:S(2)}) collective-permute-start(bf16[2,32,896]{2,1,0:T(8,128)(2,1)S(1)} %get-tuple-element.105), channel_id=1, source_target_pairs={{0,1},{1,0},{2,3},{3,2},{4,5},{5,4},{6,7},{7,6},{8,9},{9,8},{10,11... | collective-permute-start | bytes 344072 | tf_op jit(solution)/shard_map/ppermute | solution.py:299
  104.5 6.0 %collective-permute-start.23 = (bf16[2,32,896]{2,1,0:T(8,128)(2,1)S(1)}, bf16[2,32,896]{2,1,0:T(8,128)(2,1)}, u32[]{:S(2)}, u32[]{:S(2)}) collective-permute-start(bf16[2,32,896]{2,1,0:T(8,128)(2,1)S(1)} %get-tuple-element.108), channel_id=1, source_target_pairs={{0,1},{1,0},{2,3},{3,2},{4,5},{5,4},{6,7},{7,6},{8,9},{9,8},{10,11... | collective-permute-start | bytes 344072 | tf_op jit(solution)/shard_map/ppermute | solution.py:299
  108.5 5.1 %collective-permute-start.22 = (bf16[32,896]{1,0:T(8,128)(2,1)S(1)}, bf16[32,896]{1,0:T(8,128)(2,1)S(1)}, u32[]{:S(2)}, u32[]{:S(2)}) collective-permute-start(bf16[32,896]{1,0:T(8,128)(2,1)S(1)} %fusion.9), channel_id=1, source_target_pairs={{0,2},{1,3},{2,0},{3,1},{4,6},{5,7},{6,4},{7,5},{8,10},{9,11},{10,... | collective-permute-start | bytes 172040 | tf_op jit(solution)/shard_map/ppermute | solution.py:310
  111.5 5.5 %collective-permute-start.24 = (bf16[32,896]{1,0:T(8,128)(2,1)S(1)}, bf16[32,896]{1,0:T(8,128)(2,1)S(1)}, u32[]{:S(2)}, u32[]{:S(2)}) collective-permute-start(bf16[32,896]{1,0:T(8,128)(2,1)S(1)} %get-tuple-element.133), channel_id=1, source_target_pairs={{0,2},{1,3},{2,0},{3,1},{4,6},{5,7},{6,4},{7,5},{8,10},{9,11},{10,... | collective-permute-start | bytes 172040 | tf_op jit(solution)/shard_map/ppermute | solution.py:310
  (2 other events, 28.4 us)

commit v4 on v3

--- a/solution.py
+++ b/solution.py
@@ -8,7 +8,7 @@
 from jax.sharding import PartitionSpec as P
 
 CHUNKS = 2
-PARTS = 2
+PARTS = 1
 
 
 def attention_kernel(number_ref, *refs, distances):
@@ -314,6 +314,17 @@
     return outs
 
 
+def sum_direct(near, far, sent, own):
+    far = far.astype(jnp.bfloat16)
+    came = [
+        lax.ppermute(x, "ffn", swap_perm(4, d)) for d, x in ((2, far), (3, sent[1]), (1, sent[0]))
+    ]
+    total = lax.optimization_barrier(own.astype(jnp.float32) + near)
+    for part in came:
+        total = total + part.astype(jnp.float32)
+    return total.astype(jnp.bfloat16)
+
+
 def paired_rows(
     pieces, row_picker, residual, turn, position, pages, w_out, w_gate, w_up, w_down
 ):
@@ -326,12 +337,12 @@
     landed = list(pages)
     landed[2] = lax.ppermute(pages[2], "attn", swap_perm(4, 2))
     near, far, sent = project(row_picker, pieces, w_out)
-    sent, landed[2], pages[1] = lax.optimization_barrier((sent, landed[2], pages[1]))
+    sent, pages[1] = lax.optimization_barrier((sent, pages[1]))
     landed[1] = lax.ppermute(pages[1], "attn", swap_perm(4, 1))
-    came, leaving = fold_first(sent, far, "ffn")
-    leaving, landed[1] = lax.optimization_barrier((leaving, landed[1]))
-    kept = fold_last(leaving, (mine, near, came), "ffn").astype(jnp.bfloat16)
-    mixed = spread(kept, "ffn")
+    kept = sum_direct(near, far, sent, mine)
+    came = {d: lax.ppermute(kept, "ffn", swap_perm(4, d)) for d in (2, 3, 1)}
+    mixed = jnp.stack([kept, came[1], came[2], came[3]])
+    mixed, landed[1], landed[2] = lax.optimization_barrier((mixed, landed[1], landed[2]))
     mixed, pages[3] = lax.optimization_barrier((mixed, pages[3]))
     landed[3] = lax.ppermute(pages[3], "attn", swap_perm(4, 3))
     rows = mixed.reshape(count, columns)
@@ -358,10 +369,8 @@
         hiddens.append(hidden)
     sums = down_project(position, hiddens, w_down)
     sums, landed = lax.optimization_barrier((sums, landed))
-    near, leaving = sum_first(sums)
     kept = lax.dynamic_index_in_dim(mixed, position, 0, keepdims=False)
-    part = columns // PARTS
-    outs = sum_last(leaving, [kept[:, p * part : (p + 1) * part] for p in range(PARTS)], near)
+    outs = [sum_direct(*sums[0], kept)]
     return jnp.concatenate(outs, axis=1), landed
 
 

time: 118 us -> 113 us (0.958)
  starting transfers between devices: 29.9 us -> 25.2 us
    ppermute x6 -> x9, waiting for transfers between devices: 12.4 us -> 22.1 us  [the longest x6 14.6 us: sum_direct(): lax.ppermute(x, 'ffn', swap_perm(4, d))]
    ppermute x3 -> x2, waiting for transfers between devices: 5.76 us -> 0.01 us  [fold_first(): came = lax.ppermute(sent, axis, swap_perm(4, 1))]
    ppermute x3 -> x2, waiting for transfers between devices: 8.98 us -> 5.72 us  [fold_last(): far = lax.ppermute(leaving, axis, swap_perm(4, 2))]
    ppermute x3 -> x2, starting transfers between devices: 4.98 us -> 2.3 us  [fold_last(): far = lax.ppermute(leaving, axis, swap_perm(4, 2))]
    ppermute x3 -> x2, starting transfers between devices: 2.02 us -> 0.19 us  [fold_first(): came = lax.ppermute(sent, axis, swap_perm(4, 1))]
    ppermute x6 -> x9, starting transfers between devices: 14.1 us -> 13.2 us  [the longest x6 8.74 us: sum_direct(): lax.ppermute(x, 'ffn', swap_perm(4, d))]
  transfers between devices with their start and end apart: 25 -> 26, of which waited for: 19 -> 16; matrix products, arithmetic and copies ran while one was open for 7% -> 7% of each run, Pallas kernels for 16% -> 12%
where the time goes in v4:
time: 113 us; the launch traced here: 112 us
  waiting for transfers between devices  48.1 us (43%)
  Pallas kernels  26.6 us (24%)
  starting transfers between devices  25.2 us (22%)
  other arithmetic  5.91 us (5%)
  local copies, waits for them, and re-layouts  4.3 us (4%)
  matrix products  1.19 us (1%)
    ppermute x6, waiting for transfers between devices, sum_direct(): lax.ppermute(x, 'ffn', swap_perm(4, d))  14.6 us
    pallas_call x2, Pallas kernels, gate_and_up(): pl.pallas_call(functools.partial(gate_kernel, start=start), out_shape=spl...  13.3 us
    ppermute x2, waiting for transfers between devices, paired_rows(): across = lax.ppermute(quarter, 'attn', swap_perm(4, 2))  8.85 us
    ppermute x6, starting transfers between devices, sum_direct(): lax.ppermute(x, 'ffn', swap_perm(4, d))  8.74 us
    ppermute x3, waiting for transfers between devices, paired_rows(): came = {d: lax.ppermute(kept, 'ffn', swap_perm(4, d)) for d in (2, 3, 1)}  7.49 us
    pallas_call x1, Pallas kernels, project(): pl.pallas_call(project_kernel, out_shape=split_shapes(picker.shape[0] //...  5.75 us
    ppermute x2, waiting for transfers between devices, fold_last(): far = lax.ppermute(leaving, axis, swap_perm(4, 2))  5.72 us
    pallas_call x1, Pallas kernels, attend(): pl.pallas_call(functools.partial(attention_kernel, distances=distances),...  5.25 us
  transfers between devices with their start and end apart: 26, of which 16 were waited for; matrix products, arithmetic and copies ran while one was open for 7% of the time, Pallas kernels for 12%

profile of v4, /device:TPU:0, one launch (start us, length us, event | category | flops | bytes accessed | tf_op | source)
XLA Modules:
  0.0 112.4 jit_solution(11659514808129037843)
XLA Ops:
  0.7 0.8 eq.30
  1.7 1.2 %convolution_convert_fusion = bf16[32,4608]{1,0:T(8,128)(2,1)S(1)} fusion(bf16[32,512]{1,0:T(8,128)(2,1)} %param.12, bf16[32,4096]{1,0:T(8,128)(2,1)} %param.11, s32[32]{0:T(128)S(1)} %fusion.20), kind=kOutput, calls=%fused_computation.2 | convolution fusion | flops 10175488 | bytes 589952 | tf_op jit(solution)/shard_map/dot_general | solution.py:432
  3.4 2.6 %collective-permute-start.1 = (bf16[8,4608]{1,0:T(8,128)(2,1)S(1)}, bf16[8,4608]{1,0:T(8,128)(2,1)S(1)}, u32[]{:S(2)}, u32[]{:S(2)}) collective-permute-start(bf16[8,4608]{1,0:T(8,128)(2,1)S(1)} %get-tuple-element.106), channel_id=1, source_target_pairs={{0,12},{4,8},{8,4},{12,0},{1,13},{5,9},{9,5},{13,1},{2,14},{6,10},... | collective-permute-start | bytes 221192 | tf_op jit(solution)/shard_map/ppermute | solution.py:440
  8.7 1.8 %collective-permute-done.refs_1_ = bf16[8,4608]{1,0:T(8,128)(2,1)S(1)} collective-permute-done((bf16[8,4608]{1,0:T(8,128)(2,1)S(1)}, bf16[8,4608]{1,0:T(8,128)(2,1)S(1)}, u32[]{:S(2)}, u32[]{:S(2)}) %collective-permute-start) | collective-permute-done | bytes 73760 | tf_op jit(solution)/shard_map/ppermute | solution.py:440
  10.5 5.2 %attention.1 = (bf16[32,4096]{1,0:T(8,128)(2,1)}, bf16[32,4096]{1,0:T(8,128)(2,1)S(1)}, bf16[1,256,512]{2,1,0:T(8,128)(2,1)S(1)}, bf16[1,256,512]{2,1,0:T(8,128)...) custom-call(s32[147]{0:T(256)S(1)} %pad_add_fusion.number_ref, ...), custom_call_target="tpu_custom_call" | custom-call | tf_op jit(solution)/shard_map/attention/pallas_call | solution.py:106
  15.7 1.8 %collective-permute-start.3 = (bf16[32,4096]{1,0:T(8,128)(2,1)S(1)}, bf16[32,4096]{1,0:T(8,128)(2,1)S(1)}, u32[]{:S(2)}, u32[]{:S(2)}) collective-permute-start(bf16[32,4096]{1,0:T(8,128)(2,1)S(1)} %get-tuple-element.57.refs_0_), channel_id=1, source_target_pairs={{0,8},{4,12},{8,0},{12,4},{1,9},{5,13},{9,1},{13,5},{2,10},{6,14},... | collective-permute-start | bytes 786440 | tf_op jit(solution)/shard_map/ppermute | solution.py:468
  18.3 5.2 %collective-permute-done.3.refs_1_ = bf16[32,4096]{1,0:T(8,128)(2,1)S(1)} collective-permute-done((bf16[32,4096]{1,0:T(8,128)(2,1)S(1)}, bf16[32,4096]{1,0:T(8,128)(2,1)S(1)}, u32[]{:S(2)}, u32[]{:S(2)}) %collective-permute-start.3) | collective-permute-done | bytes 262176 | tf_op jit(solution)/shard_map/ppermute | solution.py:468
  23.7 1.4 %collective-permute-done.5.refs_3_ = bf16[32,4096]{1,0:T(8,128)(2,1)S(1)} collective-permute-done((bf16[32,4096]{1,0:T(8,128)(2,1)S(1)}, bf16[32,4096]{1,0:T(8,128)(2,1)S(1)}, u32[]{:S(2)}, u32[]{:S(2)}) %collective-permute-start.5) | collective-permute-done | bytes 262176 | tf_op jit(solution)/shard_map/ppermute | solution.py:470
  25.1 5.8 %project.1 = (f32[32,1792]{1,0:T(8,128)S(1)}, f32[32,1792]{1,0:T(8,128)S(1)}, bf16[2,32,1792]{2,1,0:T(8,128)(2,1)S(1)}) custom-call(bf16[128,128]{1,0:T(8,128)(2,1)S(1)} %fusion.7.picker_ref, bf16[32,4096]{1,0:T(8,128)(2,1)S(1)} %get-tuple-element.57.refs_0_, bf16[32,4096]{1,0:T(8,128)(2,1)S(1)} %collective-permute-done.3.refs_1_, ...), custom_call_target="tpu_custom_call" | custom-call | tf_op jit(solution)/shard_map/project/pallas_call | solution.py:198
  30.9 2.9 %collective-permute-start.6 = (bf16[32,1792]{1,0:T(8,128)(2,1)S(1)}, bf16[32,1792]{1,0:T(8,128)(2,1)S(1)}, u32[]{:S(2)}, u32[]{:S(2)}) collective-permute-start(bf16[32,1792]{1,0:T(8,128)(2,1)S(1)} %convert_element_type.112), channel_id=1, source_target_pairs={{0,2},{1,3},{2,0},{3,1},{4,6},{5,7},{6,4},{7,5},{8,10},{9,11},{10,... | collective-permute-start | bytes 344072 | tf_op jit(solution)/shard_map/ppermute | solution.py:320
  33.8 1.3 %collective-permute-start.7 = (bf16[32,1792]{1,0:T(8,128)(2,1)S(1)}, bf16[32,1792]{1,0:T(8,128)(2,1)S(1)}, u32[]{:S(2)}, u32[]{:S(2)}) collective-permute-start(bf16[32,1792]{1,0:T(8,128)(2,1)S(1)} %get-tuple-element.111), channel_id=1, source_target_pairs={{0,3},{1,2},{2,1},{3,0},{4,7},{5,6},{6,5},{7,4},{8,11},{9,10},{10,... | collective-permute-start | bytes 344072 | tf_op jit(solution)/shard_map/ppermute | solution.py:320
  35.4 7.4 %collective-permute-done.6 = bf16[32,1792]{1,0:T(8,128)(2,1)S(1)} collective-permute-done((bf16[32,1792]{1,0:T(8,128)(2,1)S(1)}, bf16[32,1792]{1,0:T(8,128)(2,1)S(1)}, u32[]{:S(2)}, u32[]{:S(2)}) %collective-permute-start.6) | collective-permute-done | bytes 114720 | tf_op jit(solution)/shard_map/ppermute | solution.py:320
  43.6 3.6 %collective-permute-start.11 = (bf16[32,1792]{1,0:T(8,128)(2,1)S(1)}, bf16[32,1792]{1,0:T(8,128)(2,1)S(1)}, u32[]{:S(2)}, u32[]{:S(2)}) collective-permute-start(bf16[32,1792]{1,0:T(8,128)(2,1)S(1)} %add_convert_fusion.1), channel_id=1, source_target_pairs={{0,3},{1,2},{2,1},{3,0},{4,7},{5,6},{6,5},{7,4},{8,11},{9,10},{10,... | collective-permute-start | bytes 344072 | tf_op jit(solution)/shard_map/ppermute | solution.py:343
  48.0 1.5 %collective-permute-start.13 = (bf16[1,256,512]{2,1,0:T(8,128)(2,1)S(1)}, bf16[1,256,512]{2,1,0:T(8,128)(2,1)S(1)}, u32[]{:S(2)}, u32[]{:S(2)}) collective-permute-start(bf16[1,256,512]{2,1,0:T(8,128)(2,1)S(1)} %get-tuple-element.67), channel_id=1, source_target_pairs={{0,8},{4,12},{8,0},{12,4},{1,9},{5,13},{9,1},{13,5},{2,10},{6,14},... | collective-permute-start | bytes 786440 | tf_op jit(solution)/shard_map/ppermute | solution.py:338
  49.6 1.2 %collective-permute-done.11 = bf16[32,1792]{1,0:T(8,128)(2,1)S(1)} collective-permute-done((bf16[32,1792]{1,0:T(8,128)(2,1)S(1)}, bf16[32,1792]{1,0:T(8,128)(2,1)S(1)}, u32[]{:S(2)}, u32[]{:S(2)}) %collective-permute-start.11) | collective-permute-done | bytes 114720 | tf_op jit(solution)/shard_map/ppermute | solution.py:343
  50.8 6.3 %collective-permute-done.10 = bf16[32,1792]{1,0:T(8,128)(2,1)S(1)} collective-permute-done((bf16[32,1792]{1,0:T(8,128)(2,1)S(1)}, bf16[32,1792]{1,0:T(8,128)(2,1)S(1)}, u32[]{:S(2)}, u32[]{:S(2)}) %collective-permute-start.10) | collective-permute-done | bytes 114720 | tf_op jit(solution)/shard_map/ppermute | solution.py:343
  57.2 0.8 collective-permute-start.14
  58.0 6.6 %gate_and_up.2 = (f32[32,4608]{1,0:T(8,128)S(1)}, f32[32,4608]{1,0:T(8,128)S(1)}, bf16[2,32,4608]{2,1,0:T(8,128)(2,1)S(1)}) custom-call(bf16[128,1792]{1,0:T(8,128)(2,1)S(1)} %bitcast.58, bf16[1792,4608]{1,0:T(8,128)(2,1)} %gate_ref.3, bf16[1792,4608]{1,0:T(8,128)(2,1)} %up_ref.3), custom_call_target="tpu_custom_call" | custom-call | tf_op jit(solution)/shard_map/gate_and_up/pallas_call | solution.py:236
  64.6 1.2 %collective-permute-done.14 = bf16[1,256,512]{2,1,0:T(8,128)(2,1)S(1)} collective-permute-done((bf16[1,256,512]{2,1,0:T(8,128)(2,1)S(1)}, bf16[1,256,512]{2,1,0:T(8,128)(2,1)S(1)}, u32[]{:S(2)}, u32[]{:S(2)}) %collective-permute-start.14) | collective-permute-done | bytes 262176 | tf_op jit(solution)/shard_map/ppermute | solution.py:347
  67.2 0.9 iota_reduce_fusion
  68.2 1.5 %collective-permute-start.16 = (bf16[32,4608]{1,0:T(8,128)(2,1)S(1)}, bf16[32,4608]{1,0:T(8,128)(2,1)S(1)}, u32[]{:S(2)}, u32[]{:S(2)}) collective-permute-start(bf16[32,4608]{1,0:T(8,128)(2,1)S(1)} %get-tuple-element.99), channel_id=1, source_target_pairs={{0,8},{4,12},{8,0},{12,4},{1,9},{5,13},{9,1},{13,5},{2,10},{6,14},... | collective-permute-start | bytes 884744 | tf_op jit(solution)/shard_map/ppermute | solution.py:139
  69.8 6.7 %gate_and_up.3 = (f32[32,4608]{1,0:T(8,128)S(1)}, f32[32,4608]{1,0:T(8,128)S(1)}, bf16[2,32,4608]{2,1,0:T(8,128)(2,1)S(1)}) custom-call(bf16[128,1792]{1,0:T(8,128)(2,1)S(1)} %bitcast.59, bf16[1792,4608]{1,0:T(8,128)(2,1)} %gate_ref.3, bf16[1792,4608]{1,0:T(8,128)(2,1)} %up_ref.3), custom_call_target="tpu_custom_call" | custom-call | tf_op jit(solution)/shard_map/gate_and_up/pallas_call | solution.py:236
  77.4 1.3 %collective-permute-start.17 = (bf16[32,2304]{1,0:T(8,128)(2,1)S(1)}, bf16[32,2304]{1,0:T(8,128)(2,1)S(1)}, u32[]{:S(2)}, u32[]{:S(2)}) collective-permute-start(bf16[32,2304]{1,0:T(8,128)(2,1)S(1)} %fusion.3), channel_id=1, source_target_pairs={{0,8},{4,12},{8,0},{12,4},{1,9},{5,13},{9,1},{13,5},{2,10},{6,14},... | collective-permute-start | bytes 442376 | tf_op jit(solution)/shard_map/ppermute | solution.py:363
  79.0 0.8 collective-permute-start.20
  79.8 4.4 %collective-permute-done.17 = bf16[32,2304]{1,0:T(8,128)(2,1)S(1)} collective-permute-done((bf16[32,2304]{1,0:T(8,128)(2,1)S(1)}, bf16[32,2304]{1,0:T(8,128)(2,1)S(1)}, u32[]{:S(2)}, u32[]{:S(2)}) %collective-permute-start.17) | collective-permute-done | bytes 147488 | tf_op jit(solution)/shard_map/ppermute | solution.py:363
  84.3 5.1 %collective-permute-done.20 = bf16[32,4608]{1,0:T(8,128)(2,1)S(1)} collective-permute-done((bf16[32,4608]{1,0:T(8,128)(2,1)S(1)}, bf16[32,4608]{1,0:T(8,128)(2,1)S(1)}, u32[]{:S(2)}, u32[]{:S(2)}) %collective-permute-start.20) | collective-permute-done | bytes 294944 | tf_op jit(solution)/shard_map/ppermute | solution.py:139
  90.4 4.5 %collective-permute-done.21 = bf16[32,2304]{1,0:T(8,128)(2,1)S(1)} collective-permute-done((bf16[32,2304]{1,0:T(8,128)(2,1)S(1)}, bf16[32,2304]{1,0:T(8,128)(2,1)S(1)}, u32[]{:S(2)}, u32[]{:S(2)}) %collective-permute-start.21) | collective-permute-done | bytes 147488 | tf_op jit(solution)/shard_map/ppermute | solution.py:363
  95.1 1.5 %collective-permute-done.22 = bf16[2,32,2304]{2,1,0:T(8,128)(2,1)S(1)} collective-permute-done((bf16[2,32,2304]{2,1,0:T(8,128)(2,1)S(1)}, bf16[2,32,2304]{2,1,0:T(8,128)(2,1)S(1)}, u32[]{:S(2)}, u32[]{:S(2)}) %collective-permute-start.22) | collective-permute-done | bytes 294944 | tf_op jit(solution)/shard_map/ppermute | solution.py:367
  96.7 2.4 %down_project.1 = (f32[32,1792]{1,0:T(8,128)S(1)}, f32[32,1792]{1,0:T(8,128)S(1)}, bf16[2,32,1792]{2,1,0:T(8,128)(2,1)S(1)}) custom-call(s32[1]{0:T(128)} %bitcast.at_ref, bf16[128,2304]{1,0:T(8,128)(2,1)S(1)} %bitcast.60, bf16[128,2304]{1,0:T(8,128)(2,1)S(1)} %bitcast.61, bf16[4608,1792]{1,0:T(8,128)(2,1)S(1)} %bitcast.57), custom_call_target="tpu_custom_call" | custom-call | tf_op jit(solution)/shard_map/down_project/pallas_call | solution.py:284
  99.8 3.0 %collective-permute-start.24 = (bf16[32,1792]{1,0:T(8,128)(2,1)S(1)}, bf16[32,1792]{1,0:T(8,128)(2,1)S(1)}, u32[]{:S(2)}, u32[]{:S(2)}) collective-permute-start(bf16[32,1792]{1,0:T(8,128)(2,1)S(1)} %get-tuple-element.109), channel_id=1, source_target_pairs={{0,3},{1,2},{2,1},{3,0},{4,7},{5,6},{6,5},{7,4},{8,11},{9,10},{10,... | collective-permute-start | bytes 344072 | tf_op jit(solution)/shard_map/ppermute | solution.py:320
  104.2 1.0 select_select_fusion
  105.2 5.9 %collective-permute-done.23 = bf16[32,1792]{1,0:T(8,128)(2,1)S(1)} collective-permute-done((bf16[32,1792]{1,0:T(8,128)(2,1)S(1)}, bf16[32,1792]{1,0:T(8,128)(2,1)S(1)}, u32[]{:S(2)}, u32[]{:S(2)}) %collective-permute-start.23) | collective-permute-done | bytes 114720 | tf_op jit(solution)/shard_map/ppermute | solution.py:320
  (108 shorter events, 13.8 us)
Async XLA Ops:
  2.9 5.5 %collective-permute-start.2 = (bf16[8,4608]{1,0:T(8,128)(2,1)S(1)}, bf16[8,4608]{1,0:T(8,128)(2,1)S(1)}, u32[]{:S(2)}, u32[]{:S(2)}) collective-permute-start(bf16[8,4608]{1,0:T(8,128)(2,1)S(1)} %get-tuple-element.105), channel_id=1, source_target_pairs={{0,4},{4,0},{8,12},{12,8},{1,5},{5,1},{9,13},{13,9},{2,6},{6,2},{1... | collective-permute-start | bytes 221192 | tf_op jit(solution)/shard_map/ppermute | solution.py:440
  3.4 5.2 %collective-permute-start.1 = (bf16[8,4608]{1,0:T(8,128)(2,1)S(1)}, bf16[8,4608]{1,0:T(8,128)(2,1)S(1)}, u32[]{:S(2)}, u32[]{:S(2)}) collective-permute-start(bf16[8,4608]{1,0:T(8,128)(2,1)S(1)} %get-tuple-element.106), channel_id=1, source_target_pairs={{0,12},{4,8},{8,4},{12,0},{1,13},{5,9},{9,5},{13,1},{2,14},{6,10},... | collective-permute-start | bytes 221192 | tf_op jit(solution)/shard_map/ppermute | solution.py:440
  6.1 4.4 %collective-permute-start = (bf16[8,4608]{1,0:T(8,128)(2,1)S(1)}, bf16[8,4608]{1,0:T(8,128)(2,1)S(1)}, u32[]{:S(2)}, u32[]{:S(2)}) collective-permute-start(bf16[8,4608]{1,0:T(8,128)(2,1)S(1)} %get-tuple-element.107), channel_id=1, source_target_pairs={{0,8},{4,12},{8,0},{12,4},{1,9},{5,13},{9,1},{13,5},{2,10},{6,14},... | collective-permute-start | bytes 221192 | tf_op jit(solution)/shard_map/ppermute | solution.py:440
  15.7 7.8 %collective-permute-start.3 = (bf16[32,4096]{1,0:T(8,128)(2,1)S(1)}, bf16[32,4096]{1,0:T(8,128)(2,1)S(1)}, u32[]{:S(2)}, u32[]{:S(2)}) collective-permute-start(bf16[32,4096]{1,0:T(8,128)(2,1)S(1)} %get-tuple-element.57.refs_0_), channel_id=1, source_target_pairs={{0,8},{4,12},{8,0},{12,4},{1,9},{5,13},{9,1},{13,5},{2,10},{6,14},... | collective-permute-start | bytes 786440 | tf_op jit(solution)/shard_map/ppermute | solution.py:468
  18.3 5.3 %collective-permute-start.4 = (bf16[32,4096]{1,0:T(8,128)(2,1)S(1)}, bf16[32,4096]{1,0:T(8,128)(2,1)S(1)}, u32[]{:S(2)}, u32[]{:S(2)}) collective-permute-start(bf16[32,4096]{1,0:T(8,128)(2,1)S(1)} %get-tuple-element.57.refs_0_), channel_id=1, source_target_pairs={{0,4},{4,0},{8,12},{12,8},{1,5},{5,1},{9,13},{13,9},{2,6},{6,2},{1... | collective-permute-start | bytes 786440 | tf_op jit(solution)/shard_map/ppermute | solution.py:469
  23.5 1.5 %collective-permute-start.5 = (bf16[32,4096]{1,0:T(8,128)(2,1)S(1)}, bf16[32,4096]{1,0:T(8,128)(2,1)S(1)}, u32[]{:S(2)}, u32[]{:S(2)}) collective-permute-start(bf16[32,4096]{1,0:T(8,128)(2,1)S(1)} %collective-permute-done.3.refs_1_), channel_id=1, source_target_pairs={{0,4},{4,0},{8,12},{12,8},{1,5},{5,1},{9,13},{13,9},{2,6},{6,2},{1... | collective-permute-start | bytes 786440 | tf_op jit(solution)/shard_map/ppermute | solution.py:470
  30.9 11.9 %collective-permute-start.6 = (bf16[32,1792]{1,0:T(8,128)(2,1)S(1)}, bf16[32,1792]{1,0:T(8,128)(2,1)S(1)}, u32[]{:S(2)}, u32[]{:S(2)}) collective-permute-start(bf16[32,1792]{1,0:T(8,128)(2,1)S(1)} %convert_element_type.112), channel_id=1, source_target_pairs={{0,2},{1,3},{2,0},{3,1},{4,6},{5,7},{6,4},{7,5},{8,10},{9,11},{10,... | collective-permute-start | bytes 344072 | tf_op jit(solution)/shard_map/ppermute | solution.py:320
  33.8 9.0 %collective-permute-start.7 = (bf16[32,1792]{1,0:T(8,128)(2,1)S(1)}, bf16[32,1792]{1,0:T(8,128)(2,1)S(1)}, u32[]{:S(2)}, u32[]{:S(2)}) collective-permute-start(bf16[32,1792]{1,0:T(8,128)(2,1)S(1)} %get-tuple-element.111), channel_id=1, source_target_pairs={{0,3},{1,2},{2,1},{3,0},{4,7},{5,6},{6,5},{7,4},{8,11},{9,10},{10,... | collective-permute-start | bytes 344072 | tf_op jit(solution)/shard_map/ppermute | solution.py:320
  35.1 8.4 %collective-permute-start.8 = (bf16[32,1792]{1,0:T(8,128)(2,1)S(1)}, bf16[32,1792]{1,0:T(8,128)(2,1)S(1)}, u32[]{:S(2)}, u32[]{:S(2)}) collective-permute-start(bf16[32,1792]{1,0:T(8,128)(2,1)S(1)} %get-tuple-element.112), channel_id=1, source_target_pairs={{0,1},{1,0},{2,3},{3,2},{4,5},{5,4},{6,7},{7,6},{8,9},{9,8},{10,11... | collective-permute-start | bytes 344072 | tf_op jit(solution)/shard_map/ppermute | solution.py:320
  43.6 7.2 %collective-permute-start.11 = (bf16[32,1792]{1,0:T(8,128)(2,1)S(1)}, bf16[32,1792]{1,0:T(8,128)(2,1)S(1)}, u32[]{:S(2)}, u32[]{:S(2)}) collective-permute-start(bf16[32,1792]{1,0:T(8,128)(2,1)S(1)} %add_convert_fusion.1), channel_id=1, source_target_pairs={{0,3},{1,2},{2,1},{3,0},{4,7},{5,6},{6,5},{7,4},{8,11},{9,10},{10,... | collective-permute-start | bytes 344072 | tf_op jit(solution)/shard_map/ppermute | solution.py:343
  47.2 9.9 %collective-permute-start.10 = (bf16[32,1792]{1,0:T(8,128)(2,1)S(1)}, bf16[32,1792]{1,0:T(8,128)(2,1)S(1)}, u32[]{:S(2)}, u32[]{:S(2)}) collective-permute-start(bf16[32,1792]{1,0:T(8,128)(2,1)S(1)} %add_convert_fusion.1), channel_id=1, source_target_pairs={{0,2},{1,3},{2,0},{3,1},{4,6},{5,7},{6,4},{7,5},{8,10},{9,11},{10,... | collective-permute-start | bytes 344072 | tf_op jit(solution)/shard_map/ppermute | solution.py:343
  47.5 9.6 %collective-permute-start.9 = (bf16[32,1792]{1,0:T(8,128)(2,1)S(1)}, bf16[32,1792]{1,0:T(8,128)(2,1)S(1)}, u32[]{:S(2)}, u32[]{:S(2)}) collective-permute-start(bf16[32,1792]{1,0:T(8,128)(2,1)S(1)} %add_convert_fusion.1), channel_id=1, source_target_pairs={{0,1},{1,0},{2,3},{3,2},{4,5},{5,4},{6,7},{7,6},{8,9},{9,8},{10,11... | collective-permute-start | bytes 344072 | tf_op jit(solution)/shard_map/ppermute | solution.py:343
  48.0 9.1 %collective-permute-start.13 = (bf16[1,256,512]{2,1,0:T(8,128)(2,1)S(1)}, bf16[1,256,512]{2,1,0:T(8,128)(2,1)S(1)}, u32[]{:S(2)}, u32[]{:S(2)}) collective-permute-start(bf16[1,256,512]{2,1,0:T(8,128)(2,1)S(1)} %get-tuple-element.67), channel_id=1, source_target_pairs={{0,8},{4,12},{8,0},{12,4},{1,9},{5,13},{9,1},{13,5},{2,10},{6,14},... | collective-permute-start | bytes 786440 | tf_op jit(solution)/shard_map/ppermute | solution.py:338
  49.6 7.6 %collective-permute-start.12 = (bf16[1,256,512]{2,1,0:T(8,128)(2,1)S(1)}, bf16[1,256,512]{2,1,0:T(8,128)(2,1)S(1)}, u32[]{:S(2)}, u32[]{:S(2)}) collective-permute-start(bf16[1,256,512]{2,1,0:T(8,128)(2,1)S(1)} %get-tuple-element.66), channel_id=1, source_target_pairs={{0,4},{4,0},{8,12},{12,8},{1,5},{5,1},{9,13},{13,9},{2,6},{6,2},{1... | collective-permute-start | bytes 786440 | tf_op jit(solution)/shard_map/ppermute | solution.py:341
  57.2 8.6 %collective-permute-start.14 = (bf16[1,256,512]{2,1,0:T(8,128)(2,1)S(1)}, bf16[1,256,512]{2,1,0:T(8,128)(2,1)S(1)}, u32[]{:S(2)}, u32[]{:S(2)}) collective-permute-start(bf16[1,256,512]{2,1,0:T(8,128)(2,1)S(1)} %get-tuple-element.73), channel_id=1, source_target_pairs={{0,12},{4,8},{8,4},{12,0},{1,13},{5,9},{9,5},{13,1},{2,14},{6,10},... | collective-permute-start | bytes 786440 | tf_op jit(solution)/shard_map/ppermute | solution.py:347
  65.8 2.3 %collective-permute-start.15 = (bf16[2,32,4608]{2,1,0:T(8,128)(2,1)S(1)}, bf16[2,32,4608]{2,1,0:T(8,128)(2,1)S(1)}, u32[]{:S(2)}, u32[]{:S(2)}) collective-permute-start(bf16[2,32,4608]{2,1,0:T(8,128)(2,1)S(1)} %get-tuple-element.74), channel_id=1, source_target_pairs={{0,4},{4,0},{8,12},{12,8},{1,5},{5,1},{9,13},{13,9},{2,6},{6,2},{1... | collective-permute-start | bytes 1769480 | tf_op jit(solution)/shard_map/ppermute | solution.py:134
  68.2 9.1 %collective-permute-start.16 = (bf16[32,4608]{1,0:T(8,128)(2,1)S(1)}, bf16[32,4608]{1,0:T(8,128)(2,1)S(1)}, u32[]{:S(2)}, u32[]{:S(2)}) collective-permute-start(bf16[32,4608]{1,0:T(8,128)(2,1)S(1)} %get-tuple-element.99), channel_id=1, source_target_pairs={{0,8},{4,12},{8,0},{12,4},{1,9},{5,13},{9,1},{13,5},{2,10},{6,14},... | collective-permute-start | bytes 884744 | tf_op jit(solution)/shard_map/ppermute | solution.py:139
  69.8 26.9 %slice-start.1 = ((s8[16515072]{0:T(1024)(128)(4,1)}), s8[4194304]{0:T(1024)(128)(4,1)S(1)}, s32[]{:S(2)}) async-start(s8[16515072]{0:T(1024)(128)(4,1)} %bitcast.56), calls=%async_computation.1 | async-start | bytes 8388608
  69.8 26.9 %slice-start.2 = ((s8[16515072]{0:T(1024)(128)(4,1)}), s8[4194304]{0:T(1024)(128)(4,1)S(1)}, s32[]{:S(2)}) async-start(s8[16515072]{0:T(1024)(128)(4,1)} %bitcast.56), calls=%async_computation.2 | async-start | bytes 8388608
  76.5 27.0 %copy-start.3 = (bf16[1,256,512]{2,1,0:T(8,128)(2,1)S(1)}, bf16[1,256,512]{2,1,0:T(8,128)(2,1)}, u32[]{:S(2)}) copy-start(bf16[1,256,512]{2,1,0:T(8,128)(2,1)} %copy-done.2) | copy-start | bytes 786436
  76.5 27.0 %copy-start.5 = (bf16[1,256,512]{2,1,0:T(8,128)(2,1)S(1)}, bf16[1,256,512]{2,1,0:T(8,128)(2,1)}, u32[]{:S(2)}) copy-start(bf16[1,256,512]{2,1,0:T(8,128)(2,1)} %copy-done.4) | copy-start | bytes 786436
  76.5 26.9 %copy-start.7 = (bf16[1,256,512]{2,1,0:T(8,128)(2,1)S(1)}, bf16[1,256,512]{2,1,0:T(8,128)(2,1)}, u32[]{:S(2)}) copy-start(bf16[1,256,512]{2,1,0:T(8,128)(2,1)} %copy-done.6) | copy-start | bytes 786436
  76.5 2.3 %collective-permute-start.18 = (bf16[2,32,4608]{2,1,0:T(8,128)(2,1)S(1)}, bf16[2,32,4608]{2,1,0:T(8,128)(2,1)S(1)}, u32[]{:S(2)}, u32[]{:S(2)}) collective-permute-start(bf16[2,32,4608]{2,1,0:T(8,128)(2,1)S(1)} %get-tuple-element.78), channel_id=1, source_target_pairs={{0,4},{4,0},{8,12},{12,8},{1,5},{5,1},{9,13},{13,9},{2,6},{6,2},{1... | collective-permute-start | bytes 1769480 | tf_op jit(solution)/shard_map/ppermute | solution.py:134
  77.4 6.8 %collective-permute-start.17 = (bf16[32,2304]{1,0:T(8,128)(2,1)S(1)}, bf16[32,2304]{1,0:T(8,128)(2,1)S(1)}, u32[]{:S(2)}, u32[]{:S(2)}) collective-permute-start(bf16[32,2304]{1,0:T(8,128)(2,1)S(1)} %fusion.3), channel_id=1, source_target_pairs={{0,8},{4,12},{8,0},{12,4},{1,9},{5,13},{9,1},{13,5},{2,10},{6,14},... | collective-permute-start | bytes 442376 | tf_op jit(solution)/shard_map/ppermute | solution.py:363
  78.8 33.6 %copy-start.1 = (bf16[128,1792]{1,0:T(8,128)(2,1)S(1)}, bf16[128,1792]{1,0:T(8,128)(2,1)}, u32[]{:S(2)}) copy-start(bf16[128,1792]{1,0:T(8,128)(2,1)} %param.17) | copy-start | bytes 1376260
  79.0 10.4 %collective-permute-start.20 = (bf16[32,4608]{1,0:T(8,128)(2,1)S(1)}, bf16[32,4608]{1,0:T(8,128)(2,1)S(1)}, u32[]{:S(2)}, u32[]{:S(2)}) collective-permute-start(bf16[32,4608]{1,0:T(8,128)(2,1)S(1)} %get-tuple-element.98), channel_id=1, source_target_pairs={{0,8},{4,12},{8,0},{12,4},{1,9},{5,13},{9,1},{13,5},{2,10},{6,14},... | collective-permute-start | bytes 884744 | tf_op jit(solution)/shard_map/ppermute | solution.py:139
  84.2 6.1 %collective-permute-start.19 = (bf16[2,32,2304]{2,1,0:T(8,128)(2,1)S(1)}, bf16[2,32,2304]{2,1,0:T(8,128)(2,1)S(1)}, u32[]{:S(2)}, u32[]{:S(2)}) collective-permute-start(bf16[2,32,2304]{2,1,0:T(8,128)(2,1)S(1)} %pad_maximum_fusion.4), channel_id=1, source_target_pairs={{0,4},{4,0},{8,12},{12,8},{1,5},{5,1},{9,13},{13,9},{2,6},{6,2},{1... | collective-permute-start | bytes 884744 | tf_op jit(solution)/shard_map/ppermute | solution.py:367
  89.7 5.2 %collective-permute-start.21 = (bf16[32,2304]{1,0:T(8,128)(2,1)S(1)}, bf16[32,2304]{1,0:T(8,128)(2,1)S(1)}, u32[]{:S(2)}, u32[]{:S(2)}) collective-permute-start(bf16[32,2304]{1,0:T(8,128)(2,1)S(1)} %fusion.2), channel_id=1, source_target_pairs={{0,8},{4,12},{8,0},{12,4},{1,9},{5,13},{9,1},{13,5},{2,10},{6,14},... | collective-permute-start | bytes 442376 | tf_op jit(solution)/shard_map/ppermute | solution.py:363
  94.9 1.6 %collective-permute-start.22 = (bf16[2,32,2304]{2,1,0:T(8,128)(2,1)S(1)}, bf16[2,32,2304]{2,1,0:T(8,128)(2,1)S(1)}, u32[]{:S(2)}, u32[]{:S(2)}) collective-permute-start(bf16[2,32,2304]{2,1,0:T(8,128)(2,1)S(1)} %pad_maximum_fusion.5), channel_id=1, source_target_pairs={{0,4},{4,0},{8,12},{12,8},{1,5},{5,1},{9,13},{13,9},{2,6},{6,2},{1... | collective-permute-start | bytes 884744 | tf_op jit(solution)/shard_map/ppermute | solution.py:367
  99.2 11.9 %collective-permute-start.23 = (bf16[32,1792]{1,0:T(8,128)(2,1)S(1)}, bf16[32,1792]{1,0:T(8,128)(2,1)S(1)}, u32[]{:S(2)}, u32[]{:S(2)}) collective-permute-start(bf16[32,1792]{1,0:T(8,128)(2,1)S(1)} %convert_element_type.133), channel_id=1, source_target_pairs={{0,2},{1,3},{2,0},{3,1},{4,6},{5,7},{6,4},{7,5},{8,10},{9,11},{10,... | collective-permute-start | bytes 344072 | tf_op jit(solution)/shard_map/ppermute | solution.py:320
  99.8 11.3 %collective-permute-start.24 = (bf16[32,1792]{1,0:T(8,128)(2,1)S(1)}, bf16[32,1792]{1,0:T(8,128)(2,1)S(1)}, u32[]{:S(2)}, u32[]{:S(2)}) collective-permute-start(bf16[32,1792]{1,0:T(8,128)(2,1)S(1)} %get-tuple-element.109), channel_id=1, source_target_pairs={{0,3},{1,2},{2,1},{3,0},{4,7},{5,6},{6,5},{7,4},{8,11},{9,10},{10,... | collective-permute-start | bytes 344072 | tf_op jit(solution)/shard_map/ppermute | solution.py:320
  102.8 8.9 %collective-permute-start.25 = (bf16[32,1792]{1,0:T(8,128)(2,1)S(1)}, bf16[32,1792]{1,0:T(8,128)(2,1)S(1)}, u32[]{:S(2)}, u32[]{:S(2)}) collective-permute-start(bf16[32,1792]{1,0:T(8,128)(2,1)S(1)} %get-tuple-element.110), channel_id=1, source_target_pairs={{0,1},{1,0},{2,3},{3,2},{4,5},{5,4},{6,7},{7,6},{8,9},{9,8},{10,11... | collective-permute-start | bytes 344072 | tf_op jit(solution)/shard_map/ppermute | solution.py:320
  (7 other events, 80.2 us)

commit v5 on v4

--- a/solution.py
+++ b/solution.py
@@ -143,12 +143,6 @@
     return lax.optimization_barrier(total) + far.astype(jnp.float32)
 
 
-def spread(x, axis):
-    half = jnp.stack([x, lax.ppermute(x, axis, swap_perm(4, 2))])
-    other = lax.ppermute(half, axis, swap_perm(4, 1))
-    return jnp.stack([half[0], other[0], half[1], other[1]])
-
-
 def split_store(block, columns, near_ref, far_ref, sent_ref):
     share = near_ref.shape[0]
     near_ref[:, columns] = block[:share].astype(near_ref.dtype)
@@ -293,27 +287,6 @@
     return [outs[3 * p : 3 * p + 3] for p in range(PARTS)]
 
 
-def sum_first(sums):
-    near, leaving = [], []
-    for at_hand, far, sent in sums:
-        came = lax.ppermute(sent, "ffn", swap_perm(4, 1))
-        if leaving:
-            came = tie(came, leaving[-1])
-        near.append((at_hand, came[0]))
-        leaving.append((far + came[1].astype(jnp.float32)).astype(jnp.bfloat16))
-    return near, leaving
-
-
-def sum_last(leaving, own, near):
-    outs = []
-    for p, last in enumerate(leaving):
-        far = lax.ppermute(last, "ffn", swap_perm(4, 2))
-        far = tie(far, outs[-1] if outs else leaving[-1])
-        base = own[p].astype(jnp.float32) + near[p][0] + near[p][1].astype(jnp.float32)
-        outs.append((lax.optimization_barrier(base) + far.astype(jnp.float32)).astype(jnp.bfloat16))
-    return outs
-
-
 def sum_direct(near, far, sent, own):
     far = far.astype(jnp.bfloat16)
     came = [
@@ -335,23 +308,23 @@
     mine = lax.dynamic_slice_in_dim(residual, turn * share, share, 0)
     pieces, mine, pages = lax.optimization_barrier((pieces, mine, pages))
     landed = list(pages)
+    near, far, sent = project(row_picker, pieces, w_out)
+    sent, pages = lax.optimization_barrier((sent, pages))
     landed[2] = lax.ppermute(pages[2], "attn", swap_perm(4, 2))
-    near, far, sent = project(row_picker, pieces, w_out)
-    sent, pages[1] = lax.optimization_barrier((sent, pages[1]))
     landed[1] = lax.ppermute(pages[1], "attn", swap_perm(4, 1))
     kept = sum_direct(near, far, sent, mine)
+    kept, landed[1], landed[2], pages[3] = lax.optimization_barrier(
+        (kept, landed[1], landed[2], pages[3])
+    )
+    landed[3] = lax.ppermute(pages[3], "attn", swap_perm(4, 3))
     came = {d: lax.ppermute(kept, "ffn", swap_perm(4, d)) for d in (2, 3, 1)}
     mixed = jnp.stack([kept, came[1], came[2], came[3]])
-    mixed, landed[1], landed[2] = lax.optimization_barrier((mixed, landed[1], landed[2]))
-    mixed, pages[3] = lax.optimization_barrier((mixed, pages[3]))
-    landed[3] = lax.ppermute(pages[3], "attn", swap_perm(4, 3))
+    mixed, landed[3] = lax.optimization_barrier((mixed, landed[3]))
     rows = mixed.reshape(count, columns)
 
     stages = []
     for c in range(CHUNKS):
         near, far, sent = gate_and_up(rows, w_gate, w_up, c * step, step)
-        if c == 0:
-            sent, landed[3] = lax.optimization_barrier((sent, landed[3]))
         came, leaving = fold_first(sent, far, "attn")
         rows = tie(rows, leaving)
         stages.append((near, came, leaving))

time: 113 us -> 112 us (level)
  starting transfers between devices: 25.2 us -> 24 us
    ppermute x3, waiting for transfers between devices: 7.49 us -> 9.49 us  [paired_rows(): came = {d: lax.ppermute(kept, 'ffn', swap_perm(4, d)) for d in (2, 3, 1)}]
    ppermute x1, waiting for transfers between devices: 1.21 us -> 0.01 us  [paired_rows(): landed[3] = lax.ppermute(pages[3], 'attn', swap_perm(4, 3))]
  transfers between devices with their start and end apart: 26 -> 26, of which waited for: 16 -> 17; matrix products, arithmetic and copies ran while one was open for 7% -> 7% of each run, Pallas kernels for 12% -> 6%
where the time goes in v5:
time: 112 us
  waiting for transfers between devices  48.6 us (43%)
  Pallas kernels  26.7 us (24%)
  starting transfers between devices  24 us (21%)
  other arithmetic  5.91 us (5%)
  local copies, waits for them, and re-layouts  4.41 us (4%)
  matrix products  1.19 us (1%)
    ppermute x6, waiting for transfers between devices, sum_direct(): lax.ppermute(x, 'ffn', swap_perm(4, d))  13.7 us
    pallas_call x2, Pallas kernels, gate_and_up(): pl.pallas_call(functools.partial(gate_kernel, start=start), out_shape=spl...  13.3 us
    ppermute x3, waiting for transfers between devices, paired_rows(): came = {d: lax.ppermute(kept, 'ffn', swap_perm(4, d)) for d in (2, 3, 1)}  9.49 us
    ppermute x2, waiting for transfers between devices, paired_rows(): across = lax.ppermute(quarter, 'attn', swap_perm(4, 2))  8.62 us
    ppermute x6, starting transfers between devices, sum_direct(): lax.ppermute(x, 'ffn', swap_perm(4, d))  8.15 us
    pallas_call x1, Pallas kernels, project(): pl.pallas_call(project_kernel, out_shape=split_shapes(picker.shape[0] //...  5.75 us
    ppermute x2, waiting for transfers between devices, fold_last(): far = lax.ppermute(leaving, axis, swap_perm(4, 2))  5.73 us
    pallas_call x1, Pallas kernels, attend(): pl.pallas_call(functools.partial(attention_kernel, distances=distances),...  5.25 us
  transfers between devices with their start and end apart: 26, of which 17 were waited for; matrix products, arithmetic and copies ran while one was open for 7% of the time, Pallas kernels for 6%

profile of v5, /device:TPU:0, one launch (start us, length us, event | category | flops | bytes accessed | tf_op | source)
XLA Modules:
  0.0 111.9 jit_solution(15481541595191052106)
XLA Ops:
  1.7 1.2 %convolution_convert_fusion = bf16[32,4608]{1,0:T(8,128)(2,1)S(1)} fusion(bf16[32,512]{1,0:T(8,128)(2,1)} %param.12, bf16[32,4096]{1,0:T(8,128)(2,1)} %param.11, s32[32]{0:T(128)S(1)} %fusion.20), kind=kOutput, calls=%fused_computation.2 | convolution fusion | flops 10175488 | bytes 589952 | tf_op jit(solution)/shard_map/dot_general | solution.py:405
  3.4 2.6 %collective-permute-start.1 = (bf16[8,4608]{1,0:T(8,128)(2,1)S(1)}, bf16[8,4608]{1,0:T(8,128)(2,1)S(1)}, u32[]{:S(2)}, u32[]{:S(2)}) collective-permute-start(bf16[8,4608]{1,0:T(8,128)(2,1)S(1)} %get-tuple-element.108), channel_id=1, source_target_pairs={{0,12},{4,8},{8,4},{12,0},{1,13},{5,9},{9,5},{13,1},{2,14},{6,10},... | collective-permute-start | bytes 221192 | tf_op jit(solution)/shard_map/ppermute | solution.py:413
  8.7 1.8 %collective-permute-done.refs_1_ = bf16[8,4608]{1,0:T(8,128)(2,1)S(1)} collective-permute-done((bf16[8,4608]{1,0:T(8,128)(2,1)S(1)}, bf16[8,4608]{1,0:T(8,128)(2,1)S(1)}, u32[]{:S(2)}, u32[]{:S(2)}) %collective-permute-start) | collective-permute-done | bytes 73760 | tf_op jit(solution)/shard_map/ppermute | solution.py:413
  10.5 5.3 %attention.1 = (bf16[32,4096]{1,0:T(8,128)(2,1)}, bf16[32,4096]{1,0:T(8,128)(2,1)S(1)}, bf16[1,256,512]{2,1,0:T(8,128)(2,1)S(1)}, bf16[1,256,512]{2,1,0:T(8,128)...) custom-call(s32[147]{0:T(256)S(1)} %pad_add_fusion.number_ref, ...), custom_call_target="tpu_custom_call" | custom-call | tf_op jit(solution)/shard_map/attention/pallas_call | solution.py:106
  15.7 1.8 %collective-permute-start.3 = (bf16[32,4096]{1,0:T(8,128)(2,1)S(1)}, bf16[32,4096]{1,0:T(8,128)(2,1)S(1)}, u32[]{:S(2)}, u32[]{:S(2)}) collective-permute-start(bf16[32,4096]{1,0:T(8,128)(2,1)S(1)} %get-tuple-element.58.refs_0_), channel_id=1, source_target_pairs={{0,8},{4,12},{8,0},{12,4},{1,9},{5,13},{9,1},{13,5},{2,10},{6,14},... | collective-permute-start | bytes 786440 | tf_op jit(solution)/shard_map/ppermute | solution.py:441
  18.3 5.2 %collective-permute-done.3.refs_1_ = bf16[32,4096]{1,0:T(8,128)(2,1)S(1)} collective-permute-done((bf16[32,4096]{1,0:T(8,128)(2,1)S(1)}, bf16[32,4096]{1,0:T(8,128)(2,1)S(1)}, u32[]{:S(2)}, u32[]{:S(2)}) %collective-permute-start.3) | collective-permute-done | bytes 262176 | tf_op jit(solution)/shard_map/ppermute | solution.py:441
  23.7 1.4 %collective-permute-done.5.refs_3_ = bf16[32,4096]{1,0:T(8,128)(2,1)S(1)} collective-permute-done((bf16[32,4096]{1,0:T(8,128)(2,1)S(1)}, bf16[32,4096]{1,0:T(8,128)(2,1)S(1)}, u32[]{:S(2)}, u32[]{:S(2)}) %collective-permute-start.5) | collective-permute-done | bytes 262176 | tf_op jit(solution)/shard_map/ppermute | solution.py:443
  25.1 5.8 %project.1 = (f32[32,1792]{1,0:T(8,128)S(1)}, f32[32,1792]{1,0:T(8,128)S(1)}, bf16[2,32,1792]{2,1,0:T(8,128)(2,1)S(1)}) custom-call(bf16[128,128]{1,0:T(8,128)(2,1)S(1)} %fusion.7.picker_ref, bf16[32,4096]{1,0:T(8,128)(2,1)S(1)} %get-tuple-element.58.refs_0_, bf16[32,4096]{1,0:T(8,128)(2,1)S(1)} %collective-permute-done.3.refs_1_, ...), custom_call_target="tpu_custom_call" | custom-call | tf_op jit(solution)/shard_map/project/pallas_call | solution.py:192
  30.9 2.9 %collective-permute-start.6 = (bf16[32,1792]{1,0:T(8,128)(2,1)S(1)}, bf16[32,1792]{1,0:T(8,128)(2,1)S(1)}, u32[]{:S(2)}, u32[]{:S(2)}) collective-permute-start(bf16[32,1792]{1,0:T(8,128)(2,1)S(1)} %convert_element_type.112), channel_id=1, source_target_pairs={{0,2},{1,3},{2,0},{3,1},{4,6},{5,7},{6,4},{7,5},{8,10},{9,11},{10,... | collective-permute-start | bytes 344072 | tf_op jit(solution)/shard_map/ppermute | solution.py:293
  33.8 1.4 %collective-permute-start.7 = (bf16[32,1792]{1,0:T(8,128)(2,1)S(1)}, bf16[32,1792]{1,0:T(8,128)(2,1)S(1)}, u32[]{:S(2)}, u32[]{:S(2)}) collective-permute-start(bf16[32,1792]{1,0:T(8,128)(2,1)S(1)} %get-tuple-element.113), channel_id=1, source_target_pairs={{0,3},{1,2},{2,1},{3,0},{4,7},{5,6},{6,5},{7,4},{8,11},{9,10},{10,... | collective-permute-start | bytes 344072 | tf_op jit(solution)/shard_map/ppermute | solution.py:293
  35.5 1.5 %collective-permute-start.10 = (bf16[1,256,512]{2,1,0:T(8,128)(2,1)S(1)}, bf16[1,256,512]{2,1,0:T(8,128)(2,1)S(1)}, u32[]{:S(2)}, u32[]{:S(2)}) collective-permute-start(bf16[1,256,512]{2,1,0:T(8,128)(2,1)S(1)} %get-tuple-element.71), channel_id=1, source_target_pairs={{0,8},{4,12},{8,0},{12,4},{1,9},{5,13},{9,1},{13,5},{2,10},{6,14},... | collective-permute-start | bytes 786440 | tf_op jit(solution)/shard_map/ppermute | solution.py:313
  37.0 5.7 %collective-permute-done.6 = bf16[32,1792]{1,0:T(8,128)(2,1)S(1)} collective-permute-done((bf16[32,1792]{1,0:T(8,128)(2,1)S(1)}, bf16[32,1792]{1,0:T(8,128)(2,1)S(1)}, u32[]{:S(2)}, u32[]{:S(2)}) %collective-permute-start.6) | collective-permute-done | bytes 114720 | tf_op jit(solution)/shard_map/ppermute | solution.py:293
  44.2 3.0 %collective-permute-start.13 = (bf16[32,1792]{1,0:T(8,128)(2,1)S(1)}, bf16[32,1792]{1,0:T(8,128)(2,1)S(1)}, u32[]{:S(2)}, u32[]{:S(2)}) collective-permute-start(bf16[32,1792]{1,0:T(8,128)(2,1)S(1)} %add_convert_fusion.1), channel_id=1, source_target_pairs={{0,3},{1,2},{2,1},{3,0},{4,7},{5,6},{6,5},{7,4},{8,11},{9,10},{10,... | collective-permute-start | bytes 344072 | tf_op jit(solution)/shard_map/ppermute | solution.py:320
  47.6 1.0 collective-permute-start.11
  48.6 2.4 %collective-permute-done.13 = bf16[32,1792]{1,0:T(8,128)(2,1)S(1)} collective-permute-done((bf16[32,1792]{1,0:T(8,128)(2,1)S(1)}, bf16[32,1792]{1,0:T(8,128)(2,1)S(1)}, u32[]{:S(2)}, u32[]{:S(2)}) %collective-permute-start.13) | collective-permute-done | bytes 114720 | tf_op jit(solution)/shard_map/ppermute | solution.py:320
  51.0 7.1 %collective-permute-done.12 = bf16[32,1792]{1,0:T(8,128)(2,1)S(1)} collective-permute-done((bf16[32,1792]{1,0:T(8,128)(2,1)S(1)}, bf16[32,1792]{1,0:T(8,128)(2,1)S(1)}, u32[]{:S(2)}, u32[]{:S(2)}) %collective-permute-start.12) | collective-permute-done | bytes 114720 | tf_op jit(solution)/shard_map/ppermute | solution.py:320
  58.9 6.6 %gate_and_up.2 = (f32[32,4608]{1,0:T(8,128)S(1)}, f32[32,4608]{1,0:T(8,128)S(1)}, bf16[2,32,4608]{2,1,0:T(8,128)(2,1)S(1)}) custom-call(bf16[128,1792]{1,0:T(8,128)(2,1)S(1)} %bitcast.58, bf16[1792,4608]{1,0:T(8,128)(2,1)} %gate_ref.3, bf16[1792,4608]{1,0:T(8,128)(2,1)} %up_ref.3), custom_call_target="tpu_custom_call" | custom-call | tf_op jit(solution)/shard_map/gate_and_up/pallas_call | solution.py:230
  66.3 0.9 iota_reduce_fusion
  67.6 1.5 %collective-permute-start.16 = (bf16[32,4608]{1,0:T(8,128)(2,1)S(1)}, bf16[32,4608]{1,0:T(8,128)(2,1)S(1)}, u32[]{:S(2)}, u32[]{:S(2)}) collective-permute-start(bf16[32,4608]{1,0:T(8,128)(2,1)S(1)} %get-tuple-element.101), channel_id=1, source_target_pairs={{0,8},{4,12},{8,0},{12,4},{1,9},{5,13},{9,1},{13,5},{2,10},{6,14},... | collective-permute-start | bytes 884744 | tf_op jit(solution)/shard_map/ppermute | solution.py:139
  69.3 6.7 %gate_and_up.3 = (f32[32,4608]{1,0:T(8,128)S(1)}, f32[32,4608]{1,0:T(8,128)S(1)}, bf16[2,32,4608]{2,1,0:T(8,128)(2,1)S(1)}) custom-call(bf16[128,1792]{1,0:T(8,128)(2,1)S(1)} %bitcast.59, bf16[1792,4608]{1,0:T(8,128)(2,1)} %gate_ref.3, bf16[1792,4608]{1,0:T(8,128)(2,1)} %up_ref.3), custom_call_target="tpu_custom_call" | custom-call | tf_op jit(solution)/shard_map/gate_and_up/pallas_call | solution.py:230
  76.9 1.5 %collective-permute-start.17 = (bf16[32,2304]{1,0:T(8,128)(2,1)S(1)}, bf16[32,2304]{1,0:T(8,128)(2,1)S(1)}, u32[]{:S(2)}, u32[]{:S(2)}) collective-permute-start(bf16[32,2304]{1,0:T(8,128)(2,1)S(1)} %fusion.3), channel_id=1, source_target_pairs={{0,8},{4,12},{8,0},{12,4},{1,9},{5,13},{9,1},{13,5},{2,10},{6,14},... | collective-permute-start | bytes 442376 | tf_op jit(solution)/shard_map/ppermute | solution.py:336
  79.3 4.4 %collective-permute-done.17 = bf16[32,2304]{1,0:T(8,128)(2,1)S(1)} collective-permute-done((bf16[32,2304]{1,0:T(8,128)(2,1)S(1)}, bf16[32,2304]{1,0:T(8,128)(2,1)S(1)}, u32[]{:S(2)}, u32[]{:S(2)}) %collective-permute-start.17) | collective-permute-done | bytes 147488 | tf_op jit(solution)/shard_map/ppermute | solution.py:336
  83.8 5.1 %collective-permute-done.20 = bf16[32,4608]{1,0:T(8,128)(2,1)S(1)} collective-permute-done((bf16[32,4608]{1,0:T(8,128)(2,1)S(1)}, bf16[32,4608]{1,0:T(8,128)(2,1)S(1)}, u32[]{:S(2)}, u32[]{:S(2)}) %collective-permute-start.20) | collective-permute-done | bytes 294944 | tf_op jit(solution)/shard_map/ppermute | solution.py:139
  89.2 0.9 collective-permute-start.21
  90.2 4.2 %collective-permute-done.21 = bf16[32,2304]{1,0:T(8,128)(2,1)S(1)} collective-permute-done((bf16[32,2304]{1,0:T(8,128)(2,1)S(1)}, bf16[32,2304]{1,0:T(8,128)(2,1)S(1)}, u32[]{:S(2)}, u32[]{:S(2)}) %collective-permute-start.21) | collective-permute-done | bytes 147488 | tf_op jit(solution)/shard_map/ppermute | solution.py:336
  94.6 1.5 %collective-permute-done.22 = bf16[2,32,2304]{2,1,0:T(8,128)(2,1)S(1)} collective-permute-done((bf16[2,32,2304]{2,1,0:T(8,128)(2,1)S(1)}, bf16[2,32,2304]{2,1,0:T(8,128)(2,1)S(1)}, u32[]{:S(2)}, u32[]{:S(2)}) %collective-permute-start.22) | collective-permute-done | bytes 294944 | tf_op jit(solution)/shard_map/ppermute | solution.py:340
  96.3 2.4 %down_project.1 = (f32[32,1792]{1,0:T(8,128)S(1)}, f32[32,1792]{1,0:T(8,128)S(1)}, bf16[2,32,1792]{2,1,0:T(8,128)(2,1)S(1)}) custom-call(s32[1]{0:T(128)} %bitcast.at_ref, bf16[128,2304]{1,0:T(8,128)(2,1)S(1)} %bitcast.60, bf16[128,2304]{1,0:T(8,128)(2,1)S(1)} %bitcast.61, bf16[4608,1792]{1,0:T(8,128)(2,1)S(1)} %bitcast.57), custom_call_target="tpu_custom_call" | custom-call | tf_op jit(solution)/shard_map/down_project/pallas_call | solution.py:278
  98.7 0.9 collective-permute-start.23
  99.6 2.0 %collective-permute-start.24 = (bf16[32,1792]{1,0:T(8,128)(2,1)S(1)}, bf16[32,1792]{1,0:T(8,128)(2,1)S(1)}, u32[]{:S(2)}, u32[]{:S(2)}) collective-permute-start(bf16[32,1792]{1,0:T(8,128)(2,1)S(1)} %get-tuple-element.111), channel_id=1, source_target_pairs={{0,3},{1,2},{2,1},{3,0},{4,7},{5,6},{6,5},{7,4},{8,11},{9,10},{10,... | collective-permute-start | bytes 344072 | tf_op jit(solution)/shard_map/ppermute | solution.py:293
  103.1 1.0 select_select_fusion
  104.1 5.9 %collective-permute-done.23 = bf16[32,1792]{1,0:T(8,128)(2,1)S(1)} collective-permute-done((bf16[32,1792]{1,0:T(8,128)(2,1)S(1)}, bf16[32,1792]{1,0:T(8,128)(2,1)S(1)}, u32[]{:S(2)}, u32[]{:S(2)}) %collective-permute-start.23) | collective-permute-done | bytes 114720 | tf_op jit(solution)/shard_map/ppermute | solution.py:293
  110.0 1.2 %collective-permute-done.25 = bf16[32,1792]{1,0:T(8,128)(2,1)S(1)} collective-permute-done((bf16[32,1792]{1,0:T(8,128)(2,1)S(1)}, bf16[32,1792]{1,0:T(8,128)(2,1)S(1)}, u32[]{:S(2)}, u32[]{:S(2)}) %collective-permute-start.25) | collective-permute-done | bytes 114720 | tf_op jit(solution)/shard_map/ppermute | solution.py:293
  (108 shorter events, 14.0 us)
Async XLA Ops:
  2.9 5.5 %collective-permute-start.2 = (bf16[8,4608]{1,0:T(8,128)(2,1)S(1)}, bf16[8,4608]{1,0:T(8,128)(2,1)S(1)}, u32[]{:S(2)}, u32[]{:S(2)}) collective-permute-start(bf16[8,4608]{1,0:T(8,128)(2,1)S(1)} %get-tuple-element.107), channel_id=1, source_target_pairs={{0,4},{4,0},{8,12},{12,8},{1,5},{5,1},{9,13},{13,9},{2,6},{6,2},{1... | collective-permute-start | bytes 221192 | tf_op jit(solution)/shard_map/ppermute | solution.py:413
  3.4 5.2 %collective-permute-start.1 = (bf16[8,4608]{1,0:T(8,128)(2,1)S(1)}, bf16[8,4608]{1,0:T(8,128)(2,1)S(1)}, u32[]{:S(2)}, u32[]{:S(2)}) collective-permute-start(bf16[8,4608]{1,0:T(8,128)(2,1)S(1)} %get-tuple-element.108), channel_id=1, source_target_pairs={{0,12},{4,8},{8,4},{12,0},{1,13},{5,9},{9,5},{13,1},{2,14},{6,10},... | collective-permute-start | bytes 221192 | tf_op jit(solution)/shard_map/ppermute | solution.py:413
  6.1 4.4 %collective-permute-start = (bf16[8,4608]{1,0:T(8,128)(2,1)S(1)}, bf16[8,4608]{1,0:T(8,128)(2,1)S(1)}, u32[]{:S(2)}, u32[]{:S(2)}) collective-permute-start(bf16[8,4608]{1,0:T(8,128)(2,1)S(1)} %get-tuple-element.109), channel_id=1, source_target_pairs={{0,8},{4,12},{8,0},{12,4},{1,9},{5,13},{9,1},{13,5},{2,10},{6,14},... | collective-permute-start | bytes 221192 | tf_op jit(solution)/shard_map/ppermute | solution.py:413
  15.7 7.8 %collective-permute-start.3 = (bf16[32,4096]{1,0:T(8,128)(2,1)S(1)}, bf16[32,4096]{1,0:T(8,128)(2,1)S(1)}, u32[]{:S(2)}, u32[]{:S(2)}) collective-permute-start(bf16[32,4096]{1,0:T(8,128)(2,1)S(1)} %get-tuple-element.58.refs_0_), channel_id=1, source_target_pairs={{0,8},{4,12},{8,0},{12,4},{1,9},{5,13},{9,1},{13,5},{2,10},{6,14},... | collective-permute-start | bytes 786440 | tf_op jit(solution)/shard_map/ppermute | solution.py:441
  18.3 5.3 %collective-permute-start.4 = (bf16[32,4096]{1,0:T(8,128)(2,1)S(1)}, bf16[32,4096]{1,0:T(8,128)(2,1)S(1)}, u32[]{:S(2)}, u32[]{:S(2)}) collective-permute-start(bf16[32,4096]{1,0:T(8,128)(2,1)S(1)} %get-tuple-element.58.refs_0_), channel_id=1, source_target_pairs={{0,4},{4,0},{8,12},{12,8},{1,5},{5,1},{9,13},{13,9},{2,6},{6,2},{1... | collective-permute-start | bytes 786440 | tf_op jit(solution)/shard_map/ppermute | solution.py:442
  23.5 1.5 %collective-permute-start.5 = (bf16[32,4096]{1,0:T(8,128)(2,1)S(1)}, bf16[32,4096]{1,0:T(8,128)(2,1)S(1)}, u32[]{:S(2)}, u32[]{:S(2)}) collective-permute-start(bf16[32,4096]{1,0:T(8,128)(2,1)S(1)} %collective-permute-done.3.refs_1_), channel_id=1, source_target_pairs={{0,4},{4,0},{8,12},{12,8},{1,5},{5,1},{9,13},{13,9},{2,6},{6,2},{1... | collective-permute-start | bytes 786440 | tf_op jit(solution)/shard_map/ppermute | solution.py:443
  30.9 11.9 %collective-permute-start.6 = (bf16[32,1792]{1,0:T(8,128)(2,1)S(1)}, bf16[32,1792]{1,0:T(8,128)(2,1)S(1)}, u32[]{:S(2)}, u32[]{:S(2)}) collective-permute-start(bf16[32,1792]{1,0:T(8,128)(2,1)S(1)} %convert_element_type.112), channel_id=1, source_target_pairs={{0,2},{1,3},{2,0},{3,1},{4,6},{5,7},{6,4},{7,5},{8,10},{9,11},{10,... | collective-permute-start | bytes 344072 | tf_op jit(solution)/shard_map/ppermute | solution.py:293
  33.8 8.9 %collective-permute-start.7 = (bf16[32,1792]{1,0:T(8,128)(2,1)S(1)}, bf16[32,1792]{1,0:T(8,128)(2,1)S(1)}, u32[]{:S(2)}, u32[]{:S(2)}) collective-permute-start(bf16[32,1792]{1,0:T(8,128)(2,1)S(1)} %get-tuple-element.113), channel_id=1, source_target_pairs={{0,3},{1,2},{2,1},{3,0},{4,7},{5,6},{6,5},{7,4},{8,11},{9,10},{10,... | collective-permute-start | bytes 344072 | tf_op jit(solution)/shard_map/ppermute | solution.py:293
  35.2 8.4 %collective-permute-start.8 = (bf16[32,1792]{1,0:T(8,128)(2,1)S(1)}, bf16[32,1792]{1,0:T(8,128)(2,1)S(1)}, u32[]{:S(2)}, u32[]{:S(2)}) collective-permute-start(bf16[32,1792]{1,0:T(8,128)(2,1)S(1)} %get-tuple-element.114), channel_id=1, source_target_pairs={{0,1},{1,0},{2,3},{3,2},{4,5},{5,4},{6,7},{7,6},{8,9},{9,8},{10,11... | collective-permute-start | bytes 344072 | tf_op jit(solution)/shard_map/ppermute | solution.py:293
  35.4 8.2 %collective-permute-start.9 = (bf16[1,256,512]{2,1,0:T(8,128)(2,1)S(1)}, bf16[1,256,512]{2,1,0:T(8,128)(2,1)S(1)}, u32[]{:S(2)}, u32[]{:S(2)}) collective-permute-start(bf16[1,256,512]{2,1,0:T(8,128)(2,1)S(1)} %get-tuple-element.70), channel_id=1, source_target_pairs={{0,4},{4,0},{8,12},{12,8},{1,5},{5,1},{9,13},{13,9},{2,6},{6,2},{1... | collective-permute-start | bytes 786440 | tf_op jit(solution)/shard_map/ppermute | solution.py:314
  35.5 8.7 %collective-permute-start.10 = (bf16[1,256,512]{2,1,0:T(8,128)(2,1)S(1)}, bf16[1,256,512]{2,1,0:T(8,128)(2,1)S(1)}, u32[]{:S(2)}, u32[]{:S(2)}) collective-permute-start(bf16[1,256,512]{2,1,0:T(8,128)(2,1)S(1)} %get-tuple-element.71), channel_id=1, source_target_pairs={{0,8},{4,12},{8,0},{12,4},{1,9},{5,13},{9,1},{13,5},{2,10},{6,14},... | collective-permute-start | bytes 786440 | tf_op jit(solution)/shard_map/ppermute | solution.py:313
  44.2 6.7 %collective-permute-start.13 = (bf16[32,1792]{1,0:T(8,128)(2,1)S(1)}, bf16[32,1792]{1,0:T(8,128)(2,1)S(1)}, u32[]{:S(2)}, u32[]{:S(2)}) collective-permute-start(bf16[32,1792]{1,0:T(8,128)(2,1)S(1)} %add_convert_fusion.1), channel_id=1, source_target_pairs={{0,3},{1,2},{2,1},{3,0},{4,7},{5,6},{6,5},{7,4},{8,11},{9,10},{10,... | collective-permute-start | bytes 344072 | tf_op jit(solution)/shard_map/ppermute | solution.py:320
  47.2 10.9 %collective-permute-start.12 = (bf16[32,1792]{1,0:T(8,128)(2,1)S(1)}, bf16[32,1792]{1,0:T(8,128)(2,1)S(1)}, u32[]{:S(2)}, u32[]{:S(2)}) collective-permute-start(bf16[32,1792]{1,0:T(8,128)(2,1)S(1)} %add_convert_fusion.1), channel_id=1, source_target_pairs={{0,2},{1,3},{2,0},{3,1},{4,6},{5,7},{6,4},{7,5},{8,10},{9,11},{10,... | collective-permute-start | bytes 344072 | tf_op jit(solution)/shard_map/ppermute | solution.py:320
  47.6 10.5 %collective-permute-start.11 = (bf16[32,1792]{1,0:T(8,128)(2,1)S(1)}, bf16[32,1792]{1,0:T(8,128)(2,1)S(1)}, u32[]{:S(2)}, u32[]{:S(2)}) collective-permute-start(bf16[32,1792]{1,0:T(8,128)(2,1)S(1)} %add_convert_fusion.1), channel_id=1, source_target_pairs={{0,1},{1,0},{2,3},{3,2},{4,5},{5,4},{6,7},{7,6},{8,9},{9,8},{10,11... | collective-permute-start | bytes 344072 | tf_op jit(solution)/shard_map/ppermute | solution.py:320
  48.6 9.6 %collective-permute-start.14 = (bf16[1,256,512]{2,1,0:T(8,128)(2,1)S(1)}, bf16[1,256,512]{2,1,0:T(8,128)(2,1)S(1)}, u32[]{:S(2)}, u32[]{:S(2)}) collective-permute-start(bf16[1,256,512]{2,1,0:T(8,128)(2,1)S(1)} %get-tuple-element.74), channel_id=1, source_target_pairs={{0,12},{4,8},{8,4},{12,0},{1,13},{5,9},{9,5},{13,1},{2,14},{6,10},... | collective-permute-start | bytes 786440 | tf_op jit(solution)/shard_map/ppermute | solution.py:319
  65.5 2.1 %collective-permute-start.15 = (bf16[2,32,4608]{2,1,0:T(8,128)(2,1)S(1)}, bf16[2,32,4608]{2,1,0:T(8,128)(2,1)S(1)}, u32[]{:S(2)}, u32[]{:S(2)}) collective-permute-start(bf16[2,32,4608]{2,1,0:T(8,128)(2,1)S(1)} %get-tuple-element.77), channel_id=1, source_target_pairs={{0,4},{4,0},{8,12},{12,8},{1,5},{5,1},{9,13},{13,9},{2,6},{6,2},{1... | collective-permute-start | bytes 1769480 | tf_op jit(solution)/shard_map/ppermute | solution.py:134
  67.6 9.1 %collective-permute-start.16 = (bf16[32,4608]{1,0:T(8,128)(2,1)S(1)}, bf16[32,4608]{1,0:T(8,128)(2,1)S(1)}, u32[]{:S(2)}, u32[]{:S(2)}) collective-permute-start(bf16[32,4608]{1,0:T(8,128)(2,1)S(1)} %get-tuple-element.101), channel_id=1, source_target_pairs={{0,8},{4,12},{8,0},{12,4},{1,9},{5,13},{9,1},{13,5},{2,10},{6,14},... | collective-permute-start | bytes 884744 | tf_op jit(solution)/shard_map/ppermute | solution.py:139
  69.3 26.9 %slice-start = ((s8[16515072]{0:T(1024)(128)(4,1)}), s8[3932160]{0:T(1024)(128)(4,1)S(1)}, s32[]{:S(2)}) async-start(s8[16515072]{0:T(1024)(128)(4,1)} %bitcast.56), calls=%async_computation | async-start | bytes 7864320
  69.3 26.9 %slice-start.1 = ((s8[16515072]{0:T(1024)(128)(4,1)}), s8[4194304]{0:T(1024)(128)(4,1)S(1)}, s32[]{:S(2)}) async-start(s8[16515072]{0:T(1024)(128)(4,1)} %bitcast.56), calls=%async_computation.1 | async-start | bytes 8388608
  69.3 26.9 %slice-start.2 = ((s8[16515072]{0:T(1024)(128)(4,1)}), s8[4194304]{0:T(1024)(128)(4,1)S(1)}, s32[]{:S(2)}) async-start(s8[16515072]{0:T(1024)(128)(4,1)} %bitcast.56), calls=%async_computation.2 | async-start | bytes 8388608
  76.0 26.3 %copy-start.3 = (bf16[1,256,512]{2,1,0:T(8,128)(2,1)S(1)}, bf16[1,256,512]{2,1,0:T(8,128)(2,1)}, u32[]{:S(2)}) copy-start(bf16[1,256,512]{2,1,0:T(8,128)(2,1)} %copy-done.2) | copy-start | bytes 786436
  76.0 26.3 %copy-start.5 = (bf16[1,256,512]{2,1,0:T(8,128)(2,1)S(1)}, bf16[1,256,512]{2,1,0:T(8,128)(2,1)}, u32[]{:S(2)}) copy-start(bf16[1,256,512]{2,1,0:T(8,128)(2,1)} %copy-done.4) | copy-start | bytes 786436
  76.1 2.5 %collective-permute-start.18 = (bf16[2,32,4608]{2,1,0:T(8,128)(2,1)S(1)}, bf16[2,32,4608]{2,1,0:T(8,128)(2,1)S(1)}, u32[]{:S(2)}, u32[]{:S(2)}) collective-permute-start(bf16[2,32,4608]{2,1,0:T(8,128)(2,1)S(1)} %get-tuple-element.81), channel_id=1, source_target_pairs={{0,4},{4,0},{8,12},{12,8},{1,5},{5,1},{9,13},{13,9},{2,6},{6,2},{1... | collective-permute-start | bytes 1769480 | tf_op jit(solution)/shard_map/ppermute | solution.py:134
  76.9 6.8 %collective-permute-start.17 = (bf16[32,2304]{1,0:T(8,128)(2,1)S(1)}, bf16[32,2304]{1,0:T(8,128)(2,1)S(1)}, u32[]{:S(2)}, u32[]{:S(2)}) collective-permute-start(bf16[32,2304]{1,0:T(8,128)(2,1)S(1)} %fusion.3), channel_id=1, source_target_pairs={{0,8},{4,12},{8,0},{12,4},{1,9},{5,13},{9,1},{13,5},{2,10},{6,14},... | collective-permute-start | bytes 442376 | tf_op jit(solution)/shard_map/ppermute | solution.py:336
  78.5 33.4 %copy-start.1 = (bf16[128,1792]{1,0:T(8,128)(2,1)S(1)}, bf16[128,1792]{1,0:T(8,128)(2,1)}, u32[]{:S(2)}) copy-start(bf16[128,1792]{1,0:T(8,128)(2,1)} %param.17) | copy-start | bytes 1376260
  78.7 10.3 %collective-permute-start.20 = (bf16[32,4608]{1,0:T(8,128)(2,1)S(1)}, bf16[32,4608]{1,0:T(8,128)(2,1)S(1)}, u32[]{:S(2)}, u32[]{:S(2)}) collective-permute-start(bf16[32,4608]{1,0:T(8,128)(2,1)S(1)} %get-tuple-element.100), channel_id=1, source_target_pairs={{0,8},{4,12},{8,0},{12,4},{1,9},{5,13},{9,1},{13,5},{2,10},{6,14},... | collective-permute-start | bytes 884744 | tf_op jit(solution)/shard_map/ppermute | solution.py:139
  83.8 6.4 %collective-permute-start.19 = (bf16[2,32,2304]{2,1,0:T(8,128)(2,1)S(1)}, bf16[2,32,2304]{2,1,0:T(8,128)(2,1)S(1)}, u32[]{:S(2)}, u32[]{:S(2)}) collective-permute-start(bf16[2,32,2304]{2,1,0:T(8,128)(2,1)S(1)} %pad_maximum_fusion.4), channel_id=1, source_target_pairs={{0,4},{4,0},{8,12},{12,8},{1,5},{5,1},{9,13},{13,9},{2,6},{6,2},{1... | collective-permute-start | bytes 884744 | tf_op jit(solution)/shard_map/ppermute | solution.py:340
  89.2 5.2 %collective-permute-start.21 = (bf16[32,2304]{1,0:T(8,128)(2,1)S(1)}, bf16[32,2304]{1,0:T(8,128)(2,1)S(1)}, u32[]{:S(2)}, u32[]{:S(2)}) collective-permute-start(bf16[32,2304]{1,0:T(8,128)(2,1)S(1)} %fusion.2), channel_id=1, source_target_pairs={{0,8},{4,12},{8,0},{12,4},{1,9},{5,13},{9,1},{13,5},{2,10},{6,14},... | collective-permute-start | bytes 442376 | tf_op jit(solution)/shard_map/ppermute | solution.py:336
  94.5 1.6 %collective-permute-start.22 = (bf16[2,32,2304]{2,1,0:T(8,128)(2,1)S(1)}, bf16[2,32,2304]{2,1,0:T(8,128)(2,1)S(1)}, u32[]{:S(2)}, u32[]{:S(2)}) collective-permute-start(bf16[2,32,2304]{2,1,0:T(8,128)(2,1)S(1)} %pad_maximum_fusion.5), channel_id=1, source_target_pairs={{0,4},{4,0},{8,12},{12,8},{1,5},{5,1},{9,13},{13,9},{2,6},{6,2},{1... | collective-permute-start | bytes 884744 | tf_op jit(solution)/shard_map/ppermute | solution.py:340
  98.7 11.3 %collective-permute-start.23 = (bf16[32,1792]{1,0:T(8,128)(2,1)S(1)}, bf16[32,1792]{1,0:T(8,128)(2,1)S(1)}, u32[]{:S(2)}, u32[]{:S(2)}) collective-permute-start(bf16[32,1792]{1,0:T(8,128)(2,1)S(1)} %convert_element_type.133), channel_id=1, source_target_pairs={{0,2},{1,3},{2,0},{3,1},{4,6},{5,7},{6,4},{7,5},{8,10},{9,11},{10,... | collective-permute-start | bytes 344072 | tf_op jit(solution)/shard_map/ppermute | solution.py:293
  99.6 10.4 %collective-permute-start.24 = (bf16[32,1792]{1,0:T(8,128)(2,1)S(1)}, bf16[32,1792]{1,0:T(8,128)(2,1)S(1)}, u32[]{:S(2)}, u32[]{:S(2)}) collective-permute-start(bf16[32,1792]{1,0:T(8,128)(2,1)S(1)} %get-tuple-element.111), channel_id=1, source_target_pairs={{0,3},{1,2},{2,1},{3,0},{4,7},{5,6},{6,5},{7,4},{8,11},{9,10},{10,... | collective-permute-start | bytes 344072 | tf_op jit(solution)/shard_map/ppermute | solution.py:293
  101.6 9.6 %collective-permute-start.25 = (bf16[32,1792]{1,0:T(8,128)(2,1)S(1)}, bf16[32,1792]{1,0:T(8,128)(2,1)S(1)}, u32[]{:S(2)}, u32[]{:S(2)}) collective-permute-start(bf16[32,1792]{1,0:T(8,128)(2,1)S(1)} %get-tuple-element.112), channel_id=1, source_target_pairs={{0,1},{1,0},{2,3},{3,2},{4,5},{5,4},{6,7},{7,6},{8,9},{9,8},{10,11... | collective-permute-start | bytes 344072 | tf_op jit(solution)/shard_map/ppermute | solution.py:293
  (7 other events, 104.7 us)

commit v6 on v5

--- a/solution.py
+++ b/solution.py
@@ -117,7 +117,7 @@
             pltpu.VMEM((slots, heads, 128), jnp.float32),
             pltpu.VMEM((slots, heads, size), jnp.float32),
         ],
-        compiler_params=pltpu.CompilerParams(vmem_limit_bytes=24 * 2**20),
+        compiler_params=pltpu.CompilerParams(vmem_limit_bytes=12 * 2**20),
         name="attention",
     )(numbers, *received, in_hbm(cache_pool))
 
@@ -199,7 +199,7 @@
             pltpu.VMEM((picker.shape[0], columns), jnp.float32),
             pltpu.SemaphoreType.DMA((depth // tile,)),
         ],
-        compiler_params=pltpu.CompilerParams(vmem_limit_bytes=32 * 2**20),
+        compiler_params=pltpu.CompilerParams(vmem_limit_bytes=20 * 2**20),
         name="project",
     )(picker, *pieces, in_hbm(w))
 
@@ -236,7 +236,7 @@
             pltpu.VMEM((count, x.shape[1], tile), w_gate.dtype),
             pltpu.SemaphoreType.DMA((count,)),
         ],
-        compiler_params=pltpu.CompilerParams(vmem_limit_bytes=32 * 2**20),
+        compiler_params=pltpu.CompilerParams(vmem_limit_bytes=20 * 2**20),
         name="gate_and_up",
     )(x, in_hbm(w_gate), in_hbm(w_up))
 

time: 112 us -> 112 us (level)
  no operation moved by 1% of the time
where the time goes in v6:
time: 112 us
  waiting for transfers between devices  48.6 us (43%)
  Pallas kernels  26.7 us (24%)
  starting transfers between devices  24.2 us (22%)
  other arithmetic  5.84 us (5%)
  local copies, waits for them, and re-layouts  4.41 us (4%)
  matrix products  1.19 us (1%)
  between operations  1.12 us (1%)
    ppermute x6, waiting for transfers between devices, sum_direct(): lax.ppermute(x, 'ffn', swap_perm(4, d))  13.6 us
    pallas_call x2, Pallas kernels, gate_and_up(): pl.pallas_call(functools.partial(gate_kernel, start=start), out_shape=spl...  13.3 us
    ppermute x3, waiting for transfers between devices, paired_rows(): came = {d: lax.ppermute(kept, 'ffn', swap_perm(4, d)) for d in (2, 3, 1)}  9.47 us
    ppermute x2, waiting for transfers between devices, paired_rows(): across = lax.ppermute(quarter, 'attn', swap_perm(4, 2))  8.66 us
    ppermute x6, starting transfers between devices, sum_direct(): lax.ppermute(x, 'ffn', swap_perm(4, d))  8.1 us
    pallas_call x1, Pallas kernels, project(): pl.pallas_call(project_kernel, out_shape=split_shapes(picker.shape[0] //...  5.75 us
    ppermute x2, waiting for transfers between devices, fold_last(): far = lax.ppermute(leaving, axis, swap_perm(4, 2))  5.73 us
    pallas_call x1, Pallas kernels, attend(): pl.pallas_call(functools.partial(attention_kernel, distances=distances),...  5.25 us
  transfers between devices with their start and end apart: 26, of which 17 were waited for; matrix products, arithmetic and copies ran while one was open for 7% of the time, Pallas kernels for 6%

profile of v6, /device:TPU:0, one launch (start us, length us, event | category | flops | bytes accessed | tf_op | source)
XLA Modules:
  0.0 111.9 jit_solution(7437783153563817517)
XLA Ops:
  1.7 1.2 %convolution_convert_fusion = bf16[32,4608]{1,0:T(8,128)(2,1)S(1)} fusion(bf16[32,512]{1,0:T(8,128)(2,1)} %param.12, bf16[32,4096]{1,0:T(8,128)(2,1)} %param.11, s32[32]{0:T(128)S(1)} %fusion.20), kind=kOutput, calls=%fused_computation.2 | convolution fusion | flops 10175488 | bytes 589952 | tf_op jit(solution)/shard_map/dot_general | solution.py:405
  3.4 2.6 %collective-permute-start.1 = (bf16[8,4608]{1,0:T(8,128)(2,1)S(1)}, bf16[8,4608]{1,0:T(8,128)(2,1)S(1)}, u32[]{:S(2)}, u32[]{:S(2)}) collective-permute-start(bf16[8,4608]{1,0:T(8,128)(2,1)S(1)} %get-tuple-element.108), channel_id=1, source_target_pairs={{0,12},{4,8},{8,4},{12,0},{1,13},{5,9},{9,5},{13,1},{2,14},{6,10},... | collective-permute-start | bytes 221192 | tf_op jit(solution)/shard_map/ppermute | solution.py:413
  8.7 1.8 %collective-permute-done.refs_1_ = bf16[8,4608]{1,0:T(8,128)(2,1)S(1)} collective-permute-done((bf16[8,4608]{1,0:T(8,128)(2,1)S(1)}, bf16[8,4608]{1,0:T(8,128)(2,1)S(1)}, u32[]{:S(2)}, u32[]{:S(2)}) %collective-permute-start) | collective-permute-done | bytes 73760 | tf_op jit(solution)/shard_map/ppermute | solution.py:413
  10.5 5.2 %attention.1 = (bf16[32,4096]{1,0:T(8,128)(2,1)}, bf16[32,4096]{1,0:T(8,128)(2,1)S(1)}, bf16[1,256,512]{2,1,0:T(8,128)(2,1)S(1)}, bf16[1,256,512]{2,1,0:T(8,128)...) custom-call(s32[147]{0:T(256)S(1)} %pad_add_fusion.number_ref, ...), custom_call_target="tpu_custom_call" | custom-call | tf_op jit(solution)/shard_map/attention/pallas_call | solution.py:106
  15.7 1.8 %collective-permute-start.3 = (bf16[32,4096]{1,0:T(8,128)(2,1)S(1)}, bf16[32,4096]{1,0:T(8,128)(2,1)S(1)}, u32[]{:S(2)}, u32[]{:S(2)}) collective-permute-start(bf16[32,4096]{1,0:T(8,128)(2,1)S(1)} %get-tuple-element.58.refs_0_), channel_id=1, source_target_pairs={{0,8},{4,12},{8,0},{12,4},{1,9},{5,13},{9,1},{13,5},{2,10},{6,14},... | collective-permute-start | bytes 786440 | tf_op jit(solution)/shard_map/ppermute | solution.py:441
  18.4 5.2 %collective-permute-done.3.refs_1_ = bf16[32,4096]{1,0:T(8,128)(2,1)S(1)} collective-permute-done((bf16[32,4096]{1,0:T(8,128)(2,1)S(1)}, bf16[32,4096]{1,0:T(8,128)(2,1)S(1)}, u32[]{:S(2)}, u32[]{:S(2)}) %collective-permute-start.3) | collective-permute-done | bytes 262176 | tf_op jit(solution)/shard_map/ppermute | solution.py:441
  23.7 1.4 %collective-permute-done.5.refs_3_ = bf16[32,4096]{1,0:T(8,128)(2,1)S(1)} collective-permute-done((bf16[32,4096]{1,0:T(8,128)(2,1)S(1)}, bf16[32,4096]{1,0:T(8,128)(2,1)S(1)}, u32[]{:S(2)}, u32[]{:S(2)}) %collective-permute-start.5) | collective-permute-done | bytes 262176 | tf_op jit(solution)/shard_map/ppermute | solution.py:443
  25.1 5.8 %project.1 = (f32[32,1792]{1,0:T(8,128)S(1)}, f32[32,1792]{1,0:T(8,128)S(1)}, bf16[2,32,1792]{2,1,0:T(8,128)(2,1)S(1)}) custom-call(bf16[128,128]{1,0:T(8,128)(2,1)S(1)} %fusion.7.picker_ref, bf16[32,4096]{1,0:T(8,128)(2,1)S(1)} %get-tuple-element.58.refs_0_, bf16[32,4096]{1,0:T(8,128)(2,1)S(1)} %collective-permute-done.3.refs_1_, ...), custom_call_target="tpu_custom_call" | custom-call | tf_op jit(solution)/shard_map/project/pallas_call | solution.py:192
  30.9 2.9 %collective-permute-start.6 = (bf16[32,1792]{1,0:T(8,128)(2,1)S(1)}, bf16[32,1792]{1,0:T(8,128)(2,1)S(1)}, u32[]{:S(2)}, u32[]{:S(2)}) collective-permute-start(bf16[32,1792]{1,0:T(8,128)(2,1)S(1)} %convert_element_type.112), channel_id=1, source_target_pairs={{0,2},{1,3},{2,0},{3,1},{4,6},{5,7},{6,4},{7,5},{8,10},{9,11},{10,... | collective-permute-start | bytes 344072 | tf_op jit(solution)/shard_map/ppermute | solution.py:293
  33.8 1.4 %collective-permute-start.7 = (bf16[32,1792]{1,0:T(8,128)(2,1)S(1)}, bf16[32,1792]{1,0:T(8,128)(2,1)S(1)}, u32[]{:S(2)}, u32[]{:S(2)}) collective-permute-start(bf16[32,1792]{1,0:T(8,128)(2,1)S(1)} %get-tuple-element.113), channel_id=1, source_target_pairs={{0,3},{1,2},{2,1},{3,0},{4,7},{5,6},{6,5},{7,4},{8,11},{9,10},{10,... | collective-permute-start | bytes 344072 | tf_op jit(solution)/shard_map/ppermute | solution.py:293
  35.5 1.6 %collective-permute-start.10 = (bf16[1,256,512]{2,1,0:T(8,128)(2,1)S(1)}, bf16[1,256,512]{2,1,0:T(8,128)(2,1)S(1)}, u32[]{:S(2)}, u32[]{:S(2)}) collective-permute-start(bf16[1,256,512]{2,1,0:T(8,128)(2,1)S(1)} %get-tuple-element.71), channel_id=1, source_target_pairs={{0,8},{4,12},{8,0},{12,4},{1,9},{5,13},{9,1},{13,5},{2,10},{6,14},... | collective-permute-start | bytes 786440 | tf_op jit(solution)/shard_map/ppermute | solution.py:313
  37.0 5.8 %collective-permute-done.6 = bf16[32,1792]{1,0:T(8,128)(2,1)S(1)} collective-permute-done((bf16[32,1792]{1,0:T(8,128)(2,1)S(1)}, bf16[32,1792]{1,0:T(8,128)(2,1)S(1)}, u32[]{:S(2)}, u32[]{:S(2)}) %collective-permute-start.6) | collective-permute-done | bytes 114720 | tf_op jit(solution)/shard_map/ppermute | solution.py:293
  44.2 3.0 %collective-permute-start.13 = (bf16[32,1792]{1,0:T(8,128)(2,1)S(1)}, bf16[32,1792]{1,0:T(8,128)(2,1)S(1)}, u32[]{:S(2)}, u32[]{:S(2)}) collective-permute-start(bf16[32,1792]{1,0:T(8,128)(2,1)S(1)} %add_convert_fusion.1), channel_id=1, source_target_pairs={{0,3},{1,2},{2,1},{3,0},{4,7},{5,6},{6,5},{7,4},{8,11},{9,10},{10,... | collective-permute-start | bytes 344072 | tf_op jit(solution)/shard_map/ppermute | solution.py:320
  47.5 1.0 collective-permute-start.11
  48.6 2.3 %collective-permute-done.13 = bf16[32,1792]{1,0:T(8,128)(2,1)S(1)} collective-permute-done((bf16[32,1792]{1,0:T(8,128)(2,1)S(1)}, bf16[32,1792]{1,0:T(8,128)(2,1)S(1)}, u32[]{:S(2)}, u32[]{:S(2)}) %collective-permute-start.13) | collective-permute-done | bytes 114720 | tf_op jit(solution)/shard_map/ppermute | solution.py:320
  50.9 7.1 %collective-permute-done.12 = bf16[32,1792]{1,0:T(8,128)(2,1)S(1)} collective-permute-done((bf16[32,1792]{1,0:T(8,128)(2,1)S(1)}, bf16[32,1792]{1,0:T(8,128)(2,1)S(1)}, u32[]{:S(2)}, u32[]{:S(2)}) %collective-permute-start.12) | collective-permute-done | bytes 114720 | tf_op jit(solution)/shard_map/ppermute | solution.py:320
  58.9 6.6 %gate_and_up.2 = (f32[32,4608]{1,0:T(8,128)S(1)}, f32[32,4608]{1,0:T(8,128)S(1)}, bf16[2,32,4608]{2,1,0:T(8,128)(2,1)S(1)}) custom-call(bf16[128,1792]{1,0:T(8,128)(2,1)S(1)} %bitcast.58, bf16[1792,4608]{1,0:T(8,128)(2,1)} %gate_ref.3, bf16[1792,4608]{1,0:T(8,128)(2,1)} %up_ref.3), custom_call_target="tpu_custom_call" | custom-call | tf_op jit(solution)/shard_map/gate_and_up/pallas_call | solution.py:230
  66.2 0.9 iota_reduce_fusion
  67.6 1.6 %collective-permute-start.16 = (bf16[32,4608]{1,0:T(8,128)(2,1)S(1)}, bf16[32,4608]{1,0:T(8,128)(2,1)S(1)}, u32[]{:S(2)}, u32[]{:S(2)}) collective-permute-start(bf16[32,4608]{1,0:T(8,128)(2,1)S(1)} %get-tuple-element.101), channel_id=1, source_target_pairs={{0,8},{4,12},{8,0},{12,4},{1,9},{5,13},{9,1},{13,5},{2,10},{6,14},... | collective-permute-start | bytes 884744 | tf_op jit(solution)/shard_map/ppermute | solution.py:139
  69.3 6.7 %gate_and_up.3 = (f32[32,4608]{1,0:T(8,128)S(1)}, f32[32,4608]{1,0:T(8,128)S(1)}, bf16[2,32,4608]{2,1,0:T(8,128)(2,1)S(1)}) custom-call(bf16[128,1792]{1,0:T(8,128)(2,1)S(1)} %bitcast.59, bf16[1792,4608]{1,0:T(8,128)(2,1)} %gate_ref.3, bf16[1792,4608]{1,0:T(8,128)(2,1)} %up_ref.3), custom_call_target="tpu_custom_call" | custom-call | tf_op jit(solution)/shard_map/gate_and_up/pallas_call | solution.py:230
  76.9 1.6 %collective-permute-start.17 = (bf16[32,2304]{1,0:T(8,128)(2,1)S(1)}, bf16[32,2304]{1,0:T(8,128)(2,1)S(1)}, u32[]{:S(2)}, u32[]{:S(2)}) collective-permute-start(bf16[32,2304]{1,0:T(8,128)(2,1)S(1)} %fusion.3), channel_id=1, source_target_pairs={{0,8},{4,12},{8,0},{12,4},{1,9},{5,13},{9,1},{13,5},{2,10},{6,14},... | collective-permute-start | bytes 442376 | tf_op jit(solution)/shard_map/ppermute | solution.py:336
  79.2 4.4 %collective-permute-done.17 = bf16[32,2304]{1,0:T(8,128)(2,1)S(1)} collective-permute-done((bf16[32,2304]{1,0:T(8,128)(2,1)S(1)}, bf16[32,2304]{1,0:T(8,128)(2,1)S(1)}, u32[]{:S(2)}, u32[]{:S(2)}) %collective-permute-start.17) | collective-permute-done | bytes 147488 | tf_op jit(solution)/shard_map/ppermute | solution.py:336
  83.8 5.2 %collective-permute-done.20 = bf16[32,4608]{1,0:T(8,128)(2,1)S(1)} collective-permute-done((bf16[32,4608]{1,0:T(8,128)(2,1)S(1)}, bf16[32,4608]{1,0:T(8,128)(2,1)S(1)}, u32[]{:S(2)}, u32[]{:S(2)}) %collective-permute-start.20) | collective-permute-done | bytes 294944 | tf_op jit(solution)/shard_map/ppermute | solution.py:139
  89.2 0.9 collective-permute-start.21
  90.2 4.2 %collective-permute-done.21 = bf16[32,2304]{1,0:T(8,128)(2,1)S(1)} collective-permute-done((bf16[32,2304]{1,0:T(8,128)(2,1)S(1)}, bf16[32,2304]{1,0:T(8,128)(2,1)S(1)}, u32[]{:S(2)}, u32[]{:S(2)}) %collective-permute-start.21) | collective-permute-done | bytes 147488 | tf_op jit(solution)/shard_map/ppermute | solution.py:336
  94.6 1.5 %collective-permute-done.22 = bf16[2,32,2304]{2,1,0:T(8,128)(2,1)S(1)} collective-permute-done((bf16[2,32,2304]{2,1,0:T(8,128)(2,1)S(1)}, bf16[2,32,2304]{2,1,0:T(8,128)(2,1)S(1)}, u32[]{:S(2)}, u32[]{:S(2)}) %collective-permute-start.22) | collective-permute-done | bytes 294944 | tf_op jit(solution)/shard_map/ppermute | solution.py:340
  96.2 2.4 %down_project.1 = (f32[32,1792]{1,0:T(8,128)S(1)}, f32[32,1792]{1,0:T(8,128)S(1)}, bf16[2,32,1792]{2,1,0:T(8,128)(2,1)S(1)}) custom-call(s32[1]{0:T(128)} %bitcast.at_ref, bf16[128,2304]{1,0:T(8,128)(2,1)S(1)} %bitcast.60, bf16[128,2304]{1,0:T(8,128)(2,1)S(1)} %bitcast.61, bf16[4608,1792]{1,0:T(8,128)(2,1)S(1)} %bitcast.57), custom_call_target="tpu_custom_call" | custom-call | tf_op jit(solution)/shard_map/down_project/pallas_call | solution.py:278
  98.7 0.8 collective-permute-start.23
  99.6 2.1 %collective-permute-start.24 = (bf16[32,1792]{1,0:T(8,128)(2,1)S(1)}, bf16[32,1792]{1,0:T(8,128)(2,1)S(1)}, u32[]{:S(2)}, u32[]{:S(2)}) collective-permute-start(bf16[32,1792]{1,0:T(8,128)(2,1)S(1)} %get-tuple-element.111), channel_id=1, source_target_pairs={{0,3},{1,2},{2,1},{3,0},{4,7},{5,6},{6,5},{7,4},{8,11},{9,10},{10,... | collective-permute-start | bytes 344072 | tf_op jit(solution)/shard_map/ppermute | solution.py:293
  103.1 1.0 select_select_fusion
  104.1 5.9 %collective-permute-done.23 = bf16[32,1792]{1,0:T(8,128)(2,1)S(1)} collective-permute-done((bf16[32,1792]{1,0:T(8,128)(2,1)S(1)}, bf16[32,1792]{1,0:T(8,128)(2,1)S(1)}, u32[]{:S(2)}, u32[]{:S(2)}) %collective-permute-start.23) | collective-permute-done | bytes 114720 | tf_op jit(solution)/shard_map/ppermute | solution.py:293
  110.0 1.2 %collective-permute-done.25 = bf16[32,1792]{1,0:T(8,128)(2,1)S(1)} collective-permute-done((bf16[32,1792]{1,0:T(8,128)(2,1)S(1)}, bf16[32,1792]{1,0:T(8,128)(2,1)S(1)}, u32[]{:S(2)}, u32[]{:S(2)}) %collective-permute-start.25) | collective-permute-done | bytes 114720 | tf_op jit(solution)/shard_map/ppermute | solution.py:293
  (108 shorter events, 13.8 us)
Async XLA Ops:
  2.9 5.5 %collective-permute-start.2 = (bf16[8,4608]{1,0:T(8,128)(2,1)S(1)}, bf16[8,4608]{1,0:T(8,128)(2,1)S(1)}, u32[]{:S(2)}, u32[]{:S(2)}) collective-permute-start(bf16[8,4608]{1,0:T(8,128)(2,1)S(1)} %get-tuple-element.107), channel_id=1, source_target_pairs={{0,4},{4,0},{8,12},{12,8},{1,5},{5,1},{9,13},{13,9},{2,6},{6,2},{1... | collective-permute-start | bytes 221192 | tf_op jit(solution)/shard_map/ppermute | solution.py:413
  3.4 5.2 %collective-permute-start.1 = (bf16[8,4608]{1,0:T(8,128)(2,1)S(1)}, bf16[8,4608]{1,0:T(8,128)(2,1)S(1)}, u32[]{:S(2)}, u32[]{:S(2)}) collective-permute-start(bf16[8,4608]{1,0:T(8,128)(2,1)S(1)} %get-tuple-element.108), channel_id=1, source_target_pairs={{0,12},{4,8},{8,4},{12,0},{1,13},{5,9},{9,5},{13,1},{2,14},{6,10},... | collective-permute-start | bytes 221192 | tf_op jit(solution)/shard_map/ppermute | solution.py:413
  6.1 4.4 %collective-permute-start = (bf16[8,4608]{1,0:T(8,128)(2,1)S(1)}, bf16[8,4608]{1,0:T(8,128)(2,1)S(1)}, u32[]{:S(2)}, u32[]{:S(2)}) collective-permute-start(bf16[8,4608]{1,0:T(8,128)(2,1)S(1)} %get-tuple-element.109), channel_id=1, source_target_pairs={{0,8},{4,12},{8,0},{12,4},{1,9},{5,13},{9,1},{13,5},{2,10},{6,14},... | collective-permute-start | bytes 221192 | tf_op jit(solution)/shard_map/ppermute | solution.py:413
  15.7 7.8 %collective-permute-start.3 = (bf16[32,4096]{1,0:T(8,128)(2,1)S(1)}, bf16[32,4096]{1,0:T(8,128)(2,1)S(1)}, u32[]{:S(2)}, u32[]{:S(2)}) collective-permute-start(bf16[32,4096]{1,0:T(8,128)(2,1)S(1)} %get-tuple-element.58.refs_0_), channel_id=1, source_target_pairs={{0,8},{4,12},{8,0},{12,4},{1,9},{5,13},{9,1},{13,5},{2,10},{6,14},... | collective-permute-start | bytes 786440 | tf_op jit(solution)/shard_map/ppermute | solution.py:441
  18.4 5.3 %collective-permute-start.4 = (bf16[32,4096]{1,0:T(8,128)(2,1)S(1)}, bf16[32,4096]{1,0:T(8,128)(2,1)S(1)}, u32[]{:S(2)}, u32[]{:S(2)}) collective-permute-start(bf16[32,4096]{1,0:T(8,128)(2,1)S(1)} %get-tuple-element.58.refs_0_), channel_id=1, source_target_pairs={{0,4},{4,0},{8,12},{12,8},{1,5},{5,1},{9,13},{13,9},{2,6},{6,2},{1... | collective-permute-start | bytes 786440 | tf_op jit(solution)/shard_map/ppermute | solution.py:442
  23.5 1.5 %collective-permute-start.5 = (bf16[32,4096]{1,0:T(8,128)(2,1)S(1)}, bf16[32,4096]{1,0:T(8,128)(2,1)S(1)}, u32[]{:S(2)}, u32[]{:S(2)}) collective-permute-start(bf16[32,4096]{1,0:T(8,128)(2,1)S(1)} %collective-permute-done.3.refs_1_), channel_id=1, source_target_pairs={{0,4},{4,0},{8,12},{12,8},{1,5},{5,1},{9,13},{13,9},{2,6},{6,2},{1... | collective-permute-start | bytes 786440 | tf_op jit(solution)/shard_map/ppermute | solution.py:443
  30.9 11.9 %collective-permute-start.6 = (bf16[32,1792]{1,0:T(8,128)(2,1)S(1)}, bf16[32,1792]{1,0:T(8,128)(2,1)S(1)}, u32[]{:S(2)}, u32[]{:S(2)}) collective-permute-start(bf16[32,1792]{1,0:T(8,128)(2,1)S(1)} %convert_element_type.112), channel_id=1, source_target_pairs={{0,2},{1,3},{2,0},{3,1},{4,6},{5,7},{6,4},{7,5},{8,10},{9,11},{10,... | collective-permute-start | bytes 344072 | tf_op jit(solution)/shard_map/ppermute | solution.py:293
  33.8 9.0 %collective-permute-start.7 = (bf16[32,1792]{1,0:T(8,128)(2,1)S(1)}, bf16[32,1792]{1,0:T(8,128)(2,1)S(1)}, u32[]{:S(2)}, u32[]{:S(2)}) collective-permute-start(bf16[32,1792]{1,0:T(8,128)(2,1)S(1)} %get-tuple-element.113), channel_id=1, source_target_pairs={{0,3},{1,2},{2,1},{3,0},{4,7},{5,6},{6,5},{7,4},{8,11},{9,10},{10,... | collective-permute-start | bytes 344072 | tf_op jit(solution)/shard_map/ppermute | solution.py:293
  35.1 8.4 %collective-permute-start.8 = (bf16[32,1792]{1,0:T(8,128)(2,1)S(1)}, bf16[32,1792]{1,0:T(8,128)(2,1)S(1)}, u32[]{:S(2)}, u32[]{:S(2)}) collective-permute-start(bf16[32,1792]{1,0:T(8,128)(2,1)S(1)} %get-tuple-element.114), channel_id=1, source_target_pairs={{0,1},{1,0},{2,3},{3,2},{4,5},{5,4},{6,7},{7,6},{8,9},{9,8},{10,11... | collective-permute-start | bytes 344072 | tf_op jit(solution)/shard_map/ppermute | solution.py:293
  35.4 8.2 %collective-permute-start.9 = (bf16[1,256,512]{2,1,0:T(8,128)(2,1)S(1)}, bf16[1,256,512]{2,1,0:T(8,128)(2,1)S(1)}, u32[]{:S(2)}, u32[]{:S(2)}) collective-permute-start(bf16[1,256,512]{2,1,0:T(8,128)(2,1)S(1)} %get-tuple-element.70), channel_id=1, source_target_pairs={{0,4},{4,0},{8,12},{12,8},{1,5},{5,1},{9,13},{13,9},{2,6},{6,2},{1... | collective-permute-start | bytes 786440 | tf_op jit(solution)/shard_map/ppermute | solution.py:314
  35.5 8.7 %collective-permute-start.10 = (bf16[1,256,512]{2,1,0:T(8,128)(2,1)S(1)}, bf16[1,256,512]{2,1,0:T(8,128)(2,1)S(1)}, u32[]{:S(2)}, u32[]{:S(2)}) collective-permute-start(bf16[1,256,512]{2,1,0:T(8,128)(2,1)S(1)} %get-tuple-element.71), channel_id=1, source_target_pairs={{0,8},{4,12},{8,0},{12,4},{1,9},{5,13},{9,1},{13,5},{2,10},{6,14},... | collective-permute-start | bytes 786440 | tf_op jit(solution)/shard_map/ppermute | solution.py:313
  44.2 6.7 %collective-permute-start.13 = (bf16[32,1792]{1,0:T(8,128)(2,1)S(1)}, bf16[32,1792]{1,0:T(8,128)(2,1)S(1)}, u32[]{:S(2)}, u32[]{:S(2)}) collective-permute-start(bf16[32,1792]{1,0:T(8,128)(2,1)S(1)} %add_convert_fusion.1), channel_id=1, source_target_pairs={{0,3},{1,2},{2,1},{3,0},{4,7},{5,6},{6,5},{7,4},{8,11},{9,10},{10,... | collective-permute-start | bytes 344072 | tf_op jit(solution)/shard_map/ppermute | solution.py:320
  47.2 10.9 %collective-permute-start.12 = (bf16[32,1792]{1,0:T(8,128)(2,1)S(1)}, bf16[32,1792]{1,0:T(8,128)(2,1)S(1)}, u32[]{:S(2)}, u32[]{:S(2)}) collective-permute-start(bf16[32,1792]{1,0:T(8,128)(2,1)S(1)} %add_convert_fusion.1), channel_id=1, source_target_pairs={{0,2},{1,3},{2,0},{3,1},{4,6},{5,7},{6,4},{7,5},{8,10},{9,11},{10,... | collective-permute-start | bytes 344072 | tf_op jit(solution)/shard_map/ppermute | solution.py:320
  47.5 10.5 %collective-permute-start.11 = (bf16[32,1792]{1,0:T(8,128)(2,1)S(1)}, bf16[32,1792]{1,0:T(8,128)(2,1)S(1)}, u32[]{:S(2)}, u32[]{:S(2)}) collective-permute-start(bf16[32,1792]{1,0:T(8,128)(2,1)S(1)} %add_convert_fusion.1), channel_id=1, source_target_pairs={{0,1},{1,0},{2,3},{3,2},{4,5},{5,4},{6,7},{7,6},{8,9},{9,8},{10,11... | collective-permute-start | bytes 344072 | tf_op jit(solution)/shard_map/ppermute | solution.py:320
  48.6 9.6 %collective-permute-start.14 = (bf16[1,256,512]{2,1,0:T(8,128)(2,1)S(1)}, bf16[1,256,512]{2,1,0:T(8,128)(2,1)S(1)}, u32[]{:S(2)}, u32[]{:S(2)}) collective-permute-start(bf16[1,256,512]{2,1,0:T(8,128)(2,1)S(1)} %get-tuple-element.74), channel_id=1, source_target_pairs={{0,12},{4,8},{8,4},{12,0},{1,13},{5,9},{9,5},{13,1},{2,14},{6,10},... | collective-permute-start | bytes 786440 | tf_op jit(solution)/shard_map/ppermute | solution.py:319
  65.4 2.1 %collective-permute-start.15 = (bf16[2,32,4608]{2,1,0:T(8,128)(2,1)S(1)}, bf16[2,32,4608]{2,1,0:T(8,128)(2,1)S(1)}, u32[]{:S(2)}, u32[]{:S(2)}) collective-permute-start(bf16[2,32,4608]{2,1,0:T(8,128)(2,1)S(1)} %get-tuple-element.77), channel_id=1, source_target_pairs={{0,4},{4,0},{8,12},{12,8},{1,5},{5,1},{9,13},{13,9},{2,6},{6,2},{1... | collective-permute-start | bytes 1769480 | tf_op jit(solution)/shard_map/ppermute | solution.py:134
  67.6 9.1 %collective-permute-start.16 = (bf16[32,4608]{1,0:T(8,128)(2,1)S(1)}, bf16[32,4608]{1,0:T(8,128)(2,1)S(1)}, u32[]{:S(2)}, u32[]{:S(2)}) collective-permute-start(bf16[32,4608]{1,0:T(8,128)(2,1)S(1)} %get-tuple-element.101), channel_id=1, source_target_pairs={{0,8},{4,12},{8,0},{12,4},{1,9},{5,13},{9,1},{13,5},{2,10},{6,14},... | collective-permute-start | bytes 884744 | tf_op jit(solution)/shard_map/ppermute | solution.py:139
  69.3 26.9 %slice-start = ((s8[16515072]{0:T(1024)(128)(4,1)}), s8[4194304]{0:T(1024)(128)(4,1)S(1)}, s32[]{:S(2)}) async-start(s8[16515072]{0:T(1024)(128)(4,1)} %bitcast.56), calls=%async_computation | async-start | bytes 8388608
  69.3 26.9 %slice-start.1 = ((s8[16515072]{0:T(1024)(128)(4,1)}), s8[4194304]{0:T(1024)(128)(4,1)S(1)}, s32[]{:S(2)}) async-start(s8[16515072]{0:T(1024)(128)(4,1)} %bitcast.56), calls=%async_computation.1 | async-start | bytes 8388608
  69.3 26.9 %slice-start.2 = ((s8[16515072]{0:T(1024)(128)(4,1)}), s8[4194304]{0:T(1024)(128)(4,1)S(1)}, s32[]{:S(2)}) async-start(s8[16515072]{0:T(1024)(128)(4,1)} %bitcast.56), calls=%async_computation.2 | async-start | bytes 8388608
  76.0 26.3 %copy-start.3 = (bf16[1,256,512]{2,1,0:T(8,128)(2,1)S(1)}, bf16[1,256,512]{2,1,0:T(8,128)(2,1)}, u32[]{:S(2)}) copy-start(bf16[1,256,512]{2,1,0:T(8,128)(2,1)} %copy-done.2) | copy-start | bytes 786436
  76.0 26.3 %copy-start.5 = (bf16[1,256,512]{2,1,0:T(8,128)(2,1)S(1)}, bf16[1,256,512]{2,1,0:T(8,128)(2,1)}, u32[]{:S(2)}) copy-start(bf16[1,256,512]{2,1,0:T(8,128)(2,1)} %copy-done.4) | copy-start | bytes 786436
  76.1 2.5 %collective-permute-start.18 = (bf16[2,32,4608]{2,1,0:T(8,128)(2,1)S(1)}, bf16[2,32,4608]{2,1,0:T(8,128)(2,1)S(1)}, u32[]{:S(2)}, u32[]{:S(2)}) collective-permute-start(bf16[2,32,4608]{2,1,0:T(8,128)(2,1)S(1)} %get-tuple-element.81), channel_id=1, source_target_pairs={{0,4},{4,0},{8,12},{12,8},{1,5},{5,1},{9,13},{13,9},{2,6},{6,2},{1... | collective-permute-start | bytes 1769480 | tf_op jit(solution)/shard_map/ppermute | solution.py:134
  76.9 6.8 %collective-permute-start.17 = (bf16[32,2304]{1,0:T(8,128)(2,1)S(1)}, bf16[32,2304]{1,0:T(8,128)(2,1)S(1)}, u32[]{:S(2)}, u32[]{:S(2)}) collective-permute-start(bf16[32,2304]{1,0:T(8,128)(2,1)S(1)} %fusion.3), channel_id=1, source_target_pairs={{0,8},{4,12},{8,0},{12,4},{1,9},{5,13},{9,1},{13,5},{2,10},{6,14},... | collective-permute-start | bytes 442376 | tf_op jit(solution)/shard_map/ppermute | solution.py:336
  78.5 33.4 %copy-start.1 = (bf16[128,1792]{1,0:T(8,128)(2,1)S(1)}, bf16[128,1792]{1,0:T(8,128)(2,1)}, u32[]{:S(2)}) copy-start(bf16[128,1792]{1,0:T(8,128)(2,1)} %param.17) | copy-start | bytes 1376260
  78.7 10.3 %collective-permute-start.20 = (bf16[32,4608]{1,0:T(8,128)(2,1)S(1)}, bf16[32,4608]{1,0:T(8,128)(2,1)S(1)}, u32[]{:S(2)}, u32[]{:S(2)}) collective-permute-start(bf16[32,4608]{1,0:T(8,128)(2,1)S(1)} %get-tuple-element.100), channel_id=1, source_target_pairs={{0,8},{4,12},{8,0},{12,4},{1,9},{5,13},{9,1},{13,5},{2,10},{6,14},... | collective-permute-start | bytes 884744 | tf_op jit(solution)/shard_map/ppermute | solution.py:139
  83.7 6.4 %collective-permute-start.19 = (bf16[2,32,2304]{2,1,0:T(8,128)(2,1)S(1)}, bf16[2,32,2304]{2,1,0:T(8,128)(2,1)S(1)}, u32[]{:S(2)}, u32[]{:S(2)}) collective-permute-start(bf16[2,32,2304]{2,1,0:T(8,128)(2,1)S(1)} %pad_maximum_fusion.4), channel_id=1, source_target_pairs={{0,4},{4,0},{8,12},{12,8},{1,5},{5,1},{9,13},{13,9},{2,6},{6,2},{1... | collective-permute-start | bytes 884744 | tf_op jit(solution)/shard_map/ppermute | solution.py:340
  89.2 5.2 %collective-permute-start.21 = (bf16[32,2304]{1,0:T(8,128)(2,1)S(1)}, bf16[32,2304]{1,0:T(8,128)(2,1)S(1)}, u32[]{:S(2)}, u32[]{:S(2)}) collective-permute-start(bf16[32,2304]{1,0:T(8,128)(2,1)S(1)} %fusion.2), channel_id=1, source_target_pairs={{0,8},{4,12},{8,0},{12,4},{1,9},{5,13},{9,1},{13,5},{2,10},{6,14},... | collective-permute-start | bytes 442376 | tf_op jit(solution)/shard_map/ppermute | solution.py:336
  94.4 1.6 %collective-permute-start.22 = (bf16[2,32,2304]{2,1,0:T(8,128)(2,1)S(1)}, bf16[2,32,2304]{2,1,0:T(8,128)(2,1)S(1)}, u32[]{:S(2)}, u32[]{:S(2)}) collective-permute-start(bf16[2,32,2304]{2,1,0:T(8,128)(2,1)S(1)} %pad_maximum_fusion.5), channel_id=1, source_target_pairs={{0,4},{4,0},{8,12},{12,8},{1,5},{5,1},{9,13},{13,9},{2,6},{6,2},{1... | collective-permute-start | bytes 884744 | tf_op jit(solution)/shard_map/ppermute | solution.py:340
  98.7 11.3 %collective-permute-start.23 = (bf16[32,1792]{1,0:T(8,128)(2,1)S(1)}, bf16[32,1792]{1,0:T(8,128)(2,1)S(1)}, u32[]{:S(2)}, u32[]{:S(2)}) collective-permute-start(bf16[32,1792]{1,0:T(8,128)(2,1)S(1)} %convert_element_type.133), channel_id=1, source_target_pairs={{0,2},{1,3},{2,0},{3,1},{4,6},{5,7},{6,4},{7,5},{8,10},{9,11},{10,... | collective-permute-start | bytes 344072 | tf_op jit(solution)/shard_map/ppermute | solution.py:293
  99.6 10.5 %collective-permute-start.24 = (bf16[32,1792]{1,0:T(8,128)(2,1)S(1)}, bf16[32,1792]{1,0:T(8,128)(2,1)S(1)}, u32[]{:S(2)}, u32[]{:S(2)}) collective-permute-start(bf16[32,1792]{1,0:T(8,128)(2,1)S(1)} %get-tuple-element.111), channel_id=1, source_target_pairs={{0,3},{1,2},{2,1},{3,0},{4,7},{5,6},{6,5},{7,4},{8,11},{9,10},{10,... | collective-permute-start | bytes 344072 | tf_op jit(solution)/shard_map/ppermute | solution.py:293
  101.6 9.6 %collective-permute-start.25 = (bf16[32,1792]{1,0:T(8,128)(2,1)S(1)}, bf16[32,1792]{1,0:T(8,128)(2,1)S(1)}, u32[]{:S(2)}, u32[]{:S(2)}) collective-permute-start(bf16[32,1792]{1,0:T(8,128)(2,1)S(1)} %get-tuple-element.112), channel_id=1, source_target_pairs={{0,1},{1,0},{2,3},{3,2},{4,5},{5,4},{6,7},{7,6},{8,9},{9,8},{10,11... | collective-permute-start | bytes 344072 | tf_op jit(solution)/shard_map/ppermute | solution.py:293
  (7 other events, 104.7 us)
